TPU v7x, 768 devices: a whole 4x8x12 slice. The times are simulated.
768 devices in a mesh: blk: 96 (over y_lo, x, z), wn: 8 (over y_hi, core).
Axes of the slice: x: 4, y: 8 (y_hi: 4, y_lo: 2; y = y_hi * 2 + y_lo), z: 12, core: 2. Of those that a mesh axis runs over, the one named last changes fastest.
Arguments:
- species_molar_share: float32 [11, 128, 2, 12288], P(None, 'wn', None, 'blk'), may hold values from 0.01 to 1
- flow_speed_vector: float32 [2, 128, 2, 12288], P(None, 'wn', None, 'blk'), may hold values from -6 to 6
- thermal_level: float32 [128, 2, 12288], P('wn', None, 'blk'), may hold values from 0.5 to 2
- shear_collision_terms: float32 [11, 11], replicated, may hold values from 1 to 2
- thermal_collision_terms: float32 [11, 11], replicated, may hold values from 1 to 2
Outputs:
- final_state: float32 [14, 128, 2, 12288], P(None, 'wn', None, 'blk')
- last_residual: float32 [14, 128, 2, 12288], P(None, 'wn', None, 'blk')
All inputs are finite; a program needn't handle non-finite values.
Results may differ from a plain program's by a relative error of at most 0.00005.
Values sent between devices are 32-bit elements; how exact they have to be, the bound alone decides.
No kernel may reach another device: no remote copies, remote signals or barrier semaphores. Data moves between devices by JAX's collectives and lax.ppermute only.
A program may use at most 32 MiB of HBM per device.

v0:
```python
import jax
import jax.numpy as jnp
import numpy as np
from jax import lax
from jax.sharding import PartitionSpec as P

MASSES = np.array([28.0, 32.0, 30.0, 14.0, 16.0, 28.0, 32.0, 30.0, 14.0, 16.0, 0.00055]) / 28.0


def extended(block, sides, width):
    for axis, dim in sides:
        count = lax.axis_size(axis)
        forward = [(i, i + 1) for i in range(count - 1)]
        backward = [(target, source) for source, target in forward]
        low = lax.ppermute(
            lax.slice_in_dim(block, block.shape[dim] - width, None, axis=dim), axis, forward
        )
        high = lax.ppermute(lax.slice_in_dim(block, 0, width, axis=dim), axis, backward)
        block = jnp.concatenate([low, block, high], axis=dim)
    return block


def properties(padded, shear_collision_terms, thermal_collision_terms):
    fractions = padded[:11]
    heat = padded[13]
    denom_visc = jnp.einsum(
        "sr,rjki->sjki", shear_collision_terms, fractions, precision=lax.Precision.HIGHEST
    )
    denom_cond = jnp.einsum(
        "sr,rjki->sjki", thermal_collision_terms, fractions, precision=lax.Precision.HIGHEST
    )
    mixture_viscosity = heat**0.7 * jnp.sum(
        fractions * MASSES[:, None, None, None] / denom_visc, axis=0
    )
    conduct = heat**0.5 * jnp.sum(fractions / denom_cond, axis=0)
    return (mixture_viscosity, conduct)


def shifted(field, down, across):
    rows = field.shape[-3]
    cols = field.shape[-1]
    return field[..., 1 + down : rows - 1 + down, :, 1 + across : cols - 1 + across]


def diffuse(padded, coeff):
    center_c = shifted(coeff, 0, 0)
    center_face = shifted(padded, 0, 0)
    total = jnp.zeros_like(center_face)
    for down, across in ((1, 0), (-1, 0), (0, 1), (0, -1)):
        total = total + 0.5 * (center_c + shifted(coeff, down, across)) * (
            shifted(padded, down, across) - center_face
        )
    return total


def residual_of(padded, mixture_viscosity, conduct):
    return jnp.concatenate(
        [
            diffuse(padded[:11], conduct),
            diffuse(padded[11:13], mixture_viscosity),
            diffuse(padded[13:], conduct),
        ],
        axis=0,
    )


def assemble(payload, row_ext, col_ext):
    wn_here = lax.axis_index("wn")
    wn_count = lax.axis_size("wn")
    blk_here = lax.axis_index("blk")
    blk_count = lax.axis_size("blk")
    bottom = jnp.where(wn_here == 0, payload[:, 1:2, ::-1, :], row_ext[:, :1])
    top = jnp.where(wn_here == wn_count - 1, payload[:, -1:], row_ext[:, -1:])
    left = jnp.where(blk_here == 0, payload[..., :1], col_ext[..., :1])
    right = jnp.where(blk_here == blk_count - 1, payload[:, :, ::-1, -1:], col_ext[..., -1:])
    middle = jnp.concatenate([left, payload, right], axis=3)
    edge_pad = ((0, 0), (0, 0), (0, 0), (1, 1))
    return jnp.concatenate([jnp.pad(bottom, edge_pad), middle, jnp.pad(top, edge_pad)], axis=1)


def evaluate(state, shear_collision_terms, thermal_collision_terms):
    mixture_viscosity, conduct = properties(state, shear_collision_terms, thermal_collision_terms)
    payload = jnp.concatenate([state, mixture_viscosity[None], conduct[None]], axis=0)
    row_ext = extended(payload, (("wn", 1),), 1)
    col_ext = extended(payload, (("blk", 3),), 1)
    padded = assemble(payload, row_ext, col_ext)
    return residual_of(padded[:14], padded[14], padded[15])


def local(
    species_molar_share,
    flow_speed_vector,
    thermal_level,
    shear_collision_terms,
    thermal_collision_terms,
):
    step = 0.16
    first_position = jnp.concatenate(
        [species_molar_share, flow_speed_vector, thermal_level[None]], axis=0
    )
    first = first_position + step * evaluate(
        first_position, shear_collision_terms, thermal_collision_terms
    )
    second = 0.75 * first_position + 0.25 * (
        first + step * evaluate(first, shear_collision_terms, thermal_collision_terms)
    )
    last_residual = evaluate(second, shear_collision_terms, thermal_collision_terms)
    final_state = first_position / 3.0 + 2.0 / 3.0 * (second + step * last_residual)
    return (final_state, last_residual)


def solution(mesh):
    return jax.shard_map(
        local,
        mesh=mesh,
        in_specs=(
            P(None, "wn", None, "blk"),
            P(None, "wn", None, "blk"),
            P("wn", None, "blk"),
            P(),
            P(),
        ),
        out_specs=(P(None, "wn", None, "blk"), P(None, "wn", None, "blk")),
        check_vma=False,
    )
```

profile of v0, /device:TPU:40, one launch (start us, length us, event | category | flops | bytes accessed | tf_op | source)
XLA Modules:
  0.0 103.0 jit_solution(17182016558722293597)
XLA Ops:
  0.7 1.5 %fusion = f32[16,2,128]{2,1,0:T(2,128)S(1)} fusion(f32[11,16,2,128]{3,2,1,0:T(2,128)} %param.8, f32[11,11]{1,0:T(8,128)} %param.12), kind=kOutput, calls=%fused_computation.1 | convolution fusion | flops 6033408 | bytes 197092 | tf_op jit(solution)/shard_map/sr,rjki->sjki/dot_general | solution.py:29
  2.2 0.4 fusion.10
  2.6 0.2 copy-done.5
  2.8 0.1 fusion.146
  3.0 0.6 copy-done.3
  3.6 0.7 copy-done.2
  4.5 4.3 %collective-permute-start.1 = (f32[16,16,2,1]{3,1,2,0:T(8,128)S(1)}, f32[16,16,2,1]{3,1,2,0:T(8,128)S(1)}, u32[]{:S(2)}, u32[]{:S(2)}) collective-permute-start(f32[16,16,2,1]{3,1,2,0:T(8,128)S(1)} %slice.550), channel_id=1, source_target_pairs={{0,8},{8,16},{16,24},{24,32},{32,40},{40,48},{48,56},{56,64},{64,7... | collective-permute-start | bytes 6152 | tf_op jit(solution)/shard_map/ppermute | solution.py:15
  8.8 2.3 %collective-permute-start.3 = (f32[16,1,2,128]{3,1,2,0:T(1,128)S(1)}, f32[16,1,2,128]{3,1,2,0:T(1,128)S(1)}, u32[]{:S(2)}, u32[]{:S(2)}) collective-permute-start(f32[16,1,2,128]{3,1,2,0:T(1,128)S(1)} %slice.551), channel_id=1, source_target_pairs={{1,0},{2,1},{3,2},{4,3},{5,4},{6,5},{7,6},{9,8},{10,9},{11,10},{12... | collective-permute-start | bytes 49160 | tf_op jit(solution)/shard_map/ppermute | solution.py:18
  11.1 17.2 %collective-permute-done.1 = f32[16,16,2,1]{3,1,2,0:T(8,128)S(1)} collective-permute-done((f32[16,16,2,1]{3,1,2,0:T(8,128)S(1)}, f32[16,16,2,1]{3,1,2,0:T(8,128)S(1)}, u32[]{:S(2)}, u32[]{:S(2)}) %collective-permute-start.1) | collective-permute-done | bytes 2080 | tf_op jit(solution)/shard_map/ppermute | solution.py:15
  28.4 3.6 %collective-permute-start.2 = (f32[16,16,2,1]{3,1,2,0:T(8,128)S(1)}, f32[16,16,2,1]{3,1,2,0:T(8,128)S(1)}, u32[]{:S(2)}, u32[]{:S(2)}) collective-permute-start(f32[16,16,2,1]{3,1,2,0:T(8,128)S(1)} %get-tuple-element.52), channel_id=1, source_target_pairs={{8,0},{16,8},{24,16},{32,24},{40,32},{48,40},{56,48},{64,56},{72,6... | collective-permute-start | bytes 6152 | tf_op jit(solution)/shard_map/ppermute | solution.py:18
  32.1 1.9 %collective-permute-start = (f32[16,1,2,128]{3,1,2,0:T(1,128)S(1)}, f32[16,1,2,128]{3,1,2,0:T(1,128)S(1)}, u32[]{:S(2)}, u32[]{:S(2)}) collective-permute-start(f32[16,1,2,128]{3,1,2,0:T(1,128)S(1)} %get-tuple-element.50), channel_id=1, source_target_pairs={{0,1},{1,2},{2,3},{3,4},{4,5},{5,6},{6,7},{8,9},{9,10},{10,11},{11... | collective-permute-start | bytes 49160 | tf_op jit(solution)/shard_map/ppermute | solution.py:15
  34.0 3.7 %collective-permute-done.2 = f32[16,16,2,1]{3,1,2,0:T(8,128)S(1)} collective-permute-done((f32[16,16,2,1]{3,1,2,0:T(8,128)S(1)}, f32[16,16,2,1]{3,1,2,0:T(8,128)S(1)}, u32[]{:S(2)}, u32[]{:S(2)}) %collective-permute-start.2) | collective-permute-done | bytes 2080 | tf_op jit(solution)/shard_map/ppermute | solution.py:18
  37.8 0.1 pad.20
  38.0 1.3 %collective-permute-done = f32[16,1,2,128]{3,1,2,0:T(1,128)S(1)} collective-permute-done((f32[16,1,2,128]{3,1,2,0:T(1,128)S(1)}, f32[16,1,2,128]{3,1,2,0:T(1,128)S(1)}, u32[]{:S(2)}, u32[]{:S(2)}) %collective-permute-start) | collective-permute-done | bytes 16416 | tf_op jit(solution)/shard_map/ppermute | solution.py:15
  39.3 0.1 pad.19
  39.8 0.1 fusion.70
  39.9 0.4 fusion.19
  40.3 0.5 fusion.7
  40.8 0.2 copy-done.4
  41.0 0.5 fusion.5
  41.5 0.2 fusion.44
  41.9 2.2 %collective-permute-start.5 = (f32[16,16,2,1]{3,1,2,0:T(8,128)S(1)}, f32[16,16,2,1]{3,1,2,0:T(8,128)S(1)}, u32[]{:S(2)}, u32[]{:S(2)}) collective-permute-start(f32[16,16,2,1]{3,1,2,0:T(8,128)S(1)} %slice.573), channel_id=1, source_target_pairs={{0,8},{8,16},{16,24},{24,32},{32,40},{40,48},{48,56},{56,64},{64,7... | collective-permute-start | bytes 6152 | tf_op jit(solution)/shard_map/ppermute | solution.py:15
  44.2 10.3 %collective-permute-done.5 = f32[16,16,2,1]{3,1,2,0:T(8,128)S(1)} collective-permute-done((f32[16,16,2,1]{3,1,2,0:T(8,128)S(1)}, f32[16,16,2,1]{3,1,2,0:T(8,128)S(1)}, u32[]{:S(2)}, u32[]{:S(2)}) %collective-permute-start.5) | collective-permute-done | bytes 2080 | tf_op jit(solution)/shard_map/ppermute | solution.py:15
  54.5 2.0 %collective-permute-start.6 = (f32[16,16,2,1]{3,1,2,0:T(8,128)S(1)}, f32[16,16,2,1]{3,1,2,0:T(8,128)S(1)}, u32[]{:S(2)}, u32[]{:S(2)}) collective-permute-start(f32[16,16,2,1]{3,1,2,0:T(8,128)S(1)} %get-tuple-element.47), channel_id=1, source_target_pairs={{8,0},{16,8},{24,16},{32,24},{40,32},{48,40},{56,48},{64,56},{72,6... | collective-permute-start | bytes 6152 | tf_op jit(solution)/shard_map/ppermute | solution.py:18
  56.5 3.0 %collective-permute-start.7 = (f32[16,1,2,128]{3,1,2,0:T(1,128)S(1)}, f32[16,1,2,128]{3,1,2,0:T(1,128)S(1)}, u32[]{:S(2)}, u32[]{:S(2)}) collective-permute-start(f32[16,1,2,128]{3,1,2,0:T(1,128)S(1)} %get-tuple-element.46), channel_id=1, source_target_pairs={{1,0},{2,1},{3,2},{4,3},{5,4},{6,5},{7,6},{9,8},{10,9},{11,10},{12... | collective-permute-start | bytes 49160 | tf_op jit(solution)/shard_map/ppermute | solution.py:18
  59.5 3.2 %collective-permute-done.6 = f32[16,16,2,1]{3,1,2,0:T(8,128)S(1)} collective-permute-done((f32[16,16,2,1]{3,1,2,0:T(8,128)S(1)}, f32[16,16,2,1]{3,1,2,0:T(8,128)S(1)}, u32[]{:S(2)}, u32[]{:S(2)}) %collective-permute-start.6) | collective-permute-done | bytes 2080 | tf_op jit(solution)/shard_map/ppermute | solution.py:18
  62.8 1.9 %collective-permute-start.4 = (f32[16,1,2,128]{3,1,2,0:T(1,128)S(1)}, f32[16,1,2,128]{3,1,2,0:T(1,128)S(1)}, u32[]{:S(2)}, u32[]{:S(2)}) collective-permute-start(f32[16,1,2,128]{3,1,2,0:T(1,128)S(1)} %get-tuple-element.25), channel_id=1, source_target_pairs={{0,1},{1,2},{2,3},{3,4},{4,5},{5,6},{6,7},{8,9},{9,10},{10,11},{11... | collective-permute-start | bytes 49160 | tf_op jit(solution)/shard_map/ppermute | solution.py:15
  64.7 0.2 pad_maximum_fusion
  65.0 0.1 pad.22
  65.1 4.9 %collective-permute-done.4 = f32[16,1,2,128]{3,1,2,0:T(1,128)S(1)} collective-permute-done((f32[16,1,2,128]{3,1,2,0:T(1,128)S(1)}, f32[16,1,2,128]{3,1,2,0:T(1,128)S(1)}, u32[]{:S(2)}, u32[]{:S(2)}) %collective-permute-start.4) | collective-permute-done | bytes 16416 | tf_op jit(solution)/shard_map/ppermute | solution.py:15
  70.5 0.1 fusion.61
  70.6 0.3 fusion.32
  71.0 0.5 fusion.3
  71.5 0.5 fusion.1
  72.0 0.2 fusion.45
  72.4 1.9 %collective-permute-start.9 = (f32[16,16,2,1]{3,1,2,0:T(8,128)S(1)}, f32[16,16,2,1]{3,1,2,0:T(8,128)S(1)}, u32[]{:S(2)}, u32[]{:S(2)}) collective-permute-start(f32[16,16,2,1]{3,1,2,0:T(8,128)S(1)} %slice.590), channel_id=1, source_target_pairs={{0,8},{8,16},{16,24},{24,32},{32,40},{40,48},{48,56},{56,64},{64,7... | collective-permute-start | bytes 6152 | tf_op jit(solution)/shard_map/ppermute | solution.py:15
  74.3 10.6 %collective-permute-done.9 = f32[16,16,2,1]{3,1,2,0:T(8,128)S(1)} collective-permute-done((f32[16,16,2,1]{3,1,2,0:T(8,128)S(1)}, f32[16,16,2,1]{3,1,2,0:T(8,128)S(1)}, u32[]{:S(2)}, u32[]{:S(2)}) %collective-permute-start.9) | collective-permute-done | bytes 2080 | tf_op jit(solution)/shard_map/ppermute | solution.py:15
  84.9 2.0 %collective-permute-start.10 = (f32[16,16,2,1]{3,1,2,0:T(8,128)S(1)}, f32[16,16,2,1]{3,1,2,0:T(8,128)S(1)}, u32[]{:S(2)}, u32[]{:S(2)}) collective-permute-start(f32[16,16,2,1]{3,1,2,0:T(8,128)S(1)} %get-tuple-element.41), channel_id=1, source_target_pairs={{8,0},{16,8},{24,16},{32,24},{40,32},{48,40},{56,48},{64,56},{72,6... | collective-permute-start | bytes 6152 | tf_op jit(solution)/shard_map/ppermute | solution.py:18
  87.0 1.9 %collective-permute-start.11 = (f32[16,1,2,128]{3,1,2,0:T(1,128)S(1)}, f32[16,1,2,128]{3,1,2,0:T(1,128)S(1)}, u32[]{:S(2)}, u32[]{:S(2)}) collective-permute-start(f32[16,1,2,128]{3,1,2,0:T(1,128)S(1)} %get-tuple-element.40), channel_id=1, source_target_pairs={{1,0},{2,1},{3,2},{4,3},{5,4},{6,5},{7,6},{9,8},{10,9},{11,10},{12... | collective-permute-start | bytes 49160 | tf_op jit(solution)/shard_map/ppermute | solution.py:18
  88.9 4.3 %collective-permute-done.10 = f32[16,16,2,1]{3,1,2,0:T(8,128)S(1)} collective-permute-done((f32[16,16,2,1]{3,1,2,0:T(8,128)S(1)}, f32[16,16,2,1]{3,1,2,0:T(8,128)S(1)}, u32[]{:S(2)}, u32[]{:S(2)}) %collective-permute-start.10) | collective-permute-done | bytes 2080 | tf_op jit(solution)/shard_map/ppermute | solution.py:18
  93.3 1.9 %collective-permute-start.8 = (f32[16,1,2,128]{3,1,2,0:T(1,128)S(1)}, f32[16,1,2,128]{3,1,2,0:T(1,128)S(1)}, u32[]{:S(2)}, u32[]{:S(2)}) collective-permute-start(f32[16,1,2,128]{3,1,2,0:T(1,128)S(1)} %get-tuple-element.18), channel_id=1, source_target_pairs={{0,1},{1,2},{2,3},{3,4},{4,5},{5,6},{6,7},{8,9},{9,10},{10,11},{11... | collective-permute-start | bytes 49160 | tf_op jit(solution)/shard_map/ppermute | solution.py:15
  95.2 0.2 pad_maximum_fusion.1
  95.4 0.1 pad.24
  95.6 4.9 %collective-permute-done.8 = f32[16,1,2,128]{3,1,2,0:T(1,128)S(1)} collective-permute-done((f32[16,1,2,128]{3,1,2,0:T(1,128)S(1)}, f32[16,1,2,128]{3,1,2,0:T(1,128)S(1)}, u32[]{:S(2)}, u32[]{:S(2)}) %collective-permute-start.8) | collective-permute-done | bytes 16416 | tf_op jit(solution)/shard_map/ppermute | solution.py:15
  100.9 0.1 fusion.54
  101.1 0.3 fusion.25
  101.4 0.8 copy.111
  102.2 0.8 copy.110
  (54 shorter events, 2.4 us)
Async XLA Ops:
  0.6 1.5 %copy-start = (f32[11,11]{1,0:T(8,128)S(1)}, f32[11,11]{1,0:T(8,128)}, u32[]{:S(2)}) copy-start(f32[11,11]{1,0:T(8,128)} %param.11) | copy-start | bytes 1456
  0.6 1.5 %copy-start.1 = (f32[11,16,2,128]{3,2,1,0:T(2,128)S(1)}, f32[11,16,2,128]{3,2,1,0:T(2,128)}, u32[]{:S(2)}) copy-start(f32[11,16,2,128]{3,2,1,0:T(2,128)} %param.8) | copy-start | bytes 540676
  2.2 0.7 copy-start.5
  2.8 0.8 copy-start.3
  3.6 0.7 copy-start.2
  4.5 23.9 %collective-permute-start.1 = (f32[16,16,2,1]{3,1,2,0:T(8,128)S(1)}, f32[16,16,2,1]{3,1,2,0:T(8,128)S(1)}, u32[]{:S(2)}, u32[]{:S(2)}) collective-permute-start(f32[16,16,2,1]{3,1,2,0:T(8,128)S(1)} %slice.550), channel_id=1, source_target_pairs={{0,8},{8,16},{16,24},{24,32},{32,40},{40,48},{48,56},{56,64},{64,7... | collective-permute-start | bytes 6152 | tf_op jit(solution)/shard_map/ppermute | solution.py:15
  8.8 23.2 %collective-permute-start.3 = (f32[16,1,2,128]{3,1,2,0:T(1,128)S(1)}, f32[16,1,2,128]{3,1,2,0:T(1,128)S(1)}, u32[]{:S(2)}, u32[]{:S(2)}) collective-permute-start(f32[16,1,2,128]{3,1,2,0:T(1,128)S(1)} %slice.551), channel_id=1, source_target_pairs={{1,0},{2,1},{3,2},{4,3},{5,4},{6,5},{7,6},{9,8},{10,9},{11,10},{12... | collective-permute-start | bytes 49160 | tf_op jit(solution)/shard_map/ppermute | solution.py:18
  28.4 9.4 %collective-permute-start.2 = (f32[16,16,2,1]{3,1,2,0:T(8,128)S(1)}, f32[16,16,2,1]{3,1,2,0:T(8,128)S(1)}, u32[]{:S(2)}, u32[]{:S(2)}) collective-permute-start(f32[16,16,2,1]{3,1,2,0:T(8,128)S(1)} %get-tuple-element.52), channel_id=1, source_target_pairs={{8,0},{16,8},{24,16},{32,24},{40,32},{48,40},{56,48},{64,56},{72,6... | collective-permute-start | bytes 6152 | tf_op jit(solution)/shard_map/ppermute | solution.py:18
  32.1 7.2 %collective-permute-start = (f32[16,1,2,128]{3,1,2,0:T(1,128)S(1)}, f32[16,1,2,128]{3,1,2,0:T(1,128)S(1)}, u32[]{:S(2)}, u32[]{:S(2)}) collective-permute-start(f32[16,1,2,128]{3,1,2,0:T(1,128)S(1)} %get-tuple-element.50), channel_id=1, source_target_pairs={{0,1},{1,2},{2,3},{3,4},{4,5},{5,6},{6,7},{8,9},{9,10},{10,11},{11... | collective-permute-start | bytes 49160 | tf_op jit(solution)/shard_map/ppermute | solution.py:15
  40.3 0.7 copy-start.4
  41.9 12.5 %collective-permute-start.5 = (f32[16,16,2,1]{3,1,2,0:T(8,128)S(1)}, f32[16,16,2,1]{3,1,2,0:T(8,128)S(1)}, u32[]{:S(2)}, u32[]{:S(2)}) collective-permute-start(f32[16,16,2,1]{3,1,2,0:T(8,128)S(1)} %slice.573), channel_id=1, source_target_pairs={{0,8},{8,16},{16,24},{24,32},{32,40},{40,48},{48,56},{56,64},{64,7... | collective-permute-start | bytes 6152 | tf_op jit(solution)/shard_map/ppermute | solution.py:15
  54.5 8.3 %collective-permute-start.6 = (f32[16,16,2,1]{3,1,2,0:T(8,128)S(1)}, f32[16,16,2,1]{3,1,2,0:T(8,128)S(1)}, u32[]{:S(2)}, u32[]{:S(2)}) collective-permute-start(f32[16,16,2,1]{3,1,2,0:T(8,128)S(1)} %get-tuple-element.47), channel_id=1, source_target_pairs={{8,0},{16,8},{24,16},{32,24},{40,32},{48,40},{56,48},{64,56},{72,6... | collective-permute-start | bytes 6152 | tf_op jit(solution)/shard_map/ppermute | solution.py:18
  56.5 6.3 %collective-permute-start.7 = (f32[16,1,2,128]{3,1,2,0:T(1,128)S(1)}, f32[16,1,2,128]{3,1,2,0:T(1,128)S(1)}, u32[]{:S(2)}, u32[]{:S(2)}) collective-permute-start(f32[16,1,2,128]{3,1,2,0:T(1,128)S(1)} %get-tuple-element.46), channel_id=1, source_target_pairs={{1,0},{2,1},{3,2},{4,3},{5,4},{6,5},{7,6},{9,8},{10,9},{11,10},{12... | collective-permute-start | bytes 49160 | tf_op jit(solution)/shard_map/ppermute | solution.py:18
  62.8 7.2 %collective-permute-start.4 = (f32[16,1,2,128]{3,1,2,0:T(1,128)S(1)}, f32[16,1,2,128]{3,1,2,0:T(1,128)S(1)}, u32[]{:S(2)}, u32[]{:S(2)}) collective-permute-start(f32[16,1,2,128]{3,1,2,0:T(1,128)S(1)} %get-tuple-element.25), channel_id=1, source_target_pairs={{0,1},{1,2},{2,3},{3,4},{4,5},{5,6},{6,7},{8,9},{9,10},{10,11},{11... | collective-permute-start | bytes 49160 | tf_op jit(solution)/shard_map/ppermute | solution.py:15
  72.4 12.5 %collective-permute-start.9 = (f32[16,16,2,1]{3,1,2,0:T(8,128)S(1)}, f32[16,16,2,1]{3,1,2,0:T(8,128)S(1)}, u32[]{:S(2)}, u32[]{:S(2)}) collective-permute-start(f32[16,16,2,1]{3,1,2,0:T(8,128)S(1)} %slice.590), channel_id=1, source_target_pairs={{0,8},{8,16},{16,24},{24,32},{32,40},{40,48},{48,56},{56,64},{64,7... | collective-permute-start | bytes 6152 | tf_op jit(solution)/shard_map/ppermute | solution.py:15
  84.9 8.3 %collective-permute-start.10 = (f32[16,16,2,1]{3,1,2,0:T(8,128)S(1)}, f32[16,16,2,1]{3,1,2,0:T(8,128)S(1)}, u32[]{:S(2)}, u32[]{:S(2)}) collective-permute-start(f32[16,16,2,1]{3,1,2,0:T(8,128)S(1)} %get-tuple-element.41), channel_id=1, source_target_pairs={{8,0},{16,8},{24,16},{32,24},{40,32},{48,40},{56,48},{64,56},{72,6... | collective-permute-start | bytes 6152 | tf_op jit(solution)/shard_map/ppermute | solution.py:18
  87.0 6.2 %collective-permute-start.11 = (f32[16,1,2,128]{3,1,2,0:T(1,128)S(1)}, f32[16,1,2,128]{3,1,2,0:T(1,128)S(1)}, u32[]{:S(2)}, u32[]{:S(2)}) collective-permute-start(f32[16,1,2,128]{3,1,2,0:T(1,128)S(1)} %get-tuple-element.40), channel_id=1, source_target_pairs={{1,0},{2,1},{3,2},{4,3},{5,4},{6,5},{7,6},{9,8},{10,9},{11,10},{12... | collective-permute-start | bytes 49160 | tf_op jit(solution)/shard_map/ppermute | solution.py:18
  93.3 7.2 %collective-permute-start.8 = (f32[16,1,2,128]{3,1,2,0:T(1,128)S(1)}, f32[16,1,2,128]{3,1,2,0:T(1,128)S(1)}, u32[]{:S(2)}, u32[]{:S(2)}) collective-permute-start(f32[16,1,2,128]{3,1,2,0:T(1,128)S(1)} %get-tuple-element.18), channel_id=1, source_target_pairs={{0,1},{1,2},{2,3},{3,4},{4,5},{5,6},{6,7},{8,9},{9,10},{10,11},{11... | collective-permute-start | bytes 49160 | tf_op jit(solution)/shard_map/ppermute | solution.py:15
where the time goes:
time: 104 us; the launch traced here: 103 us
  waiting for transfers between devices  60.4 us (58%)
  starting transfers between devices  29 us (28%)
  local copies, waits for them, and re-layouts  4.53 us (4%)
  matrix products  3.92 us (4%)
  other arithmetic  3.92 us (4%)
  between operations  1.22 us (1%)
    ppermute x6, waiting for transfers between devices, extended(): lax.ppermute(lax.slice_in_dim(block, block.shape[dim] - width, None, axis...  49.1 us
    ppermute x6, starting transfers between devices, extended(): lax.ppermute(lax.slice_in_dim(block, 0, width, axis=dim), axis, backward)  14.9 us
    ppermute x6, starting transfers between devices, extended(): lax.ppermute(lax.slice_in_dim(block, block.shape[dim] - width, None, axis...  14.2 us
    ppermute x6, waiting for transfers between devices, extended(): lax.ppermute(lax.slice_in_dim(block, 0, width, axis=dim), axis, backward)  11.3 us
    unnamed x17, local copies, waits for them, and re-layouts  3.36 us
    dot_general x3, matrix products, properties(): jnp.einsum('sr,rjki->sjki', thermal_collision_terms, fractions, precision...  2.49 us
  transfers between devices with their start and end apart: 12, of which 9 were waited for; matrix products, arithmetic and copies ran while one was open for 1% of the time, Pallas kernels for 0%

commit v1 on v0

v1 whole, which is shorter than its diff:
```python
import jax
import jax.numpy as jnp
import numpy as np
from jax import lax
from jax.experimental import pallas as pl
from jax.experimental.pallas import tpu as pltpu
from jax.sharding import PartitionSpec as P

MASSES = [28.0, 32.0, 30.0, 14.0, 16.0, 28.0, 32.0, 30.0, 14.0, 16.0, 0.00055]
STEP = 0.16
WN = 8
BLK = 96
RUN = 12
OWN = 32
ROWS = 48
LANES = 128
CHUNK = 24


def iota(shape, dim):
    return lax.broadcasted_iota(jnp.int32, shape, dim)


def set_ghost_rows(state, wn):
    sub = iota((8, LANES), 0)
    low, high = wn == 0, wn == WN - 1
    for v in range(14):
        first = state[v, 0:8]
        last = state[v, 24:32]
        above = state[v, 32:40]
        below = state[v, 40:48]
        state[v, 32:40] = jnp.where(high & (sub < 2), pltpu.roll(last, 2, 0), above)
        cut = jnp.where(sub == 6, pltpu.roll(first, 3, 0), pltpu.roll(first, 5, 0))
        state[v, 40:48] = jnp.where(low & (sub >= 6), cut, below)


def coefficients(state, coeff, shear, thermal):
    for c in range(ROWS // CHUNK):
        rows = pl.ds(c * CHUNK, CHUNK)
        x = [state[r, rows] for r in range(11)]
        logs = jnp.log(state[13, rows])
        visc = cond = None
        for s in range(11):
            dv = shear[s, 0] * x[0]
            dc = thermal[s, 0] * x[0]
            for r in range(1, 11):
                dv = dv + shear[s, r] * x[r]
                dc = dc + thermal[s, r] * x[r]
            tv = x[s] * np.float32(MASSES[s] / 28.0) / dv
            tc = x[s] / dc
            visc = tv if visc is None else visc + tv
            cond = tc if cond is None else cond + tc
        coeff[0, rows] = jnp.exp(0.7 * logs) * (0.5 * visc)
        coeff[1, rows] = jnp.exp(0.5 * logs) * (0.5 * cond)


def faces(coeff):
    out = []
    for k in (coeff[1], coeff[0]):
        out.append((k + pltpu.roll(k, ROWS - 2, 0), k + pltpu.roll(k, LANES - 1, 1)))
    return out


def residual(w, face):
    down, across = face
    f = down * (pltpu.roll(w, ROWS - 2, 0) - w)
    g = across * (pltpu.roll(w, LANES - 1, 1) - w)
    return (f - pltpu.roll(f, 2, 0)) + (g - pltpu.roll(g, 1, 1))


def sections(fix, w0, wa, wb, coeff, shear, thermal, emit):
    fix(w0)
    coefficients(w0, coeff, shear, thermal)
    face = faces(coeff)
    for v in range(14):
        w = w0[v]
        wa[v] = w + STEP * residual(w, face[v in (11, 12)])
    fix(wa)
    coefficients(wa, coeff, shear, thermal)
    face = faces(coeff)
    for v in range(14):
        w = wa[v]
        wb[v] = 0.75 * w0[v] + 0.25 * (w + STEP * residual(w, face[v in (11, 12)]))
    fix(wb)
    coefficients(wb, coeff, shear, thermal)
    face = faces(coeff)
    for v in range(14):
        w = wb[v]
        last = residual(w, face[v in (11, 12)])
        final = w0[v] * np.float32(1.0 / 3.0) + np.float32(2.0 / 3.0) * (w + STEP * last)
        emit(v, final[:OWN], last[:OWN])


def pack_columns(rows):
    missing = -rows.shape[0] % LANES
    if missing:
        rows = jnp.concatenate([rows, jnp.zeros((missing, LANES), jnp.float32)], axis=0)
    left, right = [], []
    for t in range(rows.shape[0] // LANES):
        turned = rows[t * LANES : (t + 1) * LANES].T
        left.append(turned[:8])
        right.append(turned[120:])
    return left, right


def load_kernel(species, flow, heat, block, left, right, corner, top, bottom):
    block[0:11] = species[...]
    block[11:13] = flow[...]
    block[13:14] = heat[...]
    lefts, rights = pack_columns(block[...].reshape(14 * OWN, LANES))
    for t in range(4):
        left[t] = lefts[t]
        right[t] = rights[t]
    low, high = block[:, 0:8], block[:, 24:32]
    bottom[...] = low
    top[...] = high
    _, rights = pack_columns(jnp.concatenate([low, high], axis=1).reshape(14 * 16, LANES))
    for t in range(2):
        corner[t] = rights[t]


def edge_kernel(above, below, left, right, pair, other):
    even = lax.axis_index("blk") % 2 == 0
    halo = jnp.concatenate([above[...], below[...]], axis=1).reshape(14 * 16, LANES)
    lefts, rights = pack_columns(halo)
    for t in range(6):
        lo = left[t] if t < 4 else lefts[t - 4]
        hi = right[t] if t < 4 else rights[t - 4]
        pair[t] = jnp.where(even, hi, lo)
        pair[t + 6] = lo
        other[t] = jnp.where(even, lo, hi)


def gather_rows(block, above, below, w0):
    for v in range(14):
        w0[v, 0:32] = block[v]
        w0[v, 32:40] = above[v]
        w0[v, 40:48] = below[v]


def main_kernel(block, above, below, shear, thermal, final, last, w0, wa, wb, coeff):
    wn = lax.axis_index("wn")
    gather_rows(block, above, below, w0)

    def emit(v, f, r):
        final[v] = f
        last[v] = r

    sections(lambda ref: set_ghost_rows(ref, wn), w0, wa, wb, coeff, shear, thermal, emit)


def strip_kernel(
    block, above, below, pair, other, relay, wrap, wrap_up, wrap_down, shear, thermal, main_final, main_last,
    final, last, w0, wa, wb, coeff,
):
    wn = lax.axis_index("wn")
    blk = lax.axis_index("blk")
    even = blk % 2 == 0
    place = blk % RUN
    lane = iota((ROWS, LANES), 1)
    gather_rows(block, above, below, w0)
    lane8 = iota((8, LANES), 1)
    tiles = []
    for t in range(6):
        if t < 4:
            from_wrap = wrap[t]
        else:
            from_wrap = jnp.where(lane8 % 16 < 8, wrap_up[t - 4], wrap_down[t - 4])
        lo = jnp.where(place == 0, from_wrap, jnp.where(even, other[t], pair[t]))
        hi = jnp.where(place == RUN - 1, relay[t], jnp.where(even, pair[t], other[t]))
        full = jnp.concatenate([hi, lo, jnp.zeros((112, LANES), jnp.float32)], axis=0)
        tiles.append(full.T)
    for v in range(14):
        own = w0[v]
        q, h = v % 4, v % 8
        side = jnp.concatenate([tiles[v // 4][q * 32 : q * 32 + 32], tiles[4 + v // 8][h * 16 : h * 16 + 16]], axis=0)
        w0[v] = jnp.where(lane < 16, side, jnp.where(lane < 72, pltpu.roll(own, 16, 1), own))

    first, nose = blk == 0, blk == BLK - 1
    even_row = iota((ROWS, LANES), 0) % 2 == 0

    def fix(ref):
        set_ghost_rows(ref, wn)

        @pl.when(first)
        def _():
            for v in range(14):
                w = ref[v]
                ref[v] = jnp.where(lane == 15, pltpu.roll(w, LANES - 1, 1), w)

        @pl.when(nose)
        def _():
            for v in range(14):
                w = ref[v]
                moved = pltpu.roll(w, 1, 1)
                swapped = jnp.where(even_row, pltpu.roll(moved, ROWS - 1, 0), pltpu.roll(moved, 1, 0))
                ref[v] = jnp.where(lane == 0, swapped, w)

    lane_own = iota((OWN, LANES), 1)

    def emit(v, f, r):
        for out, new, old in ((final, f, main_final), (last, r, main_last)):
            out[v] = jnp.where(lane_own < 3, pltpu.roll(new, LANES - 16, 1), jnp.where(lane_own >= 125, new, old[v]))

    sections(fix, w0, wa, wb, coeff, shear, thermal, emit)


VMEM = pl.BlockSpec(memory_space=pltpu.VMEM)
SMEM = pl.BlockSpec(memory_space=pltpu.SMEM)
SCRATCH = [pltpu.VMEM((14, ROWS, LANES), jnp.float32)] * 3 + [pltpu.VMEM((2, ROWS, LANES), jnp.float32)]
PARAMS = pltpu.CompilerParams(vmem_limit_bytes=12 * 1024 * 1024)


def f32(*shape):
    return jax.ShapeDtypeStruct(shape, jnp.float32)


def call(kernel, outs, ins, scratch=()):
    return pl.pallas_call(
        kernel, out_shape=outs, in_specs=ins, out_specs=tuple(VMEM for _ in outs), scratch_shapes=scratch, compiler_params=PARAMS
    )


def at(blk, wn):
    return blk * WN + wn


def send(x, pairs):
    return lax.ppermute(x, ("blk", "wn"), pairs)


def wrap_pairs(shift):
    return [
        (at(b, w), at(b + 1, w + shift))
        for b in range(RUN - 1, BLK - 1, RUN)
        for w in range(WN)
        if 0 <= w + shift < WN
    ]


PAIRS = [(at(b + i, w), at(b + 1 - i, w)) for b in range(0, BLK, 2) for w in range(WN) for i in range(2)]
OTHERS = [
    (at(b + i, w), at(b + 1 - i, w)) for b in range(1, BLK - 1, 2) if (b + 1) % RUN for w in range(WN) for i in range(2)
]
RELAY = [(at(b + 1, w), at(b - 1, w)) for b in range(RUN, BLK, RUN) for w in range(WN)]
UP = [(at(b, w), at(b, w + 1)) for b in range(BLK) for w in range(WN - 1)]
DOWN = [(target, source) for source, target in UP]


def local(species, flow, heat, shear, thermal):
    species = species.reshape(11, OWN, LANES)
    flow = flow.reshape(2, OWN, LANES)
    heat = heat.reshape(1, OWN, LANES)
    block, left, right, corner, top, bottom = call(
        load_kernel,
        (f32(14, OWN, LANES), f32(4, 8, LANES), f32(4, 8, LANES), f32(2, 8, LANES), f32(14, 8, LANES), f32(14, 8, LANES)),
        [VMEM] * 3,
    )(species, flow, heat)
    wrap_up = send(corner, wrap_pairs(-1))
    wrap = send(right, wrap_pairs(0))
    wrap_down = send(corner, wrap_pairs(1))
    above = send(bottom, DOWN)
    below = send(top, UP)
    pair, other = call(edge_kernel, (f32(12, 8, LANES), f32(6, 8, LANES)), [VMEM] * 4)(above, below, left, right)
    got_pair = send(pair, PAIRS)
    got_other = send(other, OTHERS)
    relay = send(got_pair[6:], RELAY)
    out = f32(14, OWN, LANES)
    main_final, main_last = call(main_kernel, (out, out), [VMEM] * 3 + [SMEM] * 2, SCRATCH)(block, above, below, shear, thermal)
    final, last = call(strip_kernel, (out, out), [VMEM] * 9 + [SMEM] * 2 + [VMEM] * 2, SCRATCH)(
        block, above, below, got_pair, got_other, relay, wrap, wrap_up, wrap_down, shear, thermal, main_final, main_last
    )
    return final.reshape(14, 16, 2, LANES), last.reshape(14, 16, 2, LANES)


def solution(mesh):
    return jax.shard_map(
        local,
        mesh=mesh,
        in_specs=(P(None, "wn", None, "blk"), P(None, "wn", None, "blk"), P("wn", None, "blk"), P(), P()),
        out_specs=(P(None, "wn", None, "blk"), P(None, "wn", None, "blk")),
        check_vma=False,
    )
```

time: 104 us -> 47.8 us (0.46)
  the two profiles are of different devices: /device:TPU:40 before, /device:TPU:25 now
where the time goes in v1:
time: 47.8 us; the launch traced here: 47.4 us
  waiting for transfers between devices  19.1 us (40%)
  starting transfers between devices  17 us (36%)
  Pallas kernels  8.05 us (17%)
  local copies, waits for them, and re-layouts  2.4 us (5%)
  between operations  0.76 us (2%)
    ppermute x8, waiting for transfers between devices, send(): return lax.ppermute(x, ('blk', 'wn'), pairs)  19.1 us
    ppermute x8, starting transfers between devices, send(): return lax.ppermute(x, ('blk', 'wn'), pairs)  17 us
    pallas_call x1, Pallas kernels, local(): call(strip_kernel, (out, out), [VMEM] * 9 + [SMEM] * 2 + [VMEM] * 2, SCRA...  4.42 us
    pallas_call x1, Pallas kernels, local(): call(main_kernel, (out, out), [VMEM] * 3 + [SMEM] * 2, SCRATCH)  3.38 us
    unnamed x10, local copies, waits for them, and re-layouts  2.4 us
  transfers between devices with their start and end apart: 8, of which 4 were waited for; matrix products, arithmetic and copies ran while one was open for 0% of the time, Pallas kernels for 7%

profile of v1, /device:TPU:25, one launch (start us, length us, event | category | flops | bytes accessed | tf_op | source)
XLA Modules:
  0.0 47.4 jit_solution(1241352981624864711)
XLA Ops:
  0.6 0.0 copy-start
  0.6 0.9 %copy-done = f32[11,16,2,128]{3,2,1,0:T(2,128)S(1)} copy-done((f32[11,16,2,128]{3,2,1,0:T(2,128)S(1)}, f32[11,16,2,128]{3,2,1,0:T(2,128)}, u32[]{:S(2)}) %copy-start) | copy-done | bytes 180248
  1.6 0.0 copy-start.1
  1.6 0.8 %copy-done.1 = f32[2,16,2,128]{3,2,1,0:T(2,128)S(1)} copy-done((f32[2,16,2,128]{3,2,1,0:T(2,128)S(1)}, f32[2,16,2,128]{3,2,1,0:T(2,128)}, u32[]{:S(2)}) %copy-start.1) | copy-done | bytes 32792
  2.3 0.0 copy-start.4
  2.3 0.7 %copy-done.4 = f32[16,2,128]{2,1,0:T(2,128)S(1)} copy-done((f32[16,2,128]{2,1,0:T(2,128)S(1)}, f32[16,2,128]{2,1,0:T(2,128)}, u32[]{:S(2)}) %copy-start.4) | copy-done | bytes 16408
  3.0 0.2 shard_map.68
  3.2 2.6 %collective-permute-start = (f32[14,8,128]{2,1,0:T(8,128)S(1)}, f32[14,8,128]{2,1,0:T(8,128)S(1)}, u32[]{:S(2)}, u32[]{:S(2)}) collective-permute-start(f32[14,8,128]{2,1,0:T(8,128)S(1)} %get-tuple-element.15), channel_id=1, source_target_pairs={{1,0},{2,1},{3,2},{4,3},{5,4},{6,5},{7,6},{9,8},{10,9},{11,10},{12... | collective-permute-start | bytes 172040 | tf_op jit(solution)/shard_map/ppermute | solution.py:229
  5.8 5.1 %collective-permute-start.1 = (f32[14,8,128]{2,1,0:T(8,128)S(1)}, f32[14,8,128]{2,1,0:T(8,128)S(1)}, u32[]{:S(2)}, u32[]{:S(2)}) collective-permute-start(f32[14,8,128]{2,1,0:T(8,128)S(1)} %get-tuple-element.16), channel_id=1, source_target_pairs={{0,1},{1,2},{2,3},{3,4},{4,5},{5,6},{6,7},{8,9},{9,10},{10,11},{11... | collective-permute-start | bytes 172040 | tf_op jit(solution)/shard_map/ppermute | solution.py:229
  10.9 0.0 collective-permute-done.above
  10.9 1.7 %collective-permute-done.1.below = f32[14,8,128]{2,1,0:T(8,128)S(1)} collective-permute-done((f32[14,8,128]{2,1,0:T(8,128)S(1)}, f32[14,8,128]{2,1,0:T(8,128)S(1)}, u32[]{:S(2)}, u32[]{:S(2)}) %collective-permute-start.1) | collective-permute-done | bytes 57376 | tf_op jit(solution)/shard_map/ppermute | solution.py:229
  12.6 0.1 shard_map.69
  12.7 4.0 %collective-permute-start.2 = (f32[12,8,128]{2,1,0:T(8,128)S(1)}, f32[12,8,128]{2,1,0:T(8,128)S(1)}, u32[]{:S(2)}, u32[]{:S(2)}) collective-permute-start(f32[12,8,128]{2,1,0:T(8,128)S(1)} %get-tuple-element.19), channel_id=1, source_target_pairs={{0,8},{8,0},{1,9},{9,1},{2,10},{10,2},{3,11},{11,3},{4,12},{12,4},... | collective-permute-start | bytes 147464 | tf_op jit(solution)/shard_map/ppermute | solution.py:229
  16.7 0.7 %collective-permute-start.3 = (f32[6,8,128]{2,1,0:T(8,128)S(1)}, f32[6,8,128]{2,1,0:T(8,128)S(1)}, u32[]{:S(2)}, u32[]{:S(2)}) collective-permute-start(f32[6,8,128]{2,1,0:T(8,128)S(1)} %get-tuple-element.20), channel_id=1, source_target_pairs={{8,16},{16,8},{9,17},{17,9},{10,18},{18,10},{11,19},{19,11},{12,20... | collective-permute-start | bytes 73736 | tf_op jit(solution)/shard_map/ppermute | solution.py:229
  17.4 1.3 %collective-permute-done.2.pair = f32[12,8,128]{2,1,0:T(8,128)S(1)} collective-permute-done((f32[12,8,128]{2,1,0:T(8,128)S(1)}, f32[12,8,128]{2,1,0:T(8,128)S(1)}, u32[]{:S(2)}, u32[]{:S(2)}) %collective-permute-start.2) | collective-permute-done | bytes 49184 | tf_op jit(solution)/shard_map/ppermute | solution.py:229
  18.7 0.0 copy-start.2
  18.7 0.0 copy-start.3
  18.7 0.8 %collective-permute-start.4 = (f32[6,8,128]{2,1,0:T(8,128)S(1)}, f32[6,8,128]{2,1,0:T(8,128)S(1)}, u32[]{:S(2)}, u32[]{:S(2)}) collective-permute-start(f32[6,8,128]{2,1,0:T(8,128)S(1)} %slice.4), channel_id=1, source_target_pairs={{104,88},{105,89},{106,90},{107,91},{108,92},{109,93},{110,94},{11... | collective-permute-start | bytes 73736 | tf_op jit(solution)/shard_map/ppermute | solution.py:229
  19.5 1.3 %collective-permute-start.5 = (f32[4,8,128]{2,1,0:T(8,128)S(1)}, f32[4,8,128]{2,1,0:T(8,128)S(1)}, u32[]{:S(2)}, u32[]{:S(2)}) collective-permute-start(f32[4,8,128]{2,1,0:T(8,128)S(1)} %get-tuple-element.18.right), channel_id=1, source_target_pairs={{88,96},{89,97},{90,98},{91,99},{92,100},{93,101},{94,102},{95,103... | collective-permute-start | bytes 49160 | tf_op jit(solution)/shard_map/ppermute | solution.py:229
  20.8 1.3 %collective-permute-start.7 = (f32[2,8,128]{2,1,0:T(8,128)S(1)}, f32[2,8,128]{2,1,0:T(8,128)S(1)}, u32[]{:S(2)}, u32[]{:S(2)}) collective-permute-start(f32[2,8,128]{2,1,0:T(8,128)S(1)} %get-tuple-element.21), channel_id=1, source_target_pairs={{88,97},{89,98},{90,99},{91,100},{92,101},{93,102},{94,103},{184,1... | collective-permute-start | bytes 24584 | tf_op jit(solution)/shard_map/ppermute | solution.py:229
  22.1 1.3 %collective-permute-start.6 = (f32[2,8,128]{2,1,0:T(8,128)S(1)}, f32[2,8,128]{2,1,0:T(8,128)S(1)}, u32[]{:S(2)}, u32[]{:S(2)}) collective-permute-start(f32[2,8,128]{2,1,0:T(8,128)S(1)} %get-tuple-element.21), channel_id=1, source_target_pairs={{89,96},{90,97},{91,98},{92,99},{93,100},{94,101},{95,102},{185,19... | collective-permute-start | bytes 24584 | tf_op jit(solution)/shard_map/ppermute | solution.py:229
  23.4 0.0 copy-done.2
  23.4 0.0 copy-done.3
  23.4 3.4 %shard_map.70 = (f32[14,32,128]{2,1,0:T(8,128)S(1)}, f32[14,32,128]{2,1,0:T(8,128)S(1)}) custom-call(f32[14,32,128]{2,1,0:T(8,128)S(1)} %get-tuple-element.14.block, f32[14,8,128]{2,1,0:T(8,128)S(1)} %collective-permute-done.above, f32[14,8,128]{2,1,0:T(8,128)S(1)} %collective-permute-done.1.below, f32[11,11]{1,0:T(8,128)S(1)} %copy-done.2, ...), custom_call_target="tpu_custom_call" | custom-call | tf_op jit(solution)/shard_map/pallas_call | solution.py:269
  26.8 11.4 %collective-permute-done.7.wrap_down = f32[2,8,128]{2,1,0:T(8,128)S(1)} collective-permute-done((f32[2,8,128]{2,1,0:T(8,128)S(1)}, f32[2,8,128]{2,1,0:T(8,128)S(1)}, u32[]{:S(2)}, u32[]{:S(2)}) %collective-permute-start.7) | collective-permute-done | bytes 8224 | tf_op jit(solution)/shard_map/ppermute | solution.py:229
  38.2 4.7 %collective-permute-done.6.wrap_up = f32[2,8,128]{2,1,0:T(8,128)S(1)} collective-permute-done((f32[2,8,128]{2,1,0:T(8,128)S(1)}, f32[2,8,128]{2,1,0:T(8,128)S(1)}, u32[]{:S(2)}, u32[]{:S(2)}) %collective-permute-start.6) | collective-permute-done | bytes 8224 | tf_op jit(solution)/shard_map/ppermute | solution.py:229
  42.9 0.0 collective-permute-done.5.wrap
  42.9 0.0 collective-permute-done.3.other
  42.9 0.0 collective-permute-done.4.relay
  42.9 4.4 %shard_map.71 = (f32[14,32,128]{2,1,0:T(8,128)}, f32[14,32,128]{2,1,0:T(8,128)}) custom-call(f32[14,32,128]{2,1,0:T(8,128)S(1)} %get-tuple-element.14.block, f32[14,8,128]{2,1,0:T(8,128)S(1)} %collective-permute-done.above, f32[14,8,128]{2,1,0:T(8,128)S(1)} %collective-permute-done.1.below, f32[12,8,128]{2,1,0:T(8,128)S(1)} %collective-permute-done.2.pair, ...), custom_call_target="tpu_custom_call" | custom-call | tf_op jit(solution)/shard_map/pallas_call | solution.py:270
  (1 shorter events, 0.0 us)
Async XLA Ops:
  0.6 0.9 %copy-start = (f32[11,16,2,128]{3,2,1,0:T(2,128)S(1)}, f32[11,16,2,128]{3,2,1,0:T(2,128)}, u32[]{:S(2)}) copy-start(f32[11,16,2,128]{3,2,1,0:T(2,128)} %param.5) | copy-start | bytes 540676
  1.6 0.8 %copy-start.1 = (f32[2,16,2,128]{3,2,1,0:T(2,128)S(1)}, f32[2,16,2,128]{3,2,1,0:T(2,128)}, u32[]{:S(2)}) copy-start(f32[2,16,2,128]{3,2,1,0:T(2,128)} %param.6) | copy-start | bytes 98308
  2.3 0.7 %copy-start.4 = (f32[16,2,128]{2,1,0:T(2,128)S(1)}, f32[16,2,128]{2,1,0:T(2,128)}, u32[]{:S(2)}) copy-start(f32[16,2,128]{2,1,0:T(2,128)} %param.7) | copy-start | bytes 49156
  3.2 7.7 %collective-permute-start = (f32[14,8,128]{2,1,0:T(8,128)S(1)}, f32[14,8,128]{2,1,0:T(8,128)S(1)}, u32[]{:S(2)}, u32[]{:S(2)}) collective-permute-start(f32[14,8,128]{2,1,0:T(8,128)S(1)} %get-tuple-element.15), channel_id=1, source_target_pairs={{1,0},{2,1},{3,2},{4,3},{5,4},{6,5},{7,6},{9,8},{10,9},{11,10},{12... | collective-permute-start | bytes 172040 | tf_op jit(solution)/shard_map/ppermute | solution.py:229
  5.8 6.8 %collective-permute-start.1 = (f32[14,8,128]{2,1,0:T(8,128)S(1)}, f32[14,8,128]{2,1,0:T(8,128)S(1)}, u32[]{:S(2)}, u32[]{:S(2)}) collective-permute-start(f32[14,8,128]{2,1,0:T(8,128)S(1)} %get-tuple-element.16), channel_id=1, source_target_pairs={{0,1},{1,2},{2,3},{3,4},{4,5},{5,6},{6,7},{8,9},{9,10},{10,11},{11... | collective-permute-start | bytes 172040 | tf_op jit(solution)/shard_map/ppermute | solution.py:229
  12.7 6.0 %collective-permute-start.2 = (f32[12,8,128]{2,1,0:T(8,128)S(1)}, f32[12,8,128]{2,1,0:T(8,128)S(1)}, u32[]{:S(2)}, u32[]{:S(2)}) collective-permute-start(f32[12,8,128]{2,1,0:T(8,128)S(1)} %get-tuple-element.19), channel_id=1, source_target_pairs={{0,8},{8,0},{1,9},{9,1},{2,10},{10,2},{3,11},{11,3},{4,12},{12,4},... | collective-permute-start | bytes 147464 | tf_op jit(solution)/shard_map/ppermute | solution.py:229
  16.7 26.2 %collective-permute-start.3 = (f32[6,8,128]{2,1,0:T(8,128)S(1)}, f32[6,8,128]{2,1,0:T(8,128)S(1)}, u32[]{:S(2)}, u32[]{:S(2)}) collective-permute-start(f32[6,8,128]{2,1,0:T(8,128)S(1)} %get-tuple-element.20), channel_id=1, source_target_pairs={{8,16},{16,8},{9,17},{17,9},{10,18},{18,10},{11,19},{19,11},{12,20... | collective-permute-start | bytes 73736 | tf_op jit(solution)/shard_map/ppermute | solution.py:229
  18.7 4.7 %copy-start.2 = (f32[11,11]{1,0:T(8,128)S(1)}, f32[11,11]{1,0:T(8,128)}, u32[]{:S(2)}) copy-start(f32[11,11]{1,0:T(8,128)} %shear.3) | copy-start | bytes 1456
  18.7 4.7 %copy-start.3 = (f32[11,11]{1,0:T(8,128)S(1)}, f32[11,11]{1,0:T(8,128)}, u32[]{:S(2)}) copy-start(f32[11,11]{1,0:T(8,128)} %thermal.3) | copy-start | bytes 1456
  18.7 24.2 %collective-permute-start.4 = (f32[6,8,128]{2,1,0:T(8,128)S(1)}, f32[6,8,128]{2,1,0:T(8,128)S(1)}, u32[]{:S(2)}, u32[]{:S(2)}) collective-permute-start(f32[6,8,128]{2,1,0:T(8,128)S(1)} %slice.4), channel_id=1, source_target_pairs={{104,88},{105,89},{106,90},{107,91},{108,92},{109,93},{110,94},{11... | collective-permute-start | bytes 73736 | tf_op jit(solution)/shard_map/ppermute | solution.py:229
  19.5 23.4 %collective-permute-start.5 = (f32[4,8,128]{2,1,0:T(8,128)S(1)}, f32[4,8,128]{2,1,0:T(8,128)S(1)}, u32[]{:S(2)}, u32[]{:S(2)}) collective-permute-start(f32[4,8,128]{2,1,0:T(8,128)S(1)} %get-tuple-element.18.right), channel_id=1, source_target_pairs={{88,96},{89,97},{90,98},{91,99},{92,100},{93,101},{94,102},{95,103... | collective-permute-start | bytes 49160 | tf_op jit(solution)/shard_map/ppermute | solution.py:229
  20.8 17.4 %collective-permute-start.7 = (f32[2,8,128]{2,1,0:T(8,128)S(1)}, f32[2,8,128]{2,1,0:T(8,128)S(1)}, u32[]{:S(2)}, u32[]{:S(2)}) collective-permute-start(f32[2,8,128]{2,1,0:T(8,128)S(1)} %get-tuple-element.21), channel_id=1, source_target_pairs={{88,97},{89,98},{90,99},{91,100},{92,101},{93,102},{94,103},{184,1... | collective-permute-start | bytes 24584 | tf_op jit(solution)/shard_map/ppermute | solution.py:229
  22.1 20.8 %collective-permute-start.6 = (f32[2,8,128]{2,1,0:T(8,128)S(1)}, f32[2,8,128]{2,1,0:T(8,128)S(1)}, u32[]{:S(2)}, u32[]{:S(2)}) collective-permute-start(f32[2,8,128]{2,1,0:T(8,128)S(1)} %get-tuple-element.21), channel_id=1, source_target_pairs={{89,96},{90,97},{91,98},{92,99},{93,100},{94,101},{95,102},{185,19... | collective-permute-start | bytes 24584 | tf_op jit(solution)/shard_map/ppermute | solution.py:229

commit v2 on v1

--- a/solution.py
+++ b/solution.py
@@ -103,44 +103,90 @@
     return left, right
 
 
-def load_kernel(species, flow, heat, block, left, right, corner, top, bottom):
-    block[0:11] = species[...]
-    block[11:13] = flow[...]
-    block[13:14] = heat[...]
-    lefts, rights = pack_columns(block[...].reshape(14 * OWN, LANES))
+def load_kernel(species, flow, heat, block, right, corner, sems):
+    copies = [
+        pltpu.make_async_copy(source, block.at[pl.ds(low, count)], sems.at[i])
+        for i, (source, low, count) in enumerate(((species, 0, 11), (flow, 11, 2), (heat, 13, 1)))
+    ]
+    for copy in copies:
+        copy.start()
+    for copy in copies:
+        copy.wait()
+    _, rights = pack_columns(block[...].reshape(14 * OWN, LANES))
     for t in range(4):
-        left[t] = lefts[t]
         right[t] = rights[t]
     low, high = block[:, 0:8], block[:, 24:32]
-    bottom[...] = low
-    top[...] = high
     _, rights = pack_columns(jnp.concatenate([low, high], axis=1).reshape(14 * 16, LANES))
     for t in range(2):
         corner[t] = rights[t]
 
 
-def edge_kernel(above, below, left, right, pair, other):
+def second_rows_kernel(block, second):
+    even = lax.axis_index("wn") % 2 == 0
+    second[...] = jnp.where(even, block[:, 0:8], block[:, 24:32])
+
+
+def first_rows_kernel(block, after, first):
+    even = lax.axis_index("wn") % 2 == 0
+    for v in range(14):
+        first[pl.ds(6 * v, 6)] = jnp.where(even, block[v, 26:32], block[v, 0:6])
+
+
+def pass_kernel(value, after, out):
+    out[...] = value[...]
+
+
+def halo_of(first, second):
+    even = lax.axis_index("wn") % 2 == 0
+    zeros = jnp.zeros((2, LANES), jnp.float32)
+    two = second[...]
+    one = [first[pl.ds(6 * v, 6)] for v in range(14)]
+    above = jnp.stack([jnp.concatenate([x, zeros], axis=0) for x in one])
+    below = jnp.stack([jnp.concatenate([zeros, x], axis=0) for x in one])
+    return jnp.concatenate([jnp.where(even, above, two), jnp.where(even, two, below)], axis=1)
+
+
+def columns_of(block, halo):
+    lefts, rights = pack_columns(block[...].reshape(14 * OWN, LANES))
+    lefts_halo, rights_halo = pack_columns(halo.reshape(14 * 16, LANES))
+    return lefts + lefts_halo, rights + rights_halo
+
+
+def early_columns_kernel(first, second, block, halo, pair, lows, highs):
     even = lax.axis_index("blk") % 2 == 0
-    halo = jnp.concatenate([above[...], below[...]], axis=1).reshape(14 * 16, LANES)
-    lefts, rights = pack_columns(halo)
+    halo[...] = halo_of(first, second)
+    lefts, rights = columns_of(block, halo[...])
     for t in range(6):
-        lo = left[t] if t < 4 else lefts[t - 4]
-        hi = right[t] if t < 4 else rights[t - 4]
-        pair[t] = jnp.where(even, hi, lo)
-        pair[t + 6] = lo
-        other[t] = jnp.where(even, lo, hi)
-
-
-def gather_rows(block, above, below, w0):
-    for v in range(14):
-        w0[v, 0:32] = block[v]
-        w0[v, 32:40] = above[v]
-        w0[v, 40:48] = below[v]
-
-
-def main_kernel(block, above, below, shear, thermal, final, last, w0, wa, wb, coeff):
+        three = pl.ds(3 * t, 3)
+        pair[three] = jnp.where(even, rights[t][5:8], lefts[t][0:3])
+        lows[three] = lefts[t][0:3]
+        highs[three] = rights[t][5:8]
+
+
+def late_columns_kernel(first, second, block, halo, lows, highs):
+    halo[...] = halo_of(first, second)
+    lefts, rights = columns_of(block, halo[...])
+    for t in range(6):
+        three = pl.ds(3 * t, 3)
+        highs[three] = rights[t][5:8]
+        lows[three] = lefts[t][0:3]
+
+
+def keep_kernel(early_lows, early_highs, lows, highs):
+    lows[...] = early_lows[...]
+    highs[...] = early_highs[...]
+
+
+def gather_rows(block, halo, w0):
+    for v in range(14):
+        w0[v, 0:OWN] = block[v]
+        w0[v, OWN:ROWS] = halo[v]
+
+
+def main_sections(block, halo, shear, thermal, final, last, w0, wa, wb, coeff):
     wn = lax.axis_index("wn")
-    gather_rows(block, above, below, w0)
+    if halo is not None:
+        gather_rows(block, halo, w0)
 
     def emit(v, f, r):
         final[v] = f
@@ -149,26 +195,58 @@
     sections(lambda ref: set_ghost_rows(ref, wn), w0, wa, wb, coeff, shear, thermal, emit)
 
 
-def strip_kernel(
-    block, above, below, pair, other, relay, wrap, wrap_up, wrap_down, shear, thermal, main_final, main_last,
-    final, last, w0, wa, wb, coeff,
+def early_main_kernel(block, halo, shear, thermal, final, last, w0, wa, wb, coeff):
+    main_sections(block, halo, shear, thermal, final, last, w0, wa, wb, coeff)
+
+
+def idle_kernel(*refs):
+    pass
+
+
+def last_kernel(
+    block, early_halo, late_halo, early_pair, left, right, relay, wrap, wrap_up, wrap_down, shear, thermal, main_final, main_last,
+    final, last, w0, wa, wb, coeff, sems,
 ):
     wn = lax.axis_index("wn")
     blk = lax.axis_index("blk")
-    even = blk % 2 == 0
     place = blk % RUN
+
+    halo_rows = w0.at[:, pl.ds(OWN, 16)]
+    mains = [pltpu.make_async_copy(a, b, sems.at[i]) for i, (a, b) in enumerate(((main_final, final), (main_last, last)))]
+
+    @pl.when(place == 0)
+    def _():
+        for copy in mains:
+            copy.start()
+
+    for known, halo in ((place <= 1, early_halo), (place > 1, late_halo)):
+
+        @pl.when(known)
+        def _():
+            copy = pltpu.make_async_copy(halo, halo_rows, sems.at[2])
+            copy.start()
+            for v in range(14):
+                w0[v, 0:OWN] = block[v]
+            copy.wait()
+
+    @pl.when(place != 0)
+    def _():
+        main_sections(block, None, shear, thermal, final, last, w0, wa, wb, coeff)
+
     lane = iota((ROWS, LANES), 1)
-    gather_rows(block, above, below, w0)
-    lane8 = iota((8, LANES), 1)
+    for v in range(14):
+        w0[v, 0:OWN] = block[v]
+    lane3 = iota((3, LANES), 1)
     tiles = []
     for t in range(6):
+        three = pl.ds(3 * t, 3)
         if t < 4:
-            from_wrap = wrap[t]
+            from_wrap = wrap[t, 5:8]
         else:
-            from_wrap = jnp.where(lane8 % 16 < 8, wrap_up[t - 4], wrap_down[t - 4])
-        lo = jnp.where(place == 0, from_wrap, jnp.where(even, other[t], pair[t]))
-        hi = jnp.where(place == RUN - 1, relay[t], jnp.where(even, pair[t], other[t]))
-        full = jnp.concatenate([hi, lo, jnp.zeros((112, LANES), jnp.float32)], axis=0)
+            from_wrap = jnp.where(lane3 % 16 < 8, wrap_up[t - 4, 5:8], wrap_down[t - 4, 5:8])
+        lo = jnp.where(place == 0, from_wrap, jnp.where(place == 1, early_pair[three], left[three]))
+        hi = jnp.where(place == RUN - 1, relay[three], jnp.where(place == 0, early_pair[three], right[three]))
+        full = jnp.concatenate([hi, jnp.zeros((10, LANES), jnp.float32), lo, jnp.zeros((112, LANES), jnp.float32)], axis=0)
         tiles.append(full.T)
     for v in range(14):
         own = w0[v]
@@ -199,13 +277,22 @@
     lane_own = iota((OWN, LANES), 1)
 
     def emit(v, f, r):
-        for out, new, old in ((final, f, main_final), (last, r, main_last)):
-            out[v] = jnp.where(lane_own < 3, pltpu.roll(new, LANES - 16, 1), jnp.where(lane_own >= 125, new, old[v]))
+        if v == 0:
+
+            @pl.when(place == 0)
+            def _():
+                for copy in mains:
+                    copy.wait()
+
+        for out, new in ((final, f), (last, r)):
+            out[v] = jnp.where(lane_own < 3, pltpu.roll(new, LANES - 16, 1), jnp.where(lane_own >= 125, new, out[v]))
 
     sections(fix, w0, wa, wb, coeff, shear, thermal, emit)
 
 
 VMEM = pl.BlockSpec(memory_space=pltpu.VMEM)
+HBM = pl.BlockSpec(memory_space=pltpu.HBM)
+ANY = pl.BlockSpec(memory_space=pl.ANY)
 SMEM = pl.BlockSpec(memory_space=pltpu.SMEM)
 SCRATCH = [pltpu.VMEM((14, ROWS, LANES), jnp.float32)] * 3 + [pltpu.VMEM((2, ROWS, LANES), jnp.float32)]
 PARAMS = pltpu.CompilerParams(vmem_limit_bytes=12 * 1024 * 1024)
@@ -217,7 +304,8 @@
 
 def call(kernel, outs, ins, scratch=()):
     return pl.pallas_call(
-        kernel, out_shape=outs, in_specs=ins, out_specs=tuple(VMEM for _ in outs), scratch_shapes=scratch, compiler_params=PARAMS
+        kernel, out_shape=outs, in_specs=ins, out_specs=tuple(VMEM for _ in outs), scratch_shapes=scratch, compiler_params=PARAMS,
+        cost_estimate=pl.CostEstimate(flops=1, bytes_accessed=1, transcendentals=0),
     )
 
 
@@ -238,37 +326,117 @@
     ]
 
 
-PAIRS = [(at(b + i, w), at(b + 1 - i, w)) for b in range(0, BLK, 2) for w in range(WN) for i in range(2)]
-OTHERS = [
-    (at(b + i, w), at(b + 1 - i, w)) for b in range(1, BLK - 1, 2) if (b + 1) % RUN for w in range(WN) for i in range(2)
-]
-RELAY = [(at(b + 1, w), at(b - 1, w)) for b in range(RUN, BLK, RUN) for w in range(WN)]
-UP = [(at(b, w), at(b, w + 1)) for b in range(BLK) for w in range(WN - 1)]
-DOWN = [(target, source) for source, target in UP]
+def swap(pairs):
+    return pairs + [(target, source) for source, target in pairs]
+
+
+def rows_pairs(start, early):
+    return swap([
+        (at(b, w), at(b, w + 1)) for b in range(BLK) if (b % RUN < 2 if early else b % RUN > 1) for w in range(start, WN - 1, 2)
+    ])
+
+
+def columns_pairs(places):
+    return [(at(b, w), at(b + 1, w)) for b in range(BLK - 1) if b % RUN in places for w in range(WN)]
+
+
+FIRST = swap(columns_pairs((0,)))
+FORWARD = columns_pairs(range(1, RUN - 1))
+BACKWARD = [(target, source) for source, target in FORWARD]
+RELAY = [(at(b, w), at(b - 1, w)) for b in range(RUN, BLK, RUN) for w in range(WN)]
+
+
+def idle(*outs):
+    return tuple(pl.pallas_call(idle_kernel, out_shape=outs, out_specs=tuple(HBM for _ in outs))())
+
+
+def in_hbm(x):
+    return pltpu.with_memory_space_constraint(x, pltpu.HBM)
 
 
 def local(species, flow, heat, shear, thermal):
-    species = species.reshape(11, OWN, LANES)
-    flow = flow.reshape(2, OWN, LANES)
-    heat = heat.reshape(1, OWN, LANES)
-    block, left, right, corner, top, bottom = call(
+    strips = f32(18, LANES)
+    rows = f32(14, 8, LANES)
+    halo_shape = f32(14, 16, LANES)
+    out = f32(14, OWN, LANES)
+    place = lax.axis_index("blk") % RUN
+    shear, thermal = in_hbm(shear), in_hbm(thermal)
+    block, right, corner = call(
         load_kernel,
-        (f32(14, OWN, LANES), f32(4, 8, LANES), f32(4, 8, LANES), f32(2, 8, LANES), f32(14, 8, LANES), f32(14, 8, LANES)),
-        [VMEM] * 3,
-    )(species, flow, heat)
+        (out, f32(4, 8, LANES), f32(2, 8, LANES)),
+        [HBM] * 3,
+        [pltpu.SemaphoreType.DMA((3,))],
+    )(in_hbm(species.reshape(11, OWN, LANES)), in_hbm(flow.reshape(2, OWN, LANES)), in_hbm(heat.reshape(1, OWN, LANES)))
     wrap_up = send(corner, wrap_pairs(-1))
     wrap = send(right, wrap_pairs(0))
     wrap_down = send(corner, wrap_pairs(1))
-    above = send(bottom, DOWN)
-    below = send(top, UP)
-    pair, other = call(edge_kernel, (f32(12, 8, LANES), f32(6, 8, LANES)), [VMEM] * 4)(above, below, left, right)
-    got_pair = send(pair, PAIRS)
-    got_other = send(other, OTHERS)
-    relay = send(got_pair[6:], RELAY)
-    out = f32(14, OWN, LANES)
-    main_final, main_last = call(main_kernel, (out, out), [VMEM] * 3 + [SMEM] * 2, SCRATCH)(block, above, below, shear, thermal)
-    final, last = call(strip_kernel, (out, out), [VMEM] * 9 + [SMEM] * 2 + [VMEM] * 2, SCRATCH)(
-        block, above, below, got_pair, got_other, relay, wrap, wrap_up, wrap_down, shear, thermal, main_final, main_last
+
+    def exchange_rows(block, early):
+        second = call(second_rows_kernel, (rows,), [VMEM])(block)[0]
+        second = send(second, rows_pairs(1, early))
+        first = call(first_rows_kernel, (f32(84, LANES),), [VMEM, ANY])(block, block if early else second)[0]
+        first = send(first, rows_pairs(0, early))
+        return first, second
+
+    def early(block, shear, thermal):
+        first, second = exchange_rows(block, True)
+        halo, pair, lows, highs = call(early_columns_kernel, (halo_shape, strips, strips, strips), [VMEM] * 3)(first, second, block)
+        pair = send(pair, FIRST)
+        final, last = lax.cond(place == 0, main, no_main, block, halo, shear, thermal)
+        return halo, pair, lows, highs, final, last
+
+    def not_early(block, shear, thermal):
+        return idle(halo_shape, strips, strips, strips, out, out)
+
+    def main(block, halo, shear, thermal):
+        return tuple(call(early_main_kernel, (out, out), [VMEM] * 2 + [SMEM] * 2, SCRATCH)(block, halo, shear, thermal))
+
+    def no_main(block, halo, shear, thermal):
+        return idle(out, out)
+
+    def edges(block, lows, highs):
+        first, second = exchange_rows(block, False)
+        return tuple(call(late_columns_kernel, (halo_shape, strips, strips), [VMEM] * 3)(first, second, block))
+
+    def known_edges(block, lows, highs):
+        return (*idle(halo_shape), *call(keep_kernel, (strips, strips), [VMEM] * 2)(lows, highs))
+
+    def late(block, lows, highs):
+        halo, lows, highs = lax.cond(place > 1, edges, known_edges, block, lows, highs)
+        left = send(highs, FORWARD)
+        lows = call(pass_kernel, (strips,), [VMEM, ANY])(lows, left)[0]
+        right = send(lows, BACKWARD)
+        return halo, left, right
+
+    def not_late(block, lows, highs):
+        return idle(halo_shape, strips, strips)
+
+    def neighbours(block, shear, thermal):
+        early_halo, early_pair, lows, highs, main_final, main_last = lax.cond(place <= 1, early, not_early, block, shear, thermal)
+
+        def rest(block, lows, highs):
+            relay = send(lows, RELAY)
+            halo, left, right = lax.cond(place > 0, late, not_late, block, lows, highs)
+            return halo, left, right, relay
+
+        def no_rest(block, lows, highs):
+            return idle(halo_shape, strips, strips, strips)
+
+        halo, left, right, relay = lax.cond(
+            at(lax.axis_index("blk"), lax.axis_index("wn")) < 2 * at(BLK, WN), rest, no_rest, block, lows, highs
+        )
+        return early_halo, halo, early_pair, left, right, relay, main_final, main_last
+
+    def none(block, shear, thermal):
+        return idle(halo_shape, halo_shape, strips, strips, strips, strips, out, out)
+
+    early_halo, halo, early_pair, left, right, relay, main_final, main_last = lax.cond(
+        at(lax.axis_index("blk"), lax.axis_index("wn")) < at(BLK, WN), neighbours, none, block, shear, thermal
+    )
+    final, last = call(
+        last_kernel, (out, out), [VMEM] + [HBM] * 2 + [VMEM] * 7 + [SMEM] * 2 + [HBM] * 2, SCRATCH + [pltpu.SemaphoreType.DMA((3,))]
+    )(
+        block, early_halo, halo, early_pair, left, right, relay, wrap, wrap_up, wrap_down, shear, thermal, main_final, main_last
     )
     return final.reshape(14, 16, 2, LANES), last.reshape(14, 16, 2, LANES)
 

time: 47.8 us -> 40.2 us (0.84)
  the two profiles are of different devices: /device:TPU:25 before, /device:TPU:64 now
where the time goes in v2:
time: 40.2 us; the launch traced here: 39.7 us
  starting transfers between devices  19.9 us (50%)
  Pallas kernels  10.8 us (27%)
  waiting for transfers between devices  8.17 us (20%)
  between operations  0.69 us (2%)
    ppermute x9, starting transfers between devices, send(): return lax.ppermute(x, ('blk', 'wn'), pairs)  19.9 us
    pallas_call x1, Pallas kernels, local(): call(last_kernel, (out, out), [VMEM] + [HBM] * 2 + [VMEM] * 7 + [SMEM] *...  8.21 us
    ppermute x9, waiting for transfers between devices, send(): return lax.ppermute(x, ('blk', 'wn'), pairs)  8.17 us
    pallas_call x1, Pallas kernels, local(): call(load_kernel, (out, f32(4, 8, LANES), f32(2, 8, LANES)), [HBM] * 3, [...  1.12 us
  transfers between devices with their start and end apart: 9, of which 4 were waited for; matrix products, arithmetic and copies ran while one was open for 0% of the time, Pallas kernels for 4%

profile of v2, /device:TPU:64, one launch (start us, length us, event | category | flops | bytes accessed | tf_op | source)
XLA Modules:
  0.0 39.7 jit_solution(10556224111066855709)
XLA Ops:
  0.6 1.1 %shard_map.68 = (f32[14,32,128]{2,1,0:T(8,128)S(1)}, f32[4,8,128]{2,1,0:T(8,128)S(1)}, f32[2,8,128]{2,1,0:T(8,128)S(1)}) custom-call(f32[11,32,128]{2,1,0:T(8,128)} %bitcast.5, f32[2,32,128]{2,1,0:T(8,128)} %bitcast.6, f32[1,32,128]{2,1,0:T(8,128)} %bitcast.7), custom_call_target="tpu_custom_call" | custom-call | flops 1 | bytes 1 | tf_op jit(solution)/shard_map/pallas_call | solution.py:364
  1.8 0.7 %collective-permute-start.8 = (f32[4,8,128]{2,1,0:T(8,128)S(1)}, f32[4,8,128]{2,1,0:T(8,128)S(1)}, u32[]{:S(2)}, u32[]{:S(2)}) collective-permute-start(f32[4,8,128]{2,1,0:T(8,128)S(1)} %get-tuple-element.124), channel_id=1, source_target_pairs={{88,96},{89,97},{90,98},{91,99},{92,100},{93,101},{94,102},{95,103... | collective-permute-start | bytes 49160 | tf_op jit(solution)/shard_map/ppermute | solution.py:317
  2.4 0.7 %collective-permute-start.10 = (f32[2,8,128]{2,1,0:T(8,128)S(1)}, f32[2,8,128]{2,1,0:T(8,128)S(1)}, u32[]{:S(2)}, u32[]{:S(2)}) collective-permute-start(f32[2,8,128]{2,1,0:T(8,128)S(1)} %get-tuple-element.125), channel_id=1, source_target_pairs={{88,97},{89,98},{90,99},{91,100},{92,101},{93,102},{94,103},{184,1... | collective-permute-start | bytes 24584 | tf_op jit(solution)/shard_map/ppermute | solution.py:317
  3.1 0.7 %collective-permute-start.9 = (f32[2,8,128]{2,1,0:T(8,128)S(1)}, f32[2,8,128]{2,1,0:T(8,128)S(1)}, u32[]{:S(2)}, u32[]{:S(2)}) collective-permute-start(f32[2,8,128]{2,1,0:T(8,128)S(1)} %get-tuple-element.125), channel_id=1, source_target_pairs={{89,96},{90,97},{91,98},{92,99},{93,100},{94,101},{95,102},{185,19... | collective-permute-start | bytes 24584 | tf_op jit(solution)/shard_map/ppermute | solution.py:317
  3.8 27.7 %conditional.6 = ((f32[14,16,128]{2,1,0:T(8,128)}, f32[14,16,128]{2,1,0:T(8,128)}, f32[18,128]{1,0:T(8,128)}, f32[18,128]{1,0:T(8,128)}, f32[18,128]{1,0:T(8,128...) conditional(s32[]{:T(128)} %convert_element_type.18, () %tuple.54, (s32[]{:T(128)}, ...), branch_computations={%region_0.1_spmd, %region_1.12_spmd} | conditional | flops 31 | bytes 951132 | solution.py:433
  3.8 16.9 %conditional.3 = ((f32[14,16,128]{2,1,0:T(8,128)}, f32[18,128]{1,0:T(8,128)}, f32[18,128]{1,0:T(8,128)}, f32[18,128]{1,0:T(8,128)S(1)}, f32[14,32,128]{2,1,0:T(8,128)}, /*index=5*/f32[14,32,128]{2,1,0:T(8,128)})) conditional(s32[]{:T(128)} %convert_element_type.15, () %tuple.45, (f32[14,32,128]{2,1,0:T(8,128)S(1)}, s32[]{:T(128)}, ...), branch_computations={%region_2.2_spmd, %region_3.5_spmd} | conditional | flops 6 | bytes 438506 | solution.py:415
  3.9 0.7 %collective-permute-start.1 = (f32[14,8,128]{2,1,0:T(8,128)S(1)}, f32[14,8,128]{2,1,0:T(8,128)S(1)}, u32[]{:S(2)}, u32[]{:S(2)}) collective-permute-start(f32[14,8,128]{2,1,0:T(8,128)S(1)} %branch_1_fun.10), channel_id=1, source_target_pairs={{1,2},{3,4},{5,6},{9,10},{11,12},{13,14},{97,98},{99,100},{101,102... | collective-permute-start | bytes 172040 | tf_op jit(solution)/shard_map/cond/branch_1_fun/cond/branch_1_fun/ppermute | solution.py:317
  4.6 5.9 %collective-permute-start = (f32[84,128]{1,0:T(8,128)S(1)}, f32[84,128]{1,0:T(8,128)S(1)}, u32[]{:S(2)}, u32[]{:S(2)}) collective-permute-start(f32[84,128]{1,0:T(8,128)S(1)} %branch_1_fun.9), channel_id=1, source_target_pairs={{0,1},{2,3},{4,5},{6,7},{8,9},{10,11},{12,13},{14,15},{96,97},{98,... | collective-permute-start | bytes 129032 | tf_op jit(solution)/shard_map/cond/branch_1_fun/cond/branch_1_fun/ppermute | solution.py:317
  10.4 0.9 %collective-permute-done.first = f32[84,128]{1,0:T(8,128)S(1)} collective-permute-done((f32[84,128]{1,0:T(8,128)S(1)}, f32[84,128]{1,0:T(8,128)S(1)}, u32[]{:S(2)}, u32[]{:S(2)}) %collective-permute-start) | collective-permute-done | bytes 43040 | tf_op jit(solution)/shard_map/cond/branch_1_fun/cond/branch_1_fun/ppermute | solution.py:317
  11.3 0.0 collective-permute-done.1.second
  11.3 0.7 %branch_1_fun.11 = (f32[14,16,128]{2,1,0:T(8,128)}, f32[18,128]{1,0:T(8,128)S(1)}, f32[18,128]{1,0:T(8,128)}, f32[18,128]{1,0:T(8,128)S(1)}) custom-call(f32[84,128]{1,0:T(8,128)S(1)} %collective-permute-done.first, f32[14,8,128]{2,1,0:T(8,128)S(1)} %collective-permute-done.1.second, f32[14,32,128]{2,1,0:T(8,128)S(1)} %get-tuple-element.62.block.after), custom_call_target="tpu_custom_call" | custom-call | flops 1 | bytes 1 | tf_op jit(solution)/shard_map/cond/branch_1_fun/cond/branch_1_fun/pallas_call | solution.py:383
  12.0 7.0 %collective-permute-start.2 = (f32[18,128]{1,0:T(8,128)S(1)}, f32[18,128]{1,0:T(8,128)}, u32[]{:S(2)}, u32[]{:S(2)}) collective-permute-start(f32[18,128]{1,0:T(8,128)S(1)} %get-tuple-element.64), channel_id=1, source_target_pairs={{0,8},{1,9},{2,10},{3,11},{4,12},{5,13},{6,14},{7,15},{96,104},{97... | collective-permute-start | bytes 27656 | tf_op jit(solution)/shard_map/cond/branch_1_fun/cond/branch_1_fun/ppermute | solution.py:317
  19.0 1.7 %collective-permute-done.2 = f32[18,128]{1,0:T(8,128)} collective-permute-done((f32[18,128]{1,0:T(8,128)S(1)}, f32[18,128]{1,0:T(8,128)}, u32[]{:S(2)}, u32[]{:S(2)}) %collective-permute-start.2) | collective-permute-done | bytes 9248 | tf_op jit(solution)/shard_map/cond/branch_1_fun/cond/branch_1_fun/ppermute | solution.py:317
  20.8 10.7 %conditional.4 = ((f32[14,16,128]{2,1,0:T(8,128)}, f32[18,128]{1,0:T(8,128)}, f32[18,128]{1,0:T(8,128)}, f32[18,128]{1,0:T(8,128)})) conditional(s32[]{:T(128)} %convert_element_type.16, () %tuple.47, (s32[]{:T(128)}, f32[18,128]{1,0:T(8,128)}, f32[18,128]{1,0:T(8,128)S(1)}, f32[14,32,128]{2,1,0:T(8,128)S(1)}) %tuple.48), branch_computations={%region_6.6_spmd, %region_7.11_spmd} | conditional | flops 8 | bytes 512328 | solution.py:425
  20.8 1.2 %collective-permute-start.7 = (f32[18,128]{1,0:T(8,128)}, f32[18,128]{1,0:T(8,128)}, u32[]{:S(2)}, u32[]{:S(2)}) collective-permute-start(f32[18,128]{1,0:T(8,128)} %get-tuple-element.87), channel_id=1, source_target_pairs={{96,88},{97,89},{98,90},{99,91},{100,92},{101,93},{102,94},{103,95... | collective-permute-start | bytes 27656 | tf_op jit(solution)/shard_map/cond/branch_1_fun/cond/branch_1_fun/ppermute | solution.py:317
  22.0 9.5 %conditional.2 = ((f32[14,16,128]{2,1,0:T(8,128)}, f32[18,128]{1,0:T(8,128)}, f32[18,128]{1,0:T(8,128)})) conditional(s32[]{:T(128)} %convert_element_type.14, () %tuple.43, (s32[]{:T(128)}, f32[18,128]{1,0:T(8,128)}, f32[18,128]{1,0:T(8,128)S(1)}, f32[14,32,128]{2,1,0:T(8,128)S(1)}) %param.10), branch_computations={%region_8.7_spmd, %region_9.10_spmd} | conditional | flops 6 | bytes 475370 | solution.py:419
  22.0 0.7 %conditional.1 = ((f32[14,16,128]{2,1,0:T(8,128)}, f32[18,128]{1,0:T(8,128)S(1)}, f32[18,128]{1,0:T(8,128)S(1)})) conditional(s32[]{:T(128)} %convert_element_type.13, (f32[18,128]{1,0:T(8,128)}, f32[18,128]{1,0:T(8,128)S(1)}) %tuple.41, f32[14,32,128]{2,1,0:T(8,128)S(1)} %get-tuple-element.79), branch_computations={%region_10.8_spmd, %region_11.9_spmd} | conditional | flops 3 | bytes 401499 | solution.py:405
  22.0 0.7 %branch_0_fun.13 = (f32[18,128]{1,0:T(8,128)S(1)}, f32[18,128]{1,0:T(8,128)S(1)}) custom-call(f32[18,128]{1,0:T(8,128)} %get-tuple-element.72.early_lows, f32[18,128]{1,0:T(8,128)S(1)} %get-tuple-element.73.early_highs), custom_call_target="tpu_custom_call" | custom-call | flops 1 | bytes 1 | tf_op jit(solution)/shard_map/cond/branch_1_fun/cond/branch_1_fun/cond/branch_1_fun/cond/branch_0_fun/pallas_call | solution.py:402
  22.7 1.9 %collective-permute-start.5 = (f32[18,128]{1,0:T(8,128)S(1)}, f32[18,128]{1,0:T(8,128)}, u32[]{:S(2)}, u32[]{:S(2)}) collective-permute-start(f32[18,128]{1,0:T(8,128)S(1)} %get-tuple-element.81), channel_id=1, source_target_pairs={{8,16},{9,17},{10,18},{11,19},{12,20},{13,21},{14,22},{15,23},{16,... | collective-permute-start | bytes 27656 | tf_op jit(solution)/shard_map/cond/branch_1_fun/cond/branch_1_fun/cond/branch_1_fun/ppermute | solution.py:317
  24.6 0.8 %collective-permute-done.5.after = f32[18,128]{1,0:T(8,128)} collective-permute-done((f32[18,128]{1,0:T(8,128)S(1)}, f32[18,128]{1,0:T(8,128)}, u32[]{:S(2)}, u32[]{:S(2)}) %collective-permute-start.5) | collective-permute-done | bytes 9248 | tf_op jit(solution)/shard_map/cond/branch_1_fun/cond/branch_1_fun/cond/branch_1_fun/ppermute | solution.py:317
  25.4 1.3 %collective-permute-start.6 = (f32[18,128]{1,0:T(8,128)S(1)}, f32[18,128]{1,0:T(8,128)}, u32[]{:S(2)}, u32[]{:S(2)}) collective-permute-start(f32[18,128]{1,0:T(8,128)S(1)} %branch_1_fun.15), channel_id=1, source_target_pairs={{16,8},{17,9},{18,10},{19,11},{20,12},{21,13},{22,14},{23,15},{24,... | collective-permute-start | bytes 27656 | tf_op jit(solution)/shard_map/cond/branch_1_fun/cond/branch_1_fun/cond/branch_1_fun/ppermute | solution.py:317
  26.7 4.8 %collective-permute-done.6 = f32[18,128]{1,0:T(8,128)} collective-permute-done((f32[18,128]{1,0:T(8,128)S(1)}, f32[18,128]{1,0:T(8,128)}, u32[]{:S(2)}, u32[]{:S(2)}) %collective-permute-start.6) | collective-permute-done | bytes 9248 | tf_op jit(solution)/shard_map/cond/branch_1_fun/cond/branch_1_fun/cond/branch_1_fun/ppermute | solution.py:317
  31.5 0.0 collective-permute-done.7
  31.5 0.0 collective-permute-done.10.wrap_down
  31.5 0.0 collective-permute-done.9.wrap_up
  31.5 0.0 collective-permute-done.8.wrap
  31.5 8.2 %shard_map.69 = (f32[14,32,128]{2,1,0:T(8,128)}, f32[14,32,128]{2,1,0:T(8,128)}) custom-call(f32[14,32,128]{2,1,0:T(8,128)S(1)} %get-tuple-element.117.block, f32[14,16,128]{2,1,0:T(8,128)} %get-tuple-element.118.early_halo, f32[14,16,128]{2,1,0:T(8,128)} %get-tuple-element.119.late_halo, f32[18,128]{1,0:T(8,128)} %get-tuple-element.120.early_pair, ...), custom_call_target="tpu_custom_call" | custom-call | flops 1 | bytes 1 | tf_op jit(solution)/shard_map/pallas_call | solution.py:436
  (6 shorter events, 0.1 us)
Async XLA Ops:
  1.8 29.7 %collective-permute-start.8 = (f32[4,8,128]{2,1,0:T(8,128)S(1)}, f32[4,8,128]{2,1,0:T(8,128)S(1)}, u32[]{:S(2)}, u32[]{:S(2)}) collective-permute-start(f32[4,8,128]{2,1,0:T(8,128)S(1)} %get-tuple-element.124), channel_id=1, source_target_pairs={{88,96},{89,97},{90,98},{91,99},{92,100},{93,101},{94,102},{95,103... | collective-permute-start | bytes 49160 | tf_op jit(solution)/shard_map/ppermute | solution.py:317
  2.4 29.0 %collective-permute-start.10 = (f32[2,8,128]{2,1,0:T(8,128)S(1)}, f32[2,8,128]{2,1,0:T(8,128)S(1)}, u32[]{:S(2)}, u32[]{:S(2)}) collective-permute-start(f32[2,8,128]{2,1,0:T(8,128)S(1)} %get-tuple-element.125), channel_id=1, source_target_pairs={{88,97},{89,98},{90,99},{91,100},{92,101},{93,102},{94,103},{184,1... | collective-permute-start | bytes 24584 | tf_op jit(solution)/shard_map/ppermute | solution.py:317
  3.1 28.4 %collective-permute-start.9 = (f32[2,8,128]{2,1,0:T(8,128)S(1)}, f32[2,8,128]{2,1,0:T(8,128)S(1)}, u32[]{:S(2)}, u32[]{:S(2)}) collective-permute-start(f32[2,8,128]{2,1,0:T(8,128)S(1)} %get-tuple-element.125), channel_id=1, source_target_pairs={{89,96},{90,97},{91,98},{92,99},{93,100},{94,101},{95,102},{185,19... | collective-permute-start | bytes 24584 | tf_op jit(solution)/shard_map/ppermute | solution.py:317
  3.9 7.4 %collective-permute-start.1 = (f32[14,8,128]{2,1,0:T(8,128)S(1)}, f32[14,8,128]{2,1,0:T(8,128)S(1)}, u32[]{:S(2)}, u32[]{:S(2)}) collective-permute-start(f32[14,8,128]{2,1,0:T(8,128)S(1)} %branch_1_fun.10), channel_id=1, source_target_pairs={{1,2},{3,4},{5,6},{9,10},{11,12},{13,14},{97,98},{99,100},{101,102... | collective-permute-start | bytes 172040 | tf_op jit(solution)/shard_map/cond/branch_1_fun/cond/branch_1_fun/ppermute | solution.py:317
  4.6 6.7 %collective-permute-start = (f32[84,128]{1,0:T(8,128)S(1)}, f32[84,128]{1,0:T(8,128)S(1)}, u32[]{:S(2)}, u32[]{:S(2)}) collective-permute-start(f32[84,128]{1,0:T(8,128)S(1)} %branch_1_fun.9), channel_id=1, source_target_pairs={{0,1},{2,3},{4,5},{6,7},{8,9},{10,11},{12,13},{14,15},{96,97},{98,... | collective-permute-start | bytes 129032 | tf_op jit(solution)/shard_map/cond/branch_1_fun/cond/branch_1_fun/ppermute | solution.py:317
  12.0 8.7 %collective-permute-start.2 = (f32[18,128]{1,0:T(8,128)S(1)}, f32[18,128]{1,0:T(8,128)}, u32[]{:S(2)}, u32[]{:S(2)}) collective-permute-start(f32[18,128]{1,0:T(8,128)S(1)} %get-tuple-element.64), channel_id=1, source_target_pairs={{0,8},{1,9},{2,10},{3,11},{4,12},{5,13},{6,14},{7,15},{96,104},{97... | collective-permute-start | bytes 27656 | tf_op jit(solution)/shard_map/cond/branch_1_fun/cond/branch_1_fun/ppermute | solution.py:317
  20.8 10.7 %collective-permute-start.7 = (f32[18,128]{1,0:T(8,128)}, f32[18,128]{1,0:T(8,128)}, u32[]{:S(2)}, u32[]{:S(2)}) collective-permute-start(f32[18,128]{1,0:T(8,128)} %get-tuple-element.87), channel_id=1, source_target_pairs={{96,88},{97,89},{98,90},{99,91},{100,92},{101,93},{102,94},{103,95... | collective-permute-start | bytes 27656 | tf_op jit(solution)/shard_map/cond/branch_1_fun/cond/branch_1_fun/ppermute | solution.py:317
  22.7 2.7 %collective-permute-start.5 = (f32[18,128]{1,0:T(8,128)S(1)}, f32[18,128]{1,0:T(8,128)}, u32[]{:S(2)}, u32[]{:S(2)}) collective-permute-start(f32[18,128]{1,0:T(8,128)S(1)} %get-tuple-element.81), channel_id=1, source_target_pairs={{8,16},{9,17},{10,18},{11,19},{12,20},{13,21},{14,22},{15,23},{16,... | collective-permute-start | bytes 27656 | tf_op jit(solution)/shard_map/cond/branch_1_fun/cond/branch_1_fun/cond/branch_1_fun/ppermute | solution.py:317
  25.4 6.1 %collective-permute-start.6 = (f32[18,128]{1,0:T(8,128)S(1)}, f32[18,128]{1,0:T(8,128)}, u32[]{:S(2)}, u32[]{:S(2)}) collective-permute-start(f32[18,128]{1,0:T(8,128)S(1)} %branch_1_fun.15), channel_id=1, source_target_pairs={{16,8},{17,9},{18,10},{19,11},{20,12},{21,13},{22,14},{23,15},{24,... | collective-permute-start | bytes 27656 | tf_op jit(solution)/shard_map/cond/branch_1_fun/cond/branch_1_fun/cond/branch_1_fun/ppermute | solution.py:317

commit v3 on v2

--- a/solution.py
+++ b/solution.py
@@ -117,8 +117,8 @@
         right[t] = rights[t]
     low, high = block[:, 0:8], block[:, 24:32]
     _, rights = pack_columns(jnp.concatenate([low, high], axis=1).reshape(14 * 16, LANES))
-    for t in range(2):
-        corner[t] = rights[t]
+    for t in range(3):
+        corner[t] = rights[t % 2]
 
 
 def second_rows_kernel(block, second):
@@ -203,39 +203,37 @@
     pass
 
 
+def late_main_kernel(block, early_halo, late_halo, shear, thermal, halo, final, last, w0, wa, wb, coeff, sem):
+    place = lax.axis_index("blk") % RUN
+    for known, source in ((place <= 1, early_halo), (place > 1, late_halo)):
+
+        @pl.when(known)
+        def _():
+            copy = pltpu.make_async_copy(source, halo, sem)
+            copy.start()
+            copy.wait()
+
+    @pl.when(place != 0)
+    def _():
+        main_sections(block, halo, shear, thermal, final, last, w0, wa, wb, coeff)
+
+
 def last_kernel(
-    block, early_halo, late_halo, early_pair, left, right, relay, wrap, wrap_up, wrap_down, shear, thermal, main_final, main_last,
-    final, last, w0, wa, wb, coeff, sems,
+    block, halo, early_pair, left, right, relay, wrap, wrap_up, wrap_down, shear, thermal,
+    early_final, early_last, late_final, late_last, final, last, w0, wa, wb, coeff, finals, lasts, in_sems, out_sems,
 ):
     wn = lax.axis_index("wn")
     blk = lax.axis_index("blk")
     place = blk % RUN
-
-    halo_rows = w0.at[:, pl.ds(OWN, 16)]
-    mains = [pltpu.make_async_copy(a, b, sems.at[i]) for i, (a, b) in enumerate(((main_final, final), (main_last, last)))]
+    mains = [pltpu.make_async_copy(a, b, in_sems.at[i]) for i, (a, b) in enumerate(((early_final, finals), (early_last, lasts)))]
 
     @pl.when(place == 0)
     def _():
         for copy in mains:
             copy.start()
 
-    for known, halo in ((place <= 1, early_halo), (place > 1, late_halo)):
-
-        @pl.when(known)
-        def _():
-            copy = pltpu.make_async_copy(halo, halo_rows, sems.at[2])
-            copy.start()
-            for v in range(14):
-                w0[v, 0:OWN] = block[v]
-            copy.wait()
-
-    @pl.when(place != 0)
-    def _():
-        main_sections(block, None, shear, thermal, final, last, w0, wa, wb, coeff)
-
     lane = iota((ROWS, LANES), 1)
-    for v in range(14):
-        w0[v, 0:OWN] = block[v]
+    gather_rows(block, halo, w0)
     lane3 = iota((3, LANES), 1)
     tiles = []
     for t in range(6):
@@ -275,6 +273,7 @@
                 ref[v] = jnp.where(lane == 0, swapped, w)
 
     lane_own = iota((OWN, LANES), 1)
+    copies = []
 
     def emit(v, f, r):
         if v == 0:
@@ -284,10 +283,16 @@
                 for copy in mains:
                     copy.wait()
 
-        for out, new in ((final, f), (last, r)):
-            out[v] = jnp.where(lane_own < 3, pltpu.roll(new, LANES - 16, 1), jnp.where(lane_own >= 125, new, out[v]))
+        for i, (out, staged, late, new) in enumerate(((final, finals, late_final, f), (last, lasts, late_last, r))):
+            old = jnp.where(place == 0, staged[v], late[v])
+            staged[v] = jnp.where(lane_own < 3, pltpu.roll(new, LANES - 16, 1), jnp.where(lane_own >= 125, new, old))
+            copy = pltpu.make_async_copy(staged.at[v], out.at[v], out_sems.at[i, v])
+            copy.start()
+            copies.append(copy)
 
     sections(fix, w0, wa, wb, coeff, shear, thermal, emit)
+    for copy in copies:
+        copy.wait()
 
 
 VMEM = pl.BlockSpec(memory_space=pltpu.VMEM)
@@ -363,13 +368,13 @@
     shear, thermal = in_hbm(shear), in_hbm(thermal)
     block, right, corner = call(
         load_kernel,
-        (out, f32(4, 8, LANES), f32(2, 8, LANES)),
+        (out, f32(4, 8, LANES), f32(3, 8, LANES)),
         [HBM] * 3,
         [pltpu.SemaphoreType.DMA((3,))],
     )(in_hbm(species.reshape(11, OWN, LANES)), in_hbm(flow.reshape(2, OWN, LANES)), in_hbm(heat.reshape(1, OWN, LANES)))
+    wrap_down = send(corner, wrap_pairs(1))
+    wrap = send(right, wrap_pairs(0))
     wrap_up = send(corner, wrap_pairs(-1))
-    wrap = send(right, wrap_pairs(0))
-    wrap_down = send(corner, wrap_pairs(1))
 
     def exchange_rows(block, early):
         second = call(second_rows_kernel, (rows,), [VMEM])(block)[0]
@@ -402,11 +407,7 @@
         return (*idle(halo_shape), *call(keep_kernel, (strips, strips), [VMEM] * 2)(lows, highs))
 
     def late(block, lows, highs):
-        halo, lows, highs = lax.cond(place > 1, edges, known_edges, block, lows, highs)
-        left = send(highs, FORWARD)
-        lows = call(pass_kernel, (strips,), [VMEM, ANY])(lows, left)[0]
-        right = send(lows, BACKWARD)
-        return halo, left, right
+        return lax.cond(place > 1, edges, known_edges, block, lows, highs)
 
     def not_late(block, lows, highs):
         return idle(halo_shape, strips, strips)
@@ -416,27 +417,40 @@
 
         def rest(block, lows, highs):
             relay = send(lows, RELAY)
-            halo, left, right = lax.cond(place > 0, late, not_late, block, lows, highs)
-            return halo, left, right, relay
+            return (*lax.cond(place > 0, late, not_late, block, lows, highs), relay)
 
         def no_rest(block, lows, highs):
             return idle(halo_shape, strips, strips, strips)
 
-        halo, left, right, relay = lax.cond(
+        halo, lows, highs, relay = lax.cond(
             at(lax.axis_index("blk"), lax.axis_index("wn")) < 2 * at(BLK, WN), rest, no_rest, block, lows, highs
         )
-        return early_halo, halo, early_pair, left, right, relay, main_final, main_last
+        return early_halo, halo, early_pair, lows, highs, relay, main_final, main_last
 
     def none(block, shear, thermal):
         return idle(halo_shape, halo_shape, strips, strips, strips, strips, out, out)
 
-    early_halo, halo, early_pair, left, right, relay, main_final, main_last = lax.cond(
+    early_halo, halo, early_pair, lows, highs, relay, early_final, early_last = lax.cond(
         at(lax.axis_index("blk"), lax.axis_index("wn")) < at(BLK, WN), neighbours, none, block, shear, thermal
     )
-    final, last = call(
-        last_kernel, (out, out), [VMEM] + [HBM] * 2 + [VMEM] * 7 + [SMEM] * 2 + [HBM] * 2, SCRATCH + [pltpu.SemaphoreType.DMA((3,))]
+    left = send(highs, FORWARD)
+    right = send(lows, BACKWARD)
+    halo, late_final, late_last = call(
+        late_main_kernel, (halo_shape, out, out), [VMEM] + [HBM] * 2 + [SMEM] * 2, SCRATCH + [pltpu.SemaphoreType.DMA]
+    )(block, early_halo, halo, shear, thermal)
+    final, last = pl.pallas_call(
+        last_kernel,
+        out_shape=(out, out),
+        in_specs=[VMEM] * 9 + [SMEM] * 2 + [HBM] * 2 + [VMEM] * 2,
+        out_specs=(HBM, HBM),
+        scratch_shapes=SCRATCH
+        + [pltpu.VMEM((14, OWN, LANES), jnp.float32)] * 2
+        + [pltpu.SemaphoreType.DMA((2,)), pltpu.SemaphoreType.DMA((2, 14))],
+        compiler_params=PARAMS,
+        cost_estimate=pl.CostEstimate(flops=1, bytes_accessed=1, transcendentals=0),
     )(
-        block, early_halo, halo, early_pair, left, right, relay, wrap, wrap_up, wrap_down, shear, thermal, main_final, main_last
+        block, halo, early_pair, left, right, relay, wrap, wrap_up, wrap_down, shear, thermal,
+        early_final, early_last, late_final, late_last,
     )
     return final.reshape(14, 16, 2, LANES), last.reshape(14, 16, 2, LANES)
 

time: 40.2 us -> 36.1 us (0.90)
  the two profiles are of different devices: /device:TPU:64 before, /device:TPU:128 now
where the time goes in v3:
time: 36.1 us; the launch traced here: 35.6 us
  starting transfers between devices  22.6 us (63%)
  Pallas kernels  11.2 us (31%)
  waiting for transfers between devices  0.87 us (2%)
  between operations  0.74 us (2%)
    ppermute x8, starting transfers between devices, send(): return lax.ppermute(x, ('blk', 'wn'), pairs)  22.6 us
    pallas_call x1, Pallas kernels, local(): pl.pallas_call(last_kernel, out_shape=(out, out), in_specs=[VMEM] * 9 + [...  4.88 us
    pallas_call x1, Pallas kernels, local(): call(late_main_kernel, (halo_shape, out, out), [VMEM] + [HBM] * 2 + [SMEM...  4.45 us
    pallas_call x1, Pallas kernels, local(): call(load_kernel, (out, f32(4, 8, LANES), f32(3, 8, LANES)), [HBM] * 3, [...  1.12 us
    ppermute x8, waiting for transfers between devices, send(): return lax.ppermute(x, ('blk', 'wn'), pairs)  0.87 us
    pallas_call x1, Pallas kernels, edges(): call(late_columns_kernel, (halo_shape, strips, strips), [VMEM] * 3)  0.76 us
  transfers between devices with their start and end apart: 8, of which 1 were waited for; matrix products, arithmetic and copies ran while one was open for 0% of the time, Pallas kernels for 15%

profile of v3, /device:TPU:128, one launch (start us, length us, event | category | flops | bytes accessed | tf_op | source)
XLA Modules:
  0.0 35.6 jit_solution(10113913761009167300)
XLA Ops:
  0.6 1.1 %shard_map.68 = (f32[14,32,128]{2,1,0:T(8,128)S(1)}, f32[4,8,128]{2,1,0:T(8,128)S(1)}, f32[3,8,128]{2,1,0:T(8,128)S(1)}) custom-call(f32[11,32,128]{2,1,0:T(8,128)} %bitcast.5, f32[2,32,128]{2,1,0:T(8,128)} %bitcast.6, f32[1,32,128]{2,1,0:T(8,128)} %bitcast.7), custom_call_target="tpu_custom_call" | custom-call | flops 1 | bytes 1 | tf_op jit(solution)/shard_map/pallas_call | solution.py:369
  1.8 0.7 %collective-permute-start.8 = (f32[4,8,128]{2,1,0:T(8,128)S(1)}, f32[4,8,128]{2,1,0:T(8,128)S(1)}, u32[]{:S(2)}, u32[]{:S(2)}) collective-permute-start(f32[4,8,128]{2,1,0:T(8,128)S(1)} %get-tuple-element.125), channel_id=1, source_target_pairs={{88,96},{89,97},{90,98},{91,99},{92,100},{93,101},{94,102},{95,103... | collective-permute-start | bytes 49160 | tf_op jit(solution)/shard_map/ppermute | solution.py:322
  2.4 0.7 %collective-permute-start.10 = (f32[3,8,128]{2,1,0:T(8,128)S(1)}, f32[3,8,128]{2,1,0:T(8,128)S(1)}, u32[]{:S(2)}, u32[]{:S(2)}) collective-permute-start(f32[3,8,128]{2,1,0:T(8,128)S(1)} %get-tuple-element.126), channel_id=1, source_target_pairs={{88,97},{89,98},{90,99},{91,100},{92,101},{93,102},{94,103},{184,1... | collective-permute-start | bytes 36872 | tf_op jit(solution)/shard_map/ppermute | solution.py:322
  3.1 0.7 %collective-permute-start.9 = (f32[3,8,128]{2,1,0:T(8,128)S(1)}, f32[3,8,128]{2,1,0:T(8,128)S(1)}, u32[]{:S(2)}, u32[]{:S(2)}) collective-permute-start(f32[3,8,128]{2,1,0:T(8,128)S(1)} %get-tuple-element.126), channel_id=1, source_target_pairs={{89,96},{90,97},{91,98},{92,99},{93,100},{94,101},{95,102},{185,19... | collective-permute-start | bytes 36872 | tf_op jit(solution)/shard_map/ppermute | solution.py:322
  3.8 11.4 %conditional.6 = ((f32[14,16,128]{2,1,0:T(8,128)}, f32[14,16,128]{2,1,0:T(8,128)}, f32[18,128]{1,0:T(8,128)}, f32[18,128]{1,0:T(8,128)}, f32[18,128]{1,0:T(8,128...) conditional(s32[]{:T(128)} %convert_element_type.18, () %tuple.53, (s32[]{:T(128)}, ...), branch_computations={%region_0.1_spmd, %region_1.12_spmd} | conditional | flops 30 | bytes 877291 | solution.py:433
  3.9 11.3 %conditional.4 = ((f32[14,16,128]{2,1,0:T(8,128)}, f32[18,128]{1,0:T(8,128)}, f32[18,128]{1,0:T(8,128)}, f32[18,128]{1,0:T(8,128)})) conditional(s32[]{:T(128)} %convert_element_type.16, () %tuple.46, (s32[]{:T(128)}, f32[18,128]{1,0:T(8,128)}, f32[18,128]{1,0:T(8,128)S(1)}, f32[14,32,128]{2,1,0:T(8,128)S(1)}) %tuple.47), branch_computations={%region_6.6_spmd, %region_7.11_spmd} | conditional | flops 7 | bytes 438487 | solution.py:425
  3.9 1.3 %collective-permute-start.5 = (f32[18,128]{1,0:T(8,128)}, f32[18,128]{1,0:T(8,128)}, u32[]{:S(2)}, u32[]{:S(2)}) collective-permute-start(f32[18,128]{1,0:T(8,128)} %get-tuple-element.84), channel_id=1, source_target_pairs={{96,88},{97,89},{98,90},{99,91},{100,92},{101,93},{102,94},{103,95... | collective-permute-start | bytes 27656 | tf_op jit(solution)/shard_map/cond/branch_1_fun/cond/branch_1_fun/ppermute | solution.py:322
  5.2 10.0 %conditional.2 = ((f32[14,16,128]{2,1,0:T(8,128)}, f32[18,128]{1,0:T(8,128)}, f32[18,128]{1,0:T(8,128)})) conditional(s32[]{:T(128)} %convert_element_type.14, () %tuple.42, (s32[]{:T(128)}, f32[18,128]{1,0:T(8,128)}, f32[18,128]{1,0:T(8,128)S(1)}, f32[14,32,128]{2,1,0:T(8,128)S(1)}) %param.10), branch_computations={%region_8.7_spmd, %region_9.10_spmd} | conditional | flops 5 | bytes 401529 | solution.py:420
  5.2 10.0 %conditional.1 = ((f32[14,16,128]{2,1,0:T(8,128)}, f32[18,128]{1,0:T(8,128)}, f32[18,128]{1,0:T(8,128)})) conditional(s32[]{:T(128)} %convert_element_type.13, (f32[18,128]{1,0:T(8,128)}, f32[18,128]{1,0:T(8,128)S(1)}) %tuple.41, f32[14,32,128]{2,1,0:T(8,128)S(1)} %get-tuple-element.79), branch_computations={%region_10.8_spmd, %region_11.9_spmd} | conditional | flops 3 | bytes 401499 | solution.py:410
  5.2 0.7 %collective-permute-start.3 = (f32[14,8,128]{2,1,0:T(8,128)S(1)}, f32[14,8,128]{2,1,0:T(8,128)S(1)}, u32[]{:S(2)}, u32[]{:S(2)}) collective-permute-start(f32[14,8,128]{2,1,0:T(8,128)S(1)} %branch_1_fun.11), channel_id=1, source_target_pairs={{17,18},{19,20},{21,22},{25,26},{27,28},{29,30},{33,34},{35,36},{3... | collective-permute-start | bytes 172040 | tf_op jit(solution)/shard_map/cond/branch_1_fun/cond/branch_1_fun/cond/branch_1_fun/cond/branch_1_fun/ppermute | solution.py:322
  5.8 0.0 collective-permute-done.3.after.second
  5.9 7.7 %collective-permute-start.4 = (f32[84,128]{1,0:T(8,128)S(1)}, f32[84,128]{1,0:T(8,128)S(1)}, u32[]{:S(2)}, u32[]{:S(2)}) collective-permute-start(f32[84,128]{1,0:T(8,128)S(1)} %branch_1_fun.12), channel_id=1, source_target_pairs={{16,17},{18,19},{20,21},{22,23},{24,25},{26,27},{28,29},{30,31},{3... | collective-permute-start | bytes 129032 | tf_op jit(solution)/shard_map/cond/branch_1_fun/cond/branch_1_fun/cond/branch_1_fun/cond/branch_1_fun/ppermute | solution.py:322
  13.6 0.9 %collective-permute-done.4.first = f32[84,128]{1,0:T(8,128)S(1)} collective-permute-done((f32[84,128]{1,0:T(8,128)S(1)}, f32[84,128]{1,0:T(8,128)S(1)}, u32[]{:S(2)}, u32[]{:S(2)}) %collective-permute-start.4) | collective-permute-done | bytes 43040 | tf_op jit(solution)/shard_map/cond/branch_1_fun/cond/branch_1_fun/cond/branch_1_fun/cond/branch_1_fun/ppermute | solution.py:322
  14.4 0.8 %branch_1_fun.13 = (f32[14,16,128]{2,1,0:T(8,128)}, f32[18,128]{1,0:T(8,128)}, f32[18,128]{1,0:T(8,128)}) custom-call(f32[84,128]{1,0:T(8,128)S(1)} %collective-permute-done.4.first, f32[14,8,128]{2,1,0:T(8,128)S(1)} %collective-permute-done.3.after.second, f32[14,32,128]{2,1,0:T(8,128)S(1)} %block.2), custom_call_target="tpu_custom_call" | custom-call | flops 1 | bytes 1 | tf_op jit(solution)/shard_map/cond/branch_1_fun/cond/branch_1_fun/cond/branch_1_fun/cond/branch_1_fun/pallas_call | solution.py:404
  15.2 0.0 collective-permute-done.5
  15.2 4.3 %collective-permute-start.6 = (f32[18,128]{1,0:T(8,128)}, f32[18,128]{1,0:T(8,128)S(1)}, u32[]{:S(2)}, u32[]{:S(2)}) collective-permute-start(f32[18,128]{1,0:T(8,128)} %get-tuple-element.122), channel_id=1, source_target_pairs={{8,16},{9,17},{10,18},{11,19},{12,20},{13,21},{14,22},{15,23},{16,... | collective-permute-start | bytes 27656 | tf_op jit(solution)/shard_map/ppermute | solution.py:322
  19.5 6.7 %collective-permute-start.7 = (f32[18,128]{1,0:T(8,128)}, f32[18,128]{1,0:T(8,128)S(1)}, u32[]{:S(2)}, u32[]{:S(2)}) collective-permute-start(f32[18,128]{1,0:T(8,128)} %get-tuple-element.123), channel_id=1, source_target_pairs={{16,8},{17,9},{18,10},{19,11},{20,12},{21,13},{22,14},{23,15},{24,... | collective-permute-start | bytes 27656 | tf_op jit(solution)/shard_map/ppermute | solution.py:322
  26.2 4.5 %shard_map.69 = (f32[14,16,128]{2,1,0:T(8,128)S(1)}, f32[14,32,128]{2,1,0:T(8,128)S(1)}, f32[14,32,128]{2,1,0:T(8,128)S(1)}) custom-call(f32[14,32,128]{2,1,0:T(8,128)S(1)} %get-tuple-element.117.block, f32[14,16,128]{2,1,0:T(8,128)} %get-tuple-element.118.early_halo, f32[14,16,128]{2,1,0:T(8,128)} %get-tuple-element.119.late_halo, f32[11,11]{1,0:T(8,128)} %shear.3, ...), custom_call_target="tpu_custom_call" | custom-call | flops 1 | bytes 1 | tf_op jit(solution)/shard_map/pallas_call | solution.py:438
  30.7 0.0 collective-permute-done.6.left
  30.7 0.0 collective-permute-done.7.right
  30.7 0.0 collective-permute-done.10.wrap_down
  30.7 0.0 collective-permute-done.9.wrap_up
  30.7 0.0 collective-permute-done.8.wrap
  30.7 4.9 %shard_map.70 = (f32[14,32,128]{2,1,0:T(8,128)}, f32[14,32,128]{2,1,0:T(8,128)}) custom-call(f32[14,32,128]{2,1,0:T(8,128)S(1)} %get-tuple-element.117.block, f32[14,16,128]{2,1,0:T(8,128)S(1)} %get-tuple-element.120.halo, f32[18,128]{1,0:T(8,128)} %get-tuple-element.121.early_pair, f32[18,128]{1,0:T(8,128)S(1)} %collective-permute-done.6.left, ...), custom_call_target="tpu_custom_call" | custom-call | flops 1 | bytes 1 | tf_op jit(solution)/shard_map/pallas_call | solution.py:441
  (4 shorter events, 0.1 us)
Async XLA Ops:
  1.8 29.0 %collective-permute-start.8 = (f32[4,8,128]{2,1,0:T(8,128)S(1)}, f32[4,8,128]{2,1,0:T(8,128)S(1)}, u32[]{:S(2)}, u32[]{:S(2)}) collective-permute-start(f32[4,8,128]{2,1,0:T(8,128)S(1)} %get-tuple-element.125), channel_id=1, source_target_pairs={{88,96},{89,97},{90,98},{91,99},{92,100},{93,101},{94,102},{95,103... | collective-permute-start | bytes 49160 | tf_op jit(solution)/shard_map/ppermute | solution.py:322
  2.4 28.3 %collective-permute-start.10 = (f32[3,8,128]{2,1,0:T(8,128)S(1)}, f32[3,8,128]{2,1,0:T(8,128)S(1)}, u32[]{:S(2)}, u32[]{:S(2)}) collective-permute-start(f32[3,8,128]{2,1,0:T(8,128)S(1)} %get-tuple-element.126), channel_id=1, source_target_pairs={{88,97},{89,98},{90,99},{91,100},{92,101},{93,102},{94,103},{184,1... | collective-permute-start | bytes 36872 | tf_op jit(solution)/shard_map/ppermute | solution.py:322
  3.1 27.6 %collective-permute-start.9 = (f32[3,8,128]{2,1,0:T(8,128)S(1)}, f32[3,8,128]{2,1,0:T(8,128)S(1)}, u32[]{:S(2)}, u32[]{:S(2)}) collective-permute-start(f32[3,8,128]{2,1,0:T(8,128)S(1)} %get-tuple-element.126), channel_id=1, source_target_pairs={{89,96},{90,97},{91,98},{92,99},{93,100},{94,101},{95,102},{185,19... | collective-permute-start | bytes 36872 | tf_op jit(solution)/shard_map/ppermute | solution.py:322
  3.9 11.3 %collective-permute-start.5 = (f32[18,128]{1,0:T(8,128)}, f32[18,128]{1,0:T(8,128)}, u32[]{:S(2)}, u32[]{:S(2)}) collective-permute-start(f32[18,128]{1,0:T(8,128)} %get-tuple-element.84), channel_id=1, source_target_pairs={{96,88},{97,89},{98,90},{99,91},{100,92},{101,93},{102,94},{103,95... | collective-permute-start | bytes 27656 | tf_op jit(solution)/shard_map/cond/branch_1_fun/cond/branch_1_fun/ppermute | solution.py:322
  5.2 0.7 %collective-permute-start.3 = (f32[14,8,128]{2,1,0:T(8,128)S(1)}, f32[14,8,128]{2,1,0:T(8,128)S(1)}, u32[]{:S(2)}, u32[]{:S(2)}) collective-permute-start(f32[14,8,128]{2,1,0:T(8,128)S(1)} %branch_1_fun.11), channel_id=1, source_target_pairs={{17,18},{19,20},{21,22},{25,26},{27,28},{29,30},{33,34},{35,36},{3... | collective-permute-start | bytes 172040 | tf_op jit(solution)/shard_map/cond/branch_1_fun/cond/branch_1_fun/cond/branch_1_fun/cond/branch_1_fun/ppermute | solution.py:322
  5.9 8.5 %collective-permute-start.4 = (f32[84,128]{1,0:T(8,128)S(1)}, f32[84,128]{1,0:T(8,128)S(1)}, u32[]{:S(2)}, u32[]{:S(2)}) collective-permute-start(f32[84,128]{1,0:T(8,128)S(1)} %branch_1_fun.12), channel_id=1, source_target_pairs={{16,17},{18,19},{20,21},{22,23},{24,25},{26,27},{28,29},{30,31},{3... | collective-permute-start | bytes 129032 | tf_op jit(solution)/shard_map/cond/branch_1_fun/cond/branch_1_fun/cond/branch_1_fun/cond/branch_1_fun/ppermute | solution.py:322
  15.2 15.5 %collective-permute-start.6 = (f32[18,128]{1,0:T(8,128)}, f32[18,128]{1,0:T(8,128)S(1)}, u32[]{:S(2)}, u32[]{:S(2)}) collective-permute-start(f32[18,128]{1,0:T(8,128)} %get-tuple-element.122), channel_id=1, source_target_pairs={{8,16},{9,17},{10,18},{11,19},{12,20},{13,21},{14,22},{15,23},{16,... | collective-permute-start | bytes 27656 | tf_op jit(solution)/shard_map/ppermute | solution.py:322
  19.5 11.2 %collective-permute-start.7 = (f32[18,128]{1,0:T(8,128)}, f32[18,128]{1,0:T(8,128)S(1)}, u32[]{:S(2)}, u32[]{:S(2)}) collective-permute-start(f32[18,128]{1,0:T(8,128)} %get-tuple-element.123), channel_id=1, source_target_pairs={{16,8},{17,9},{18,10},{19,11},{20,12},{21,13},{22,14},{23,15},{24,... | collective-permute-start | bytes 27656 | tf_op jit(solution)/shard_map/ppermute | solution.py:322

commit v4 on v3

--- a/solution.py
+++ b/solution.py
@@ -34,18 +34,20 @@
         state[v, 40:48] = jnp.where(low & (sub >= 6), cut, below)
 
 
-def coefficients(state, coeff, shear, thermal):
+def coefficients(state, coeff, table):
     for c in range(ROWS // CHUNK):
         rows = pl.ds(c * CHUNK, CHUNK)
         x = [state[r, rows] for r in range(11)]
         logs = jnp.log(state[13, rows])
         visc = cond = None
         for s in range(11):
-            dv = shear[s, 0] * x[0]
-            dc = thermal[s, 0] * x[0]
+            k = 11 * s
+            dv = table[k : k + 1] * x[0]
+            dc = table[k + 121 : k + 122] * x[0]
             for r in range(1, 11):
-                dv = dv + shear[s, r] * x[r]
-                dc = dc + thermal[s, r] * x[r]
+                k = 11 * s + r
+                dv = dv + table[k : k + 1] * x[r]
+                dc = dc + table[k + 121 : k + 122] * x[r]
             tv = x[s] * np.float32(MASSES[s] / 28.0) / dv
             tc = x[s] / dc
             visc = tv if visc is None else visc + tv
@@ -68,21 +70,21 @@
     return (f - pltpu.roll(f, 2, 0)) + (g - pltpu.roll(g, 1, 1))
 
 
-def sections(fix, w0, wa, wb, coeff, shear, thermal, emit):
+def sections(fix, w0, wa, wb, coeff, table, emit):
     fix(w0)
-    coefficients(w0, coeff, shear, thermal)
+    coefficients(w0, coeff, table)
     face = faces(coeff)
     for v in range(14):
         w = w0[v]
         wa[v] = w + STEP * residual(w, face[v in (11, 12)])
     fix(wa)
-    coefficients(wa, coeff, shear, thermal)
+    coefficients(wa, coeff, table)
     face = faces(coeff)
     for v in range(14):
         w = wa[v]
         wb[v] = 0.75 * w0[v] + 0.25 * (w + STEP * residual(w, face[v in (11, 12)]))
     fix(wb)
-    coefficients(wb, coeff, shear, thermal)
+    coefficients(wb, coeff, table)
     face = faces(coeff)
     for v in range(14):
         w = wb[v]
@@ -103,13 +105,21 @@
     return left, right
 
 
-def load_kernel(species, flow, heat, block, right, corner, sems):
+def load_kernel(species, flow, heat, shear, thermal, block, right, corner, corner_again, table, matrices, sems):
     copies = [
         pltpu.make_async_copy(source, block.at[pl.ds(low, count)], sems.at[i])
         for i, (source, low, count) in enumerate(((species, 0, 11), (flow, 11, 2), (heat, 13, 1)))
     ]
-    for copy in copies:
+    small = [pltpu.make_async_copy(source, matrices.at[i], sems.at[3 + i]) for i, source in enumerate((shear, thermal))]
+    for copy in copies + small:
         copy.start()
+    for copy in small:
+        copy.wait()
+    for i in range(2):
+        for s in range(11):
+            for r in range(11):
+                k = 121 * i + 11 * s + r
+                table[k : k + 1] = jnp.full((1, LANES), matrices[i, s, r], jnp.float32)
     for copy in copies:
         copy.wait()
     _, rights = pack_columns(block[...].reshape(14 * OWN, LANES))
@@ -117,23 +127,21 @@
         right[t] = rights[t]
     low, high = block[:, 0:8], block[:, 24:32]
     _, rights = pack_columns(jnp.concatenate([low, high], axis=1).reshape(14 * 16, LANES))
+    for t in range(4):
+        corner[t] = rights[t % 2]
     for t in range(3):
-        corner[t] = rights[t % 2]
-
-
-def second_rows_kernel(block, second):
+        corner_again[t] = rights[t % 2]
+
+
+def rows_kernel(block, second, first):
     even = lax.axis_index("wn") % 2 == 0
     second[...] = jnp.where(even, block[:, 0:8], block[:, 24:32])
-
-
-def first_rows_kernel(block, after, first):
-    even = lax.axis_index("wn") % 2 == 0
     for v in range(14):
         first[pl.ds(6 * v, 6)] = jnp.where(even, block[v, 26:32], block[v, 0:6])
 
 
-def pass_kernel(value, after, out):
-    out[...] = value[...]
+def join_kernel(value, a, b, c, out):
+    pass
 
 
 def halo_of(first, second):
@@ -152,7 +160,7 @@
     return lefts + lefts_halo, rights + rights_halo
 
 
-def early_columns_kernel(first, second, block, halo, pair, lows, highs):
+def early_columns_kernel(first, second, block, halo, pair, lows, highs, offer):
     even = lax.axis_index("blk") % 2 == 0
     halo[...] = halo_of(first, second)
     lefts, rights = columns_of(block, halo[...])
@@ -160,7 +168,9 @@
         three = pl.ds(3 * t, 3)
         pair[three] = jnp.where(even, rights[t][5:8], lefts[t][0:3])
         lows[three] = lefts[t][0:3]
+        offer[three] = lefts[t][0:3]
         highs[three] = rights[t][5:8]
+    offer[18:20] = jnp.zeros((2, LANES), jnp.float32)
 
 
 def late_columns_kernel(first, second, block, halo, lows, highs):
@@ -183,7 +193,7 @@
         w0[v, OWN:ROWS] = halo[v]
 
 
-def main_sections(block, halo, shear, thermal, final, last, w0, wa, wb, coeff):
+def main_sections(block, halo, table, final, last, w0, wa, wb, coeff):
     wn = lax.axis_index("wn")
     if halo is not None:
         gather_rows(block, halo, w0)
@@ -192,18 +202,18 @@
         final[v] = f
         last[v] = r
 
-    sections(lambda ref: set_ghost_rows(ref, wn), w0, wa, wb, coeff, shear, thermal, emit)
-
-
-def early_main_kernel(block, halo, shear, thermal, final, last, w0, wa, wb, coeff):
-    main_sections(block, halo, shear, thermal, final, last, w0, wa, wb, coeff)
+    sections(lambda ref: set_ghost_rows(ref, wn), w0, wa, wb, coeff, table, emit)
+
+
+def early_main_kernel(block, halo, table, final, last, w0, wa, wb, coeff):
+    main_sections(block, halo, table, final, last, w0, wa, wb, coeff)
 
 
 def idle_kernel(*refs):
     pass
 
 
-def late_main_kernel(block, early_halo, late_halo, shear, thermal, halo, final, last, w0, wa, wb, coeff, sem):
+def late_main_kernel(block, early_halo, late_halo, table, halo, final, last, w0, wa, wb, coeff, sem):
     place = lax.axis_index("blk") % RUN
     for known, source in ((place <= 1, early_halo), (place > 1, late_halo)):
 
@@ -215,11 +225,11 @@
 
     @pl.when(place != 0)
     def _():
-        main_sections(block, halo, shear, thermal, final, last, w0, wa, wb, coeff)
+        main_sections(block, halo, table, final, last, w0, wa, wb, coeff)
 
 
 def last_kernel(
-    block, halo, early_pair, left, right, relay, wrap, wrap_up, wrap_down, shear, thermal,
+    block, halo, early_pair, left, right, relay, wrap, wrap_up, wrap_down, table,
     early_final, early_last, late_final, late_last, final, last, w0, wa, wb, coeff, finals, lasts, in_sems, out_sems,
 ):
     wn = lax.axis_index("wn")
@@ -283,14 +293,15 @@
                 for copy in mains:
                     copy.wait()
 
-        for i, (out, staged, late, new) in enumerate(((final, finals, late_final, f), (last, lasts, late_last, r))):
+        parts = ((final, finals, late_final, f), (last, lasts, late_last, r))
+        for i, (out, staged, late, new) in enumerate(parts):
             old = jnp.where(place == 0, staged[v], late[v])
             staged[v] = jnp.where(lane_own < 3, pltpu.roll(new, LANES - 16, 1), jnp.where(lane_own >= 125, new, old))
             copy = pltpu.make_async_copy(staged.at[v], out.at[v], out_sems.at[i, v])
             copy.start()
             copies.append(copy)
 
-    sections(fix, w0, wa, wb, coeff, shear, thermal, emit)
+    sections(fix, w0, wa, wb, coeff, table, emit)
     for copy in copies:
         copy.wait()
 
@@ -361,42 +372,47 @@
 
 def local(species, flow, heat, shear, thermal):
     strips = f32(18, LANES)
+    offered = f32(20, LANES)
     rows = f32(14, 8, LANES)
     halo_shape = f32(14, 16, LANES)
     out = f32(14, OWN, LANES)
     place = lax.axis_index("blk") % RUN
-    shear, thermal = in_hbm(shear), in_hbm(thermal)
-    block, right, corner = call(
+    block, right, corner, corner_again, table = call(
         load_kernel,
-        (out, f32(4, 8, LANES), f32(3, 8, LANES)),
-        [HBM] * 3,
-        [pltpu.SemaphoreType.DMA((3,))],
-    )(in_hbm(species.reshape(11, OWN, LANES)), in_hbm(flow.reshape(2, OWN, LANES)), in_hbm(heat.reshape(1, OWN, LANES)))
-    wrap_down = send(corner, wrap_pairs(1))
+        (out, f32(4, 8, LANES), f32(4, 8, LANES), f32(3, 8, LANES), f32(248, LANES)),
+        [HBM] * 5,
+        [pltpu.SMEM((2, 11, 11), jnp.float32), pltpu.SemaphoreType.DMA((5,))],
+    )(
+        in_hbm(species.reshape(11, OWN, LANES)),
+        in_hbm(flow.reshape(2, OWN, LANES)),
+        in_hbm(heat.reshape(1, OWN, LANES)),
+        in_hbm(shear),
+        in_hbm(thermal),
+    )
+    wrap_down = send(corner_again, wrap_pairs(1))
     wrap = send(right, wrap_pairs(0))
     wrap_up = send(corner, wrap_pairs(-1))
 
     def exchange_rows(block, early):
-        second = call(second_rows_kernel, (rows,), [VMEM])(block)[0]
-        second = send(second, rows_pairs(1, early))
-        first = call(first_rows_kernel, (f32(84, LANES),), [VMEM, ANY])(block, block if early else second)[0]
-        first = send(first, rows_pairs(0, early))
-        return first, second
-
-    def early(block, shear, thermal):
+        second, first = call(rows_kernel, (rows, f32(84, LANES)), [VMEM])(block)
+        return send(first, rows_pairs(0, early)), send(second, rows_pairs(1, early))
+
+    def early(block, table):
         first, second = exchange_rows(block, True)
-        halo, pair, lows, highs = call(early_columns_kernel, (halo_shape, strips, strips, strips), [VMEM] * 3)(first, second, block)
+        halo, pair, lows, highs, offer = call(early_columns_kernel, (halo_shape, strips, strips, strips, offered), [VMEM] * 3)(
+            first, second, block
+        )
         pair = send(pair, FIRST)
-        final, last = lax.cond(place == 0, main, no_main, block, halo, shear, thermal)
-        return halo, pair, lows, highs, final, last
-
-    def not_early(block, shear, thermal):
-        return idle(halo_shape, strips, strips, strips, out, out)
-
-    def main(block, halo, shear, thermal):
-        return tuple(call(early_main_kernel, (out, out), [VMEM] * 2 + [SMEM] * 2, SCRATCH)(block, halo, shear, thermal))
-
-    def no_main(block, halo, shear, thermal):
+        final, last = lax.cond(place == 0, main, no_main, block, halo, table)
+        return halo, pair, lows, highs, offer, final, last
+
+    def not_early(block, table):
+        return idle(halo_shape, strips, strips, strips, offered, out, out)
+
+    def main(block, halo, table):
+        return tuple(call(early_main_kernel, (out, out), [VMEM] * 3, SCRATCH)(block, halo, table))
+
+    def no_main(block, halo, table):
         return idle(out, out)
 
     def edges(block, lows, highs):
@@ -412,36 +428,26 @@
     def not_late(block, lows, highs):
         return idle(halo_shape, strips, strips)
 
-    def neighbours(block, shear, thermal):
-        early_halo, early_pair, lows, highs, main_final, main_last = lax.cond(place <= 1, early, not_early, block, shear, thermal)
-
-        def rest(block, lows, highs):
-            relay = send(lows, RELAY)
-            return (*lax.cond(place > 0, late, not_late, block, lows, highs), relay)
-
-        def no_rest(block, lows, highs):
-            return idle(halo_shape, strips, strips, strips)
-
-        halo, lows, highs, relay = lax.cond(
-            at(lax.axis_index("blk"), lax.axis_index("wn")) < 2 * at(BLK, WN), rest, no_rest, block, lows, highs
-        )
-        return early_halo, halo, early_pair, lows, highs, relay, main_final, main_last
-
-    def none(block, shear, thermal):
-        return idle(halo_shape, halo_shape, strips, strips, strips, strips, out, out)
-
-    early_halo, halo, early_pair, lows, highs, relay, early_final, early_last = lax.cond(
-        at(lax.axis_index("blk"), lax.axis_index("wn")) < at(BLK, WN), neighbours, none, block, shear, thermal
-    )
+    early_halo, early_pair, lows, highs, offer, early_final, early_last = lax.cond(place <= 1, early, not_early, block, table)
+    relay = send(offer, RELAY)
+    lows = pl.pallas_call(
+        join_kernel,
+        out_shape=strips,
+        in_specs=[ANY] * 4,
+        out_specs=ANY,
+        input_output_aliases={0: 0},
+        cost_estimate=pl.CostEstimate(flops=1, bytes_accessed=1, transcendentals=0),
+    )(lows, wrap, wrap_up, wrap_down)
+    halo, lows, highs = lax.cond(place > 0, late, not_late, block, lows, highs)
     left = send(highs, FORWARD)
     right = send(lows, BACKWARD)
     halo, late_final, late_last = call(
-        late_main_kernel, (halo_shape, out, out), [VMEM] + [HBM] * 2 + [SMEM] * 2, SCRATCH + [pltpu.SemaphoreType.DMA]
-    )(block, early_halo, halo, shear, thermal)
+        late_main_kernel, (halo_shape, out, out), [VMEM, HBM, HBM, VMEM], SCRATCH + [pltpu.SemaphoreType.DMA]
+    )(block, in_hbm(early_halo), in_hbm(halo), table)
     final, last = pl.pallas_call(
         last_kernel,
         out_shape=(out, out),
-        in_specs=[VMEM] * 9 + [SMEM] * 2 + [HBM] * 2 + [VMEM] * 2,
+        in_specs=[VMEM] * 10 + [HBM] * 2 + [VMEM] * 2,
         out_specs=(HBM, HBM),
         scratch_shapes=SCRATCH
         + [pltpu.VMEM((14, OWN, LANES), jnp.float32)] * 2
@@ -449,8 +455,8 @@
         compiler_params=PARAMS,
         cost_estimate=pl.CostEstimate(flops=1, bytes_accessed=1, transcendentals=0),
     )(
-        block, halo, early_pair, left, right, relay, wrap, wrap_up, wrap_down, shear, thermal,
-        early_final, early_last, late_final, late_last,
+        block, halo, early_pair, left, right, relay, wrap, wrap_up, wrap_down, table,
+        in_hbm(early_final), in_hbm(early_last), late_final, late_last,
     )
     return final.reshape(14, 16, 2, LANES), last.reshape(14, 16, 2, LANES)
 

time: 36.1 us -> 34.7 us (0.961)
  the two profiles are of different devices: /device:TPU:128 before, /device:TPU:64 now
where the time goes in v4:
time: 34.7 us; the launch traced here: 34.4 us
  starting transfers between devices  18.7 us (54%)
  Pallas kernels  10.6 us (31%)
  waiting for transfers between devices  3.54 us (10%)
  between operations  0.82 us (2%)
  local copies, waits for them, and re-layouts  0.61 us (2%)
    ppermute x9, starting transfers between devices, send(): return lax.ppermute(x, ('blk', 'wn'), pairs)  18.7 us
    pallas_call x1, Pallas kernels, local(): pl.pallas_call(last_kernel, out_shape=(out, out), in_specs=[VMEM] * 10 +...  4.56 us
    ppermute x9, waiting for transfers between devices, send(): return lax.ppermute(x, ('blk', 'wn'), pairs)  3.54 us
    pallas_call x1, Pallas kernels, local(): call(late_main_kernel, (halo_shape, out, out), [VMEM, HBM, HBM, VMEM], SC...  3.5 us
    pallas_call x1, Pallas kernels, local(): call(load_kernel, (out, f32(4, 8, LANES), f32(4, 8, LANES), f32(3, 8, LAN...  1.26 us
  transfers between devices with their start and end apart: 9, of which 3 were waited for; matrix products, arithmetic and copies ran while one was open for 0% of the time, Pallas kernels for 14%

profile of v4, /device:TPU:64, one launch (start us, length us, event | category | flops | bytes accessed | tf_op | source)
XLA Modules:
  0.0 34.4 jit_solution(8734013096948961599)
XLA Ops:
  0.6 1.3 %shard_map.68 = (f32[14,32,128]{2,1,0:T(8,128)S(1)}, f32[4,8,128]{2,1,0:T(8,128)S(1)}, f32[4,8,128]{2,1,0:T(8,128)S(1)}, f32[3,8,128]{2,1,0:T(8,128)S(1)}, f32[248,128]{1,0:T(8,128)S(1)}) custom-call(f32[11,32,128]{2,1,0:T(8,128)} %bitcast.5, f32[2,32,128]{2,1,0:T(8,128)} %bitcast.6, f32[1,32,128]{2,1,0:T(8,128)} %bitcast.7, f32[11,11]{1,0:T(8,128)} %shear.1, ...), custom_call_target="tpu_custom_call" | custom-call | flops 1 | bytes 1 | tf_op jit(solution)/shard_map/pallas_call | solution.py:380
  1.9 0.7 %collective-permute-start.5 = (f32[4,8,128]{2,1,0:T(8,128)S(1)}, f32[4,8,128]{2,1,0:T(8,128)S(1)}, u32[]{:S(2)}, u32[]{:S(2)}) collective-permute-start(f32[4,8,128]{2,1,0:T(8,128)S(1)} %get-tuple-element.76), channel_id=1, source_target_pairs={{88,96},{89,97},{90,98},{91,99},{92,100},{93,101},{94,102},{95,103... | collective-permute-start | bytes 49160 | tf_op jit(solution)/shard_map/ppermute | solution.py:333
  2.6 0.7 %collective-permute-start.6 = (f32[4,8,128]{2,1,0:T(8,128)S(1)}, f32[4,8,128]{2,1,0:T(8,128)S(1)}, u32[]{:S(2)}, u32[]{:S(2)}) collective-permute-start(f32[4,8,128]{2,1,0:T(8,128)S(1)} %get-tuple-element.77), channel_id=1, source_target_pairs={{89,96},{90,97},{91,98},{92,99},{93,100},{94,101},{95,102},{185,19... | collective-permute-start | bytes 49160 | tf_op jit(solution)/shard_map/ppermute | solution.py:333
  3.2 0.7 %collective-permute-start.7 = (f32[3,8,128]{2,1,0:T(8,128)S(1)}, f32[3,8,128]{2,1,0:T(8,128)S(1)}, u32[]{:S(2)}, u32[]{:S(2)}) collective-permute-start(f32[3,8,128]{2,1,0:T(8,128)S(1)} %get-tuple-element.78), channel_id=1, source_target_pairs={{88,97},{89,98},{90,99},{91,100},{92,101},{93,102},{94,103},{184,1... | collective-permute-start | bytes 36872 | tf_op jit(solution)/shard_map/ppermute | solution.py:333
  3.9 16.9 %conditional.4 = ((f32[14,16,128]{2,1,0:T(8,128)}, f32[18,128]{1,0:T(8,128)}, f32[18,128]{1,0:T(8,128)S(1)}, f32[18,128]{1,0:T(8,128)S(1)}, f32[20,128]{1,0:T(8,...) conditional(s32[]{:T(128)} %convert_element_type.12, () %tuple.34, (f32[14,32,128]{2,1,0:T(8,128)S(1)}, ...), branch_computations={%region_0.1_spmd, %region_1.4_spmd} | conditional | flops 5 | bytes 438505 | solution.py:431
  4.0 0.7 %collective-permute-start.1 = (f32[14,8,128]{2,1,0:T(8,128)S(1)}, f32[14,8,128]{2,1,0:T(8,128)S(1)}, u32[]{:S(2)}, u32[]{:S(2)}) collective-permute-start(f32[14,8,128]{2,1,0:T(8,128)S(1)} %get-tuple-element.30), channel_id=1, source_target_pairs={{1,2},{3,4},{5,6},{9,10},{11,12},{13,14},{97,98},{99,100},{101,102... | collective-permute-start | bytes 172040 | tf_op jit(solution)/shard_map/cond/branch_1_fun/ppermute | solution.py:333
  4.7 5.9 %collective-permute-start = (f32[84,128]{1,0:T(8,128)S(1)}, f32[84,128]{1,0:T(8,128)S(1)}, u32[]{:S(2)}, u32[]{:S(2)}) collective-permute-start(f32[84,128]{1,0:T(8,128)S(1)} %get-tuple-element.29), channel_id=1, source_target_pairs={{0,1},{2,3},{4,5},{6,7},{8,9},{10,11},{12,13},{14,15},{96,97},{98,... | collective-permute-start | bytes 129032 | tf_op jit(solution)/shard_map/cond/branch_1_fun/ppermute | solution.py:333
  10.5 0.9 %collective-permute-done.first = f32[84,128]{1,0:T(8,128)S(1)} collective-permute-done((f32[84,128]{1,0:T(8,128)S(1)}, f32[84,128]{1,0:T(8,128)S(1)}, u32[]{:S(2)}, u32[]{:S(2)}) %collective-permute-start) | collective-permute-done | bytes 43040 | tf_op jit(solution)/shard_map/cond/branch_1_fun/ppermute | solution.py:333
  11.4 0.0 collective-permute-done.1.second
  11.4 0.7 %branch_1_fun.7 = (f32[14,16,128]{2,1,0:T(8,128)}, f32[18,128]{1,0:T(8,128)S(1)}, f32[18,128]{1,0:T(8,128)S(1)}, f32[18,128]{1,0:T(8,128)S(1)}, f32[20,128]{1,0:T(8,128)S(1)}) custom-call(f32[84,128]{1,0:T(8,128)S(1)} %collective-permute-done.first, f32[14,8,128]{2,1,0:T(8,128)S(1)} %collective-permute-done.1.second, f32[14,32,128]{2,1,0:T(8,128)S(1)} %get-tuple-element.28.block), custom_call_target="tpu_custom_call" | custom-call | flops 1 | bytes 1 | tf_op jit(solution)/shard_map/cond/branch_1_fun/pallas_call | solution.py:402
  12.1 7.0 %collective-permute-start.2 = (f32[18,128]{1,0:T(8,128)S(1)}, f32[18,128]{1,0:T(8,128)}, u32[]{:S(2)}, u32[]{:S(2)}) collective-permute-start(f32[18,128]{1,0:T(8,128)S(1)} %get-tuple-element.32), channel_id=1, source_target_pairs={{0,8},{1,9},{2,10},{3,11},{4,12},{5,13},{6,14},{7,15},{96,104},{97... | collective-permute-start | bytes 27656 | tf_op jit(solution)/shard_map/cond/branch_1_fun/ppermute | solution.py:333
  19.1 1.7 %collective-permute-done.2 = f32[18,128]{1,0:T(8,128)} collective-permute-done((f32[18,128]{1,0:T(8,128)S(1)}, f32[18,128]{1,0:T(8,128)}, u32[]{:S(2)}, u32[]{:S(2)}) %collective-permute-start.2) | collective-permute-done | bytes 9248 | tf_op jit(solution)/shard_map/cond/branch_1_fun/ppermute | solution.py:333
  20.8 0.7 %collective-permute-start.10 = (f32[20,128]{1,0:T(8,128)S(1)}, f32[20,128]{1,0:T(8,128)S(1)}, u32[]{:S(2)}, u32[]{:S(2)}) collective-permute-start(f32[20,128]{1,0:T(8,128)S(1)} %get-tuple-element.85), channel_id=1, source_target_pairs={{96,88},{97,89},{98,90},{99,91},{100,92},{101,93},{102,94},{103,95... | collective-permute-start | bytes 30728 | tf_op jit(solution)/shard_map/ppermute | solution.py:333
  21.5 0.0 collective-permute-done.7.c.wrap_down
  21.5 0.0 copy-start.4
  21.5 0.0 collective-permute-done.5.a.wrap
  21.5 0.0 copy-start
  21.5 0.0 collective-permute-done.6.b.wrap_up
  21.5 0.0 copy-start.2
  21.5 0.5 %copy-done.4 = f32[3,8,128]{2,1,0:T(8,128)} copy-done((f32[3,8,128]{2,1,0:T(8,128)}, f32[3,8,128]{2,1,0:T(8,128)S(1)}, u32[]{:S(2)}) %copy-start.4) | copy-done | bytes 12312
  22.1 0.0 copy-done
  22.1 0.0 copy-done.2
  22.1 0.6 %conditional.5 = ((f32[14,16,128]{2,1,0:T(8,128)}, f32[18,128]{1,0:T(8,128)}, f32[18,128]{1,0:T(8,128)})) conditional(s32[]{:T(128)} %convert_element_type.13, () %tuple.36, (s32[]{:T(128)}, f32[18,128]{1,0:T(8,128)S(1)}, f32[18,128]{1,0:T(8,128)S(1)}, f32[14,32,128]{2,1,0:T(8,128)S(1)}) %tuple.37), branch_computations={%region_4.5_spmd, %region_5.8_spmd} | conditional | flops 4 | bytes 401528 | solution.py:441
  22.1 0.6 %conditional.1 = ((f32[14,16,128]{2,1,0:T(8,128)}, f32[18,128]{1,0:T(8,128)}, f32[18,128]{1,0:T(8,128)})) conditional(s32[]{:T(128)} %convert_element_type.9, (f32[18,128]{1,0:T(8,128)S(1)}, f32[18,128]{1,0:T(8,128)S(1)}) %tuple.27, f32[14,32,128]{2,1,0:T(8,128)S(1)} %get-tuple-element.49), branch_computations={%region_6.6_spmd, %region_7.7_spmd} | conditional | flops 2 | bytes 401498 | solution.py:426
  22.1 0.6 %branch_0_fun.9 = (f32[18,128]{1,0:T(8,128)}, f32[18,128]{1,0:T(8,128)}) custom-call(f32[18,128]{1,0:T(8,128)S(1)} %get-tuple-element.40.early_lows, f32[18,128]{1,0:T(8,128)S(1)} %get-tuple-element.41.early_highs), custom_call_target="tpu_custom_call" | custom-call | flops 1 | bytes 1 | tf_op jit(solution)/shard_map/cond/branch_1_fun/cond/branch_0_fun/pallas_call | solution.py:423
  22.7 1.3 %collective-permute-start.8 = (f32[18,128]{1,0:T(8,128)}, f32[18,128]{1,0:T(8,128)S(1)}, u32[]{:S(2)}, u32[]{:S(2)}) collective-permute-start(f32[18,128]{1,0:T(8,128)} %get-tuple-element.83), channel_id=1, source_target_pairs={{8,16},{9,17},{10,18},{11,19},{12,20},{13,21},{14,22},{15,23},{16,... | collective-permute-start | bytes 27656 | tf_op jit(solution)/shard_map/ppermute | solution.py:333
  24.0 1.3 %collective-permute-start.9 = (f32[18,128]{1,0:T(8,128)}, f32[18,128]{1,0:T(8,128)S(1)}, u32[]{:S(2)}, u32[]{:S(2)}) collective-permute-start(f32[18,128]{1,0:T(8,128)} %get-tuple-element.84), channel_id=1, source_target_pairs={{16,8},{17,9},{18,10},{19,11},{20,12},{21,13},{22,14},{23,15},{24,... | collective-permute-start | bytes 27656 | tf_op jit(solution)/shard_map/ppermute | solution.py:333
  25.3 0.0 copy-start.1
  25.3 0.0 copy-start.3
  25.3 0.0 copy-start.5
  25.3 3.5 %shard_map.70 = (f32[14,16,128]{2,1,0:T(8,128)S(1)}, f32[14,32,128]{2,1,0:T(8,128)S(1)}, f32[14,32,128]{2,1,0:T(8,128)S(1)}) custom-call(f32[14,32,128]{2,1,0:T(8,128)S(1)} %get-tuple-element.72.block, f32[14,16,128]{2,1,0:T(8,128)} %get-tuple-element.74.early_halo, f32[14,16,128]{2,1,0:T(8,128)} %get-tuple-element.80.late_halo, ...), custom_call_target="tpu_custom_call" | custom-call | flops 1 | bytes 1 | tf_op jit(solution)/shard_map/pallas_call | solution.py:444
  28.8 0.0 collective-permute-done.10.relay
  28.9 0.0 collective-permute-done.8.left
  28.9 0.9 %collective-permute-done.9.right = f32[18,128]{1,0:T(8,128)S(1)} collective-permute-done((f32[18,128]{1,0:T(8,128)}, f32[18,128]{1,0:T(8,128)S(1)}, u32[]{:S(2)}, u32[]{:S(2)}) %collective-permute-start.9) | collective-permute-done | bytes 9248 | tf_op jit(solution)/shard_map/ppermute | solution.py:333
  29.8 0.0 copy-done.1
  29.8 0.0 copy-done.3
  29.8 0.0 copy-done.5
  29.8 4.6 %shard_map.71 = (f32[14,32,128]{2,1,0:T(8,128)}, f32[14,32,128]{2,1,0:T(8,128)}) custom-call(f32[14,32,128]{2,1,0:T(8,128)S(1)} %get-tuple-element.72.block, f32[14,16,128]{2,1,0:T(8,128)S(1)} %get-tuple-element.81.halo, f32[18,128]{1,0:T(8,128)} %get-tuple-element.82.early_pair, f32[18,128]{1,0:T(8,128)S(1)} %collective-permute-done.8.left, ...), custom_call_target="tpu_custom_call" | custom-call | flops 1 | bytes 1 | tf_op jit(solution)/shard_map/pallas_call | solution.py:447
  (5 shorter events, 0.0 us)
Async XLA Ops:
  1.9 19.6 %collective-permute-start.5 = (f32[4,8,128]{2,1,0:T(8,128)S(1)}, f32[4,8,128]{2,1,0:T(8,128)S(1)}, u32[]{:S(2)}, u32[]{:S(2)}) collective-permute-start(f32[4,8,128]{2,1,0:T(8,128)S(1)} %get-tuple-element.76), channel_id=1, source_target_pairs={{88,96},{89,97},{90,98},{91,99},{92,100},{93,101},{94,102},{95,103... | collective-permute-start | bytes 49160 | tf_op jit(solution)/shard_map/ppermute | solution.py:333
  2.6 18.9 %collective-permute-start.6 = (f32[4,8,128]{2,1,0:T(8,128)S(1)}, f32[4,8,128]{2,1,0:T(8,128)S(1)}, u32[]{:S(2)}, u32[]{:S(2)}) collective-permute-start(f32[4,8,128]{2,1,0:T(8,128)S(1)} %get-tuple-element.77), channel_id=1, source_target_pairs={{89,96},{90,97},{91,98},{92,99},{93,100},{94,101},{95,102},{185,19... | collective-permute-start | bytes 49160 | tf_op jit(solution)/shard_map/ppermute | solution.py:333
  3.2 18.2 %collective-permute-start.7 = (f32[3,8,128]{2,1,0:T(8,128)S(1)}, f32[3,8,128]{2,1,0:T(8,128)S(1)}, u32[]{:S(2)}, u32[]{:S(2)}) collective-permute-start(f32[3,8,128]{2,1,0:T(8,128)S(1)} %get-tuple-element.78), channel_id=1, source_target_pairs={{88,97},{89,98},{90,99},{91,100},{92,101},{93,102},{94,103},{184,1... | collective-permute-start | bytes 36872 | tf_op jit(solution)/shard_map/ppermute | solution.py:333
  4.0 7.4 %collective-permute-start.1 = (f32[14,8,128]{2,1,0:T(8,128)S(1)}, f32[14,8,128]{2,1,0:T(8,128)S(1)}, u32[]{:S(2)}, u32[]{:S(2)}) collective-permute-start(f32[14,8,128]{2,1,0:T(8,128)S(1)} %get-tuple-element.30), channel_id=1, source_target_pairs={{1,2},{3,4},{5,6},{9,10},{11,12},{13,14},{97,98},{99,100},{101,102... | collective-permute-start | bytes 172040 | tf_op jit(solution)/shard_map/cond/branch_1_fun/ppermute | solution.py:333
  4.7 6.7 %collective-permute-start = (f32[84,128]{1,0:T(8,128)S(1)}, f32[84,128]{1,0:T(8,128)S(1)}, u32[]{:S(2)}, u32[]{:S(2)}) collective-permute-start(f32[84,128]{1,0:T(8,128)S(1)} %get-tuple-element.29), channel_id=1, source_target_pairs={{0,1},{2,3},{4,5},{6,7},{8,9},{10,11},{12,13},{14,15},{96,97},{98,... | collective-permute-start | bytes 129032 | tf_op jit(solution)/shard_map/cond/branch_1_fun/ppermute | solution.py:333
  12.1 8.7 %collective-permute-start.2 = (f32[18,128]{1,0:T(8,128)S(1)}, f32[18,128]{1,0:T(8,128)}, u32[]{:S(2)}, u32[]{:S(2)}) collective-permute-start(f32[18,128]{1,0:T(8,128)S(1)} %get-tuple-element.32), channel_id=1, source_target_pairs={{0,8},{1,9},{2,10},{3,11},{4,12},{5,13},{6,14},{7,15},{96,104},{97... | collective-permute-start | bytes 27656 | tf_op jit(solution)/shard_map/cond/branch_1_fun/ppermute | solution.py:333
  20.8 8.1 %collective-permute-start.10 = (f32[20,128]{1,0:T(8,128)S(1)}, f32[20,128]{1,0:T(8,128)S(1)}, u32[]{:S(2)}, u32[]{:S(2)}) collective-permute-start(f32[20,128]{1,0:T(8,128)S(1)} %get-tuple-element.85), channel_id=1, source_target_pairs={{96,88},{97,89},{98,90},{99,91},{100,92},{101,93},{102,94},{103,95... | collective-permute-start | bytes 30728 | tf_op jit(solution)/shard_map/ppermute | solution.py:333
  21.5 0.6 %copy-start.4 = (f32[3,8,128]{2,1,0:T(8,128)}, f32[3,8,128]{2,1,0:T(8,128)S(1)}, u32[]{:S(2)}) copy-start(f32[3,8,128]{2,1,0:T(8,128)S(1)} %collective-permute-done.7.c.wrap_down) | copy-start | bytes 36868
  21.5 0.6 %copy-start = (f32[4,8,128]{2,1,0:T(8,128)}, f32[4,8,128]{2,1,0:T(8,128)S(1)}, u32[]{:S(2)}) copy-start(f32[4,8,128]{2,1,0:T(8,128)S(1)} %collective-permute-done.5.a.wrap) | copy-start | bytes 49156
  21.5 0.6 %copy-start.2 = (f32[4,8,128]{2,1,0:T(8,128)}, f32[4,8,128]{2,1,0:T(8,128)S(1)}, u32[]{:S(2)}) copy-start(f32[4,8,128]{2,1,0:T(8,128)S(1)} %collective-permute-done.6.b.wrap_up) | copy-start | bytes 49156
  22.7 6.1 %collective-permute-start.8 = (f32[18,128]{1,0:T(8,128)}, f32[18,128]{1,0:T(8,128)S(1)}, u32[]{:S(2)}, u32[]{:S(2)}) collective-permute-start(f32[18,128]{1,0:T(8,128)} %get-tuple-element.83), channel_id=1, source_target_pairs={{8,16},{9,17},{10,18},{11,19},{12,20},{13,21},{14,22},{15,23},{16,... | collective-permute-start | bytes 27656 | tf_op jit(solution)/shard_map/ppermute | solution.py:333
  24.0 5.8 %collective-permute-start.9 = (f32[18,128]{1,0:T(8,128)}, f32[18,128]{1,0:T(8,128)S(1)}, u32[]{:S(2)}, u32[]{:S(2)}) collective-permute-start(f32[18,128]{1,0:T(8,128)} %get-tuple-element.84), channel_id=1, source_target_pairs={{16,8},{17,9},{18,10},{19,11},{20,12},{21,13},{22,14},{23,15},{24,... | collective-permute-start | bytes 27656 | tf_op jit(solution)/shard_map/ppermute | solution.py:333
  25.3 4.5 %copy-start.1 = (f32[4,8,128]{2,1,0:T(8,128)S(1)}, f32[4,8,128]{2,1,0:T(8,128)}, u32[]{:S(2)}) copy-start(f32[4,8,128]{2,1,0:T(8,128)} %copy-done) | copy-start | bytes 49156
  25.3 4.5 %copy-start.3 = (f32[4,8,128]{2,1,0:T(8,128)S(1)}, f32[4,8,128]{2,1,0:T(8,128)}, u32[]{:S(2)}) copy-start(f32[4,8,128]{2,1,0:T(8,128)} %copy-done.2) | copy-start | bytes 49156
  25.3 4.5 %copy-start.5 = (f32[3,8,128]{2,1,0:T(8,128)S(1)}, f32[3,8,128]{2,1,0:T(8,128)}, u32[]{:S(2)}) copy-start(f32[3,8,128]{2,1,0:T(8,128)} %copy-done.4) | copy-start | bytes 36868

commit v5 on v4

--- a/solution.py
+++ b/solution.py
@@ -57,10 +57,11 @@
 
 
 def faces(coeff):
-    out = []
-    for k in (coeff[1], coeff[0]):
-        out.append((k + pltpu.roll(k, ROWS - 2, 0), k + pltpu.roll(k, LANES - 1, 1)))
-    return out
+    for index, fields in ((1, (*range(11), 13)), (0, (11, 12))):
+        k = coeff[index]
+        face = (k + pltpu.roll(k, ROWS - 2, 0), k + pltpu.roll(k, LANES - 1, 1))
+        for v in fields:
+            yield v, face
 
 
 def residual(w, face):
@@ -73,22 +74,19 @@
 def sections(fix, w0, wa, wb, coeff, table, emit):
     fix(w0)
     coefficients(w0, coeff, table)
-    face = faces(coeff)
-    for v in range(14):
+    for v, face in faces(coeff):
         w = w0[v]
-        wa[v] = w + STEP * residual(w, face[v in (11, 12)])
+        wa[v] = w + STEP * residual(w, face)
     fix(wa)
     coefficients(wa, coeff, table)
-    face = faces(coeff)
-    for v in range(14):
+    for v, face in faces(coeff):
         w = wa[v]
-        wb[v] = 0.75 * w0[v] + 0.25 * (w + STEP * residual(w, face[v in (11, 12)]))
+        wb[v] = 0.75 * w0[v] + 0.25 * (w + STEP * residual(w, face))
     fix(wb)
     coefficients(wb, coeff, table)
-    face = faces(coeff)
-    for v in range(14):
+    for v, face in faces(coeff):
         w = wb[v]
-        last = residual(w, face[v in (11, 12)])
+        last = residual(w, face)
         final = w0[v] * np.float32(1.0 / 3.0) + np.float32(2.0 / 3.0) * (w + STEP * last)
         emit(v, final[:OWN], last[:OWN])
 
@@ -230,13 +228,19 @@
 
 def last_kernel(
     block, halo, early_pair, left, right, relay, wrap, wrap_up, wrap_down, table,
-    early_final, early_last, late_final, late_last, final, last, w0, wa, wb, coeff, finals, lasts, in_sems, out_sems,
+    early_final, early_last, late_final, late_last, final, last, w0, wa, wb, coeff, finals, lasts, pair_rows, in_sems, out_sems,
 ):
     wn = lax.axis_index("wn")
     blk = lax.axis_index("blk")
     place = blk % RUN
     mains = [pltpu.make_async_copy(a, b, in_sems.at[i]) for i, (a, b) in enumerate(((early_final, finals), (early_last, lasts)))]
 
+    beside = pltpu.make_async_copy(early_pair, pair_rows, in_sems.at[2])
+
+    @pl.when(place <= 1)
+    def _():
+        beside.start()
+
     @pl.when(place == 0)
     def _():
         for copy in mains:
@@ -244,6 +248,11 @@
 
     lane = iota((ROWS, LANES), 1)
     gather_rows(block, halo, w0)
+
+    @pl.when(place <= 1)
+    def _():
+        beside.wait()
+
     lane3 = iota((3, LANES), 1)
     tiles = []
     for t in range(6):
@@ -252,8 +261,8 @@
             from_wrap = wrap[t, 5:8]
         else:
             from_wrap = jnp.where(lane3 % 16 < 8, wrap_up[t - 4, 5:8], wrap_down[t - 4, 5:8])
-        lo = jnp.where(place == 0, from_wrap, jnp.where(place == 1, early_pair[three], left[three]))
-        hi = jnp.where(place == RUN - 1, relay[three], jnp.where(place == 0, early_pair[three], right[three]))
+        lo = jnp.where(place == 0, from_wrap, jnp.where(place == 1, pair_rows[three], left[three]))
+        hi = jnp.where(place == RUN - 1, relay[three], jnp.where(place == 0, pair_rows[three], right[three]))
         full = jnp.concatenate([hi, jnp.zeros((10, LANES), jnp.float32), lo, jnp.zeros((112, LANES), jnp.float32)], axis=0)
         tiles.append(full.T)
     for v in range(14):
@@ -447,15 +456,15 @@
     final, last = pl.pallas_call(
         last_kernel,
         out_shape=(out, out),
-        in_specs=[VMEM] * 10 + [HBM] * 2 + [VMEM] * 2,
+        in_specs=[VMEM] * 2 + [HBM] + [VMEM] * 7 + [HBM] * 2 + [VMEM] * 2,
         out_specs=(HBM, HBM),
         scratch_shapes=SCRATCH
         + [pltpu.VMEM((14, OWN, LANES), jnp.float32)] * 2
-        + [pltpu.SemaphoreType.DMA((2,)), pltpu.SemaphoreType.DMA((2, 14))],
+        + [pltpu.VMEM((18, LANES), jnp.float32), pltpu.SemaphoreType.DMA((3,)), pltpu.SemaphoreType.DMA((2, 14))],
         compiler_params=PARAMS,
         cost_estimate=pl.CostEstimate(flops=1, bytes_accessed=1, transcendentals=0),
     )(
-        block, halo, early_pair, left, right, relay, wrap, wrap_up, wrap_down, table,
+        block, halo, in_hbm(early_pair), left, right, relay, wrap, wrap_up, wrap_down, table,
         in_hbm(early_final), in_hbm(early_last), late_final, late_last,
     )
     return final.reshape(14, 16, 2, LANES), last.reshape(14, 16, 2, LANES)

time: 34.7 us -> 34.7 us (level)
  transfers between devices with their start and end apart: 9 -> 9, of which waited for: 3 -> 3; matrix products, arithmetic and copies ran while one was open for 0% -> 0% of each run, Pallas kernels for 14% -> 13%
where the time goes in v5:
time: 34.7 us; the launch traced here: 34.4 us
  starting transfers between devices  18.7 us (54%)
  Pallas kernels  10.4 us (30%)
  waiting for transfers between devices  3.74 us (11%)
  between operations  0.82 us (2%)
  local copies, waits for them, and re-layouts  0.61 us (2%)
    ppermute x9, starting transfers between devices, send(): return lax.ppermute(x, ('blk', 'wn'), pairs)  18.7 us
    pallas_call x1, Pallas kernels, local(): pl.pallas_call(last_kernel, out_shape=(out, out), in_specs=[VMEM] * 2 + [...  4.54 us
    ppermute x9, waiting for transfers between devices, send(): return lax.ppermute(x, ('blk', 'wn'), pairs)  3.74 us
    pallas_call x1, Pallas kernels, local(): call(late_main_kernel, (halo_shape, out, out), [VMEM, HBM, HBM, VMEM], SC...  3.3 us
    pallas_call x1, Pallas kernels, local(): call(load_kernel, (out, f32(4, 8, LANES), f32(4, 8, LANES), f32(3, 8, LAN...  1.26 us
  transfers between devices with their start and end apart: 9, of which 3 were waited for; matrix products, arithmetic and copies ran while one was open for 0% of the time, Pallas kernels for 13%

profile of v5, /device:TPU:64, one launch (start us, length us, event | category | flops | bytes accessed | tf_op | source)
XLA Modules:
  0.0 34.4 jit_solution(4478930066338617359)
XLA Ops:
  0.6 1.3 %shard_map.68 = (f32[14,32,128]{2,1,0:T(8,128)S(1)}, f32[4,8,128]{2,1,0:T(8,128)S(1)}, f32[4,8,128]{2,1,0:T(8,128)S(1)}, f32[3,8,128]{2,1,0:T(8,128)S(1)}, f32[248,128]{1,0:T(8,128)S(1)}) custom-call(f32[11,32,128]{2,1,0:T(8,128)} %bitcast.5, f32[2,32,128]{2,1,0:T(8,128)} %bitcast.6, f32[1,32,128]{2,1,0:T(8,128)} %bitcast.7, f32[11,11]{1,0:T(8,128)} %shear.1, ...), custom_call_target="tpu_custom_call" | custom-call | flops 1 | bytes 1 | tf_op jit(solution)/shard_map/pallas_call | solution.py:389
  1.9 0.7 %collective-permute-start.5 = (f32[4,8,128]{2,1,0:T(8,128)S(1)}, f32[4,8,128]{2,1,0:T(8,128)S(1)}, u32[]{:S(2)}, u32[]{:S(2)}) collective-permute-start(f32[4,8,128]{2,1,0:T(8,128)S(1)} %get-tuple-element.76), channel_id=1, source_target_pairs={{88,96},{89,97},{90,98},{91,99},{92,100},{93,101},{94,102},{95,103... | collective-permute-start | bytes 49160 | tf_op jit(solution)/shard_map/ppermute | solution.py:342
  2.6 0.7 %collective-permute-start.6 = (f32[4,8,128]{2,1,0:T(8,128)S(1)}, f32[4,8,128]{2,1,0:T(8,128)S(1)}, u32[]{:S(2)}, u32[]{:S(2)}) collective-permute-start(f32[4,8,128]{2,1,0:T(8,128)S(1)} %get-tuple-element.77), channel_id=1, source_target_pairs={{89,96},{90,97},{91,98},{92,99},{93,100},{94,101},{95,102},{185,19... | collective-permute-start | bytes 49160 | tf_op jit(solution)/shard_map/ppermute | solution.py:342
  3.2 0.7 %collective-permute-start.7 = (f32[3,8,128]{2,1,0:T(8,128)S(1)}, f32[3,8,128]{2,1,0:T(8,128)S(1)}, u32[]{:S(2)}, u32[]{:S(2)}) collective-permute-start(f32[3,8,128]{2,1,0:T(8,128)S(1)} %get-tuple-element.78), channel_id=1, source_target_pairs={{88,97},{89,98},{90,99},{91,100},{92,101},{93,102},{94,103},{184,1... | collective-permute-start | bytes 36872 | tf_op jit(solution)/shard_map/ppermute | solution.py:342
  3.9 16.9 %conditional.4 = ((f32[14,16,128]{2,1,0:T(8,128)}, f32[18,128]{1,0:T(8,128)}, f32[18,128]{1,0:T(8,128)S(1)}, f32[18,128]{1,0:T(8,128)S(1)}, f32[20,128]{1,0:T(8,...) conditional(s32[]{:T(128)} %convert_element_type.12, () %tuple.34, (f32[14,32,128]{2,1,0:T(8,128)S(1)}, ...), branch_computations={%region_0.1_spmd, %region_1.4_spmd} | conditional | flops 5 | bytes 438505 | solution.py:440
  4.0 0.7 %collective-permute-start.1 = (f32[14,8,128]{2,1,0:T(8,128)S(1)}, f32[14,8,128]{2,1,0:T(8,128)S(1)}, u32[]{:S(2)}, u32[]{:S(2)}) collective-permute-start(f32[14,8,128]{2,1,0:T(8,128)S(1)} %get-tuple-element.30), channel_id=1, source_target_pairs={{1,2},{3,4},{5,6},{9,10},{11,12},{13,14},{97,98},{99,100},{101,102... | collective-permute-start | bytes 172040 | tf_op jit(solution)/shard_map/cond/branch_1_fun/ppermute | solution.py:342
  4.7 5.9 %collective-permute-start = (f32[84,128]{1,0:T(8,128)S(1)}, f32[84,128]{1,0:T(8,128)S(1)}, u32[]{:S(2)}, u32[]{:S(2)}) collective-permute-start(f32[84,128]{1,0:T(8,128)S(1)} %get-tuple-element.29), channel_id=1, source_target_pairs={{0,1},{2,3},{4,5},{6,7},{8,9},{10,11},{12,13},{14,15},{96,97},{98,... | collective-permute-start | bytes 129032 | tf_op jit(solution)/shard_map/cond/branch_1_fun/ppermute | solution.py:342
  10.5 0.9 %collective-permute-done.first = f32[84,128]{1,0:T(8,128)S(1)} collective-permute-done((f32[84,128]{1,0:T(8,128)S(1)}, f32[84,128]{1,0:T(8,128)S(1)}, u32[]{:S(2)}, u32[]{:S(2)}) %collective-permute-start) | collective-permute-done | bytes 43040 | tf_op jit(solution)/shard_map/cond/branch_1_fun/ppermute | solution.py:342
  11.4 0.0 collective-permute-done.1.second
  11.4 0.7 %branch_1_fun.7 = (f32[14,16,128]{2,1,0:T(8,128)}, f32[18,128]{1,0:T(8,128)S(1)}, f32[18,128]{1,0:T(8,128)S(1)}, f32[18,128]{1,0:T(8,128)S(1)}, f32[20,128]{1,0:T(8,128)S(1)}) custom-call(f32[84,128]{1,0:T(8,128)S(1)} %collective-permute-done.first, f32[14,8,128]{2,1,0:T(8,128)S(1)} %collective-permute-done.1.second, f32[14,32,128]{2,1,0:T(8,128)S(1)} %get-tuple-element.28.block), custom_call_target="tpu_custom_call" | custom-call | flops 1 | bytes 1 | tf_op jit(solution)/shard_map/cond/branch_1_fun/pallas_call | solution.py:411
  12.1 7.0 %collective-permute-start.2 = (f32[18,128]{1,0:T(8,128)S(1)}, f32[18,128]{1,0:T(8,128)}, u32[]{:S(2)}, u32[]{:S(2)}) collective-permute-start(f32[18,128]{1,0:T(8,128)S(1)} %get-tuple-element.32), channel_id=1, source_target_pairs={{0,8},{1,9},{2,10},{3,11},{4,12},{5,13},{6,14},{7,15},{96,104},{97... | collective-permute-start | bytes 27656 | tf_op jit(solution)/shard_map/cond/branch_1_fun/ppermute | solution.py:342
  19.1 1.7 %collective-permute-done.2 = f32[18,128]{1,0:T(8,128)} collective-permute-done((f32[18,128]{1,0:T(8,128)S(1)}, f32[18,128]{1,0:T(8,128)}, u32[]{:S(2)}, u32[]{:S(2)}) %collective-permute-start.2) | collective-permute-done | bytes 9248 | tf_op jit(solution)/shard_map/cond/branch_1_fun/ppermute | solution.py:342
  20.8 0.7 %collective-permute-start.10 = (f32[20,128]{1,0:T(8,128)S(1)}, f32[20,128]{1,0:T(8,128)S(1)}, u32[]{:S(2)}, u32[]{:S(2)}) collective-permute-start(f32[20,128]{1,0:T(8,128)S(1)} %get-tuple-element.85), channel_id=1, source_target_pairs={{96,88},{97,89},{98,90},{99,91},{100,92},{101,93},{102,94},{103,95... | collective-permute-start | bytes 30728 | tf_op jit(solution)/shard_map/ppermute | solution.py:342
  21.5 0.0 collective-permute-done.7.c.wrap_down
  21.5 0.0 copy-start.4
  21.5 0.0 collective-permute-done.5.a.wrap
  21.5 0.0 copy-start
  21.5 0.0 collective-permute-done.6.b.wrap_up
  21.5 0.0 copy-start.2
  21.5 0.5 %copy-done.4 = f32[3,8,128]{2,1,0:T(8,128)} copy-done((f32[3,8,128]{2,1,0:T(8,128)}, f32[3,8,128]{2,1,0:T(8,128)S(1)}, u32[]{:S(2)}) %copy-start.4) | copy-done | bytes 12312
  22.1 0.0 copy-done
  22.1 0.0 copy-done.2
  22.1 0.6 %conditional.5 = ((f32[14,16,128]{2,1,0:T(8,128)}, f32[18,128]{1,0:T(8,128)}, f32[18,128]{1,0:T(8,128)})) conditional(s32[]{:T(128)} %convert_element_type.13, () %tuple.36, (s32[]{:T(128)}, f32[18,128]{1,0:T(8,128)S(1)}, f32[18,128]{1,0:T(8,128)S(1)}, f32[14,32,128]{2,1,0:T(8,128)S(1)}) %tuple.37), branch_computations={%region_4.5_spmd, %region_5.8_spmd} | conditional | flops 4 | bytes 401528 | solution.py:450
  22.1 0.6 %conditional.1 = ((f32[14,16,128]{2,1,0:T(8,128)}, f32[18,128]{1,0:T(8,128)}, f32[18,128]{1,0:T(8,128)})) conditional(s32[]{:T(128)} %convert_element_type.9, (f32[18,128]{1,0:T(8,128)S(1)}, f32[18,128]{1,0:T(8,128)S(1)}) %tuple.27, f32[14,32,128]{2,1,0:T(8,128)S(1)} %get-tuple-element.49), branch_computations={%region_6.6_spmd, %region_7.7_spmd} | conditional | flops 2 | bytes 401498 | solution.py:435
  22.1 0.6 %branch_0_fun.9 = (f32[18,128]{1,0:T(8,128)}, f32[18,128]{1,0:T(8,128)}) custom-call(f32[18,128]{1,0:T(8,128)S(1)} %get-tuple-element.40.early_lows, f32[18,128]{1,0:T(8,128)S(1)} %get-tuple-element.41.early_highs), custom_call_target="tpu_custom_call" | custom-call | flops 1 | bytes 1 | tf_op jit(solution)/shard_map/cond/branch_1_fun/cond/branch_0_fun/pallas_call | solution.py:432
  22.7 1.3 %collective-permute-start.8 = (f32[18,128]{1,0:T(8,128)}, f32[18,128]{1,0:T(8,128)S(1)}, u32[]{:S(2)}, u32[]{:S(2)}) collective-permute-start(f32[18,128]{1,0:T(8,128)} %get-tuple-element.83), channel_id=1, source_target_pairs={{8,16},{9,17},{10,18},{11,19},{12,20},{13,21},{14,22},{15,23},{16,... | collective-permute-start | bytes 27656 | tf_op jit(solution)/shard_map/ppermute | solution.py:342
  24.0 1.3 %collective-permute-start.9 = (f32[18,128]{1,0:T(8,128)}, f32[18,128]{1,0:T(8,128)S(1)}, u32[]{:S(2)}, u32[]{:S(2)}) collective-permute-start(f32[18,128]{1,0:T(8,128)} %get-tuple-element.84), channel_id=1, source_target_pairs={{16,8},{17,9},{18,10},{19,11},{20,12},{21,13},{22,14},{23,15},{24,... | collective-permute-start | bytes 27656 | tf_op jit(solution)/shard_map/ppermute | solution.py:342
  25.3 0.0 copy-start.1
  25.3 0.0 copy-start.3
  25.3 0.0 copy-start.5
  25.3 3.3 %shard_map.70 = (f32[14,16,128]{2,1,0:T(8,128)S(1)}, f32[14,32,128]{2,1,0:T(8,128)S(1)}, f32[14,32,128]{2,1,0:T(8,128)S(1)}) custom-call(f32[14,32,128]{2,1,0:T(8,128)S(1)} %get-tuple-element.72.block, f32[14,16,128]{2,1,0:T(8,128)} %get-tuple-element.74.early_halo, f32[14,16,128]{2,1,0:T(8,128)} %get-tuple-element.80.late_halo, ...), custom_call_target="tpu_custom_call" | custom-call | flops 1 | bytes 1 | tf_op jit(solution)/shard_map/pallas_call | solution.py:453
  28.7 0.0 collective-permute-done.10.relay
  28.7 0.0 collective-permute-done.8.left
  28.7 1.1 %collective-permute-done.9.right = f32[18,128]{1,0:T(8,128)S(1)} collective-permute-done((f32[18,128]{1,0:T(8,128)}, f32[18,128]{1,0:T(8,128)S(1)}, u32[]{:S(2)}, u32[]{:S(2)}) %collective-permute-start.9) | collective-permute-done | bytes 9248 | tf_op jit(solution)/shard_map/ppermute | solution.py:342
  29.8 0.0 copy-done.1
  29.8 0.0 copy-done.3
  29.8 0.0 copy-done.5
  29.8 4.5 %shard_map.71 = (f32[14,32,128]{2,1,0:T(8,128)}, f32[14,32,128]{2,1,0:T(8,128)}) custom-call(f32[14,32,128]{2,1,0:T(8,128)S(1)} %get-tuple-element.72.block, f32[14,16,128]{2,1,0:T(8,128)S(1)} %get-tuple-element.81.halo, f32[18,128]{1,0:T(8,128)} %get-tuple-element.82.early_pair, f32[18,128]{1,0:T(8,128)S(1)} %collective-permute-done.8.left, ...), custom_call_target="tpu_custom_call" | custom-call | flops 1 | bytes 1 | tf_op jit(solution)/shard_map/pallas_call | solution.py:456
  (5 shorter events, 0.0 us)
Async XLA Ops:
  1.9 19.6 %collective-permute-start.5 = (f32[4,8,128]{2,1,0:T(8,128)S(1)}, f32[4,8,128]{2,1,0:T(8,128)S(1)}, u32[]{:S(2)}, u32[]{:S(2)}) collective-permute-start(f32[4,8,128]{2,1,0:T(8,128)S(1)} %get-tuple-element.76), channel_id=1, source_target_pairs={{88,96},{89,97},{90,98},{91,99},{92,100},{93,101},{94,102},{95,103... | collective-permute-start | bytes 49160 | tf_op jit(solution)/shard_map/ppermute | solution.py:342
  2.6 18.9 %collective-permute-start.6 = (f32[4,8,128]{2,1,0:T(8,128)S(1)}, f32[4,8,128]{2,1,0:T(8,128)S(1)}, u32[]{:S(2)}, u32[]{:S(2)}) collective-permute-start(f32[4,8,128]{2,1,0:T(8,128)S(1)} %get-tuple-element.77), channel_id=1, source_target_pairs={{89,96},{90,97},{91,98},{92,99},{93,100},{94,101},{95,102},{185,19... | collective-permute-start | bytes 49160 | tf_op jit(solution)/shard_map/ppermute | solution.py:342
  3.2 18.2 %collective-permute-start.7 = (f32[3,8,128]{2,1,0:T(8,128)S(1)}, f32[3,8,128]{2,1,0:T(8,128)S(1)}, u32[]{:S(2)}, u32[]{:S(2)}) collective-permute-start(f32[3,8,128]{2,1,0:T(8,128)S(1)} %get-tuple-element.78), channel_id=1, source_target_pairs={{88,97},{89,98},{90,99},{91,100},{92,101},{93,102},{94,103},{184,1... | collective-permute-start | bytes 36872 | tf_op jit(solution)/shard_map/ppermute | solution.py:342
  4.0 7.4 %collective-permute-start.1 = (f32[14,8,128]{2,1,0:T(8,128)S(1)}, f32[14,8,128]{2,1,0:T(8,128)S(1)}, u32[]{:S(2)}, u32[]{:S(2)}) collective-permute-start(f32[14,8,128]{2,1,0:T(8,128)S(1)} %get-tuple-element.30), channel_id=1, source_target_pairs={{1,2},{3,4},{5,6},{9,10},{11,12},{13,14},{97,98},{99,100},{101,102... | collective-permute-start | bytes 172040 | tf_op jit(solution)/shard_map/cond/branch_1_fun/ppermute | solution.py:342
  4.7 6.7 %collective-permute-start = (f32[84,128]{1,0:T(8,128)S(1)}, f32[84,128]{1,0:T(8,128)S(1)}, u32[]{:S(2)}, u32[]{:S(2)}) collective-permute-start(f32[84,128]{1,0:T(8,128)S(1)} %get-tuple-element.29), channel_id=1, source_target_pairs={{0,1},{2,3},{4,5},{6,7},{8,9},{10,11},{12,13},{14,15},{96,97},{98,... | collective-permute-start | bytes 129032 | tf_op jit(solution)/shard_map/cond/branch_1_fun/ppermute | solution.py:342
  12.1 8.7 %collective-permute-start.2 = (f32[18,128]{1,0:T(8,128)S(1)}, f32[18,128]{1,0:T(8,128)}, u32[]{:S(2)}, u32[]{:S(2)}) collective-permute-start(f32[18,128]{1,0:T(8,128)S(1)} %get-tuple-element.32), channel_id=1, source_target_pairs={{0,8},{1,9},{2,10},{3,11},{4,12},{5,13},{6,14},{7,15},{96,104},{97... | collective-permute-start | bytes 27656 | tf_op jit(solution)/shard_map/cond/branch_1_fun/ppermute | solution.py:342
  20.8 7.9 %collective-permute-start.10 = (f32[20,128]{1,0:T(8,128)S(1)}, f32[20,128]{1,0:T(8,128)S(1)}, u32[]{:S(2)}, u32[]{:S(2)}) collective-permute-start(f32[20,128]{1,0:T(8,128)S(1)} %get-tuple-element.85), channel_id=1, source_target_pairs={{96,88},{97,89},{98,90},{99,91},{100,92},{101,93},{102,94},{103,95... | collective-permute-start | bytes 30728 | tf_op jit(solution)/shard_map/ppermute | solution.py:342
  21.5 0.6 %copy-start.4 = (f32[3,8,128]{2,1,0:T(8,128)}, f32[3,8,128]{2,1,0:T(8,128)S(1)}, u32[]{:S(2)}) copy-start(f32[3,8,128]{2,1,0:T(8,128)S(1)} %collective-permute-done.7.c.wrap_down) | copy-start | bytes 36868
  21.5 0.6 %copy-start = (f32[4,8,128]{2,1,0:T(8,128)}, f32[4,8,128]{2,1,0:T(8,128)S(1)}, u32[]{:S(2)}) copy-start(f32[4,8,128]{2,1,0:T(8,128)S(1)} %collective-permute-done.5.a.wrap) | copy-start | bytes 49156
  21.5 0.6 %copy-start.2 = (f32[4,8,128]{2,1,0:T(8,128)}, f32[4,8,128]{2,1,0:T(8,128)S(1)}, u32[]{:S(2)}) copy-start(f32[4,8,128]{2,1,0:T(8,128)S(1)} %collective-permute-done.6.b.wrap_up) | copy-start | bytes 49156
  22.7 5.9 %collective-permute-start.8 = (f32[18,128]{1,0:T(8,128)}, f32[18,128]{1,0:T(8,128)S(1)}, u32[]{:S(2)}, u32[]{:S(2)}) collective-permute-start(f32[18,128]{1,0:T(8,128)} %get-tuple-element.83), channel_id=1, source_target_pairs={{8,16},{9,17},{10,18},{11,19},{12,20},{13,21},{14,22},{15,23},{16,... | collective-permute-start | bytes 27656 | tf_op jit(solution)/shard_map/ppermute | solution.py:342
  24.0 5.8 %collective-permute-start.9 = (f32[18,128]{1,0:T(8,128)}, f32[18,128]{1,0:T(8,128)S(1)}, u32[]{:S(2)}, u32[]{:S(2)}) collective-permute-start(f32[18,128]{1,0:T(8,128)} %get-tuple-element.84), channel_id=1, source_target_pairs={{16,8},{17,9},{18,10},{19,11},{20,12},{21,13},{22,14},{23,15},{24,... | collective-permute-start | bytes 27656 | tf_op jit(solution)/shard_map/ppermute | solution.py:342
  25.3 4.5 %copy-start.1 = (f32[4,8,128]{2,1,0:T(8,128)S(1)}, f32[4,8,128]{2,1,0:T(8,128)}, u32[]{:S(2)}) copy-start(f32[4,8,128]{2,1,0:T(8,128)} %copy-done) | copy-start | bytes 49156
  25.3 4.5 %copy-start.3 = (f32[4,8,128]{2,1,0:T(8,128)S(1)}, f32[4,8,128]{2,1,0:T(8,128)}, u32[]{:S(2)}) copy-start(f32[4,8,128]{2,1,0:T(8,128)} %copy-done.2) | copy-start | bytes 49156
  25.3 4.5 %copy-start.5 = (f32[3,8,128]{2,1,0:T(8,128)S(1)}, f32[3,8,128]{2,1,0:T(8,128)}, u32[]{:S(2)}) copy-start(f32[3,8,128]{2,1,0:T(8,128)} %copy-done.4) | copy-start | bytes 36868

commit v6 on v5

--- a/solution.py
+++ b/solution.py
@@ -211,15 +211,22 @@
     pass
 
 
-def late_main_kernel(block, early_halo, late_halo, table, halo, final, last, w0, wa, wb, coeff, sem):
+def late_main_kernel(block, early_halo, late_halo, early_pair, table, halo, pair, final, last, w0, wa, wb, coeff, sems):
     place = lax.axis_index("blk") % RUN
-    for known, source in ((place <= 1, early_halo), (place > 1, late_halo)):
-
-        @pl.when(known)
-        def _():
-            copy = pltpu.make_async_copy(source, halo, sem)
+
+    @pl.when(place <= 1)
+    def _():
+        copies = [pltpu.make_async_copy(early_halo, halo, sems.at[0]), pltpu.make_async_copy(early_pair, pair, sems.at[1])]
+        for copy in copies:
             copy.start()
+        for copy in copies:
             copy.wait()
+
+    @pl.when(place > 1)
+    def _():
+        copy = pltpu.make_async_copy(late_halo, halo, sems.at[0])
+        copy.start()
+        copy.wait()
 
     @pl.when(place != 0)
     def _():
@@ -227,20 +234,14 @@
 
 
 def last_kernel(
-    block, halo, early_pair, left, right, relay, wrap, wrap_up, wrap_down, table,
-    early_final, early_last, late_final, late_last, final, last, w0, wa, wb, coeff, finals, lasts, pair_rows, in_sems, out_sems,
+    block, halo, pair, left, right, relay, wrap, wrap_up, wrap_down, table,
+    early_final, early_last, late_final, late_last, final, last, w0, wa, wb, coeff, finals, lasts, in_sems, out_sems,
 ):
     wn = lax.axis_index("wn")
     blk = lax.axis_index("blk")
     place = blk % RUN
     mains = [pltpu.make_async_copy(a, b, in_sems.at[i]) for i, (a, b) in enumerate(((early_final, finals), (early_last, lasts)))]
 
-    beside = pltpu.make_async_copy(early_pair, pair_rows, in_sems.at[2])
-
-    @pl.when(place <= 1)
-    def _():
-        beside.start()
-
     @pl.when(place == 0)
     def _():
         for copy in mains:
@@ -248,10 +249,6 @@
 
     lane = iota((ROWS, LANES), 1)
     gather_rows(block, halo, w0)
-
-    @pl.when(place <= 1)
-    def _():
-        beside.wait()
 
     lane3 = iota((3, LANES), 1)
     tiles = []
@@ -261,8 +258,8 @@
             from_wrap = wrap[t, 5:8]
         else:
             from_wrap = jnp.where(lane3 % 16 < 8, wrap_up[t - 4, 5:8], wrap_down[t - 4, 5:8])
-        lo = jnp.where(place == 0, from_wrap, jnp.where(place == 1, pair_rows[three], left[three]))
-        hi = jnp.where(place == RUN - 1, relay[three], jnp.where(place == 0, pair_rows[three], right[three]))
+        lo = jnp.where(place == 0, from_wrap, jnp.where(place == 1, pair[three], left[three]))
+        hi = jnp.where(place == RUN - 1, relay[three], jnp.where(place == 0, pair[three], right[three]))
         full = jnp.concatenate([hi, jnp.zeros((10, LANES), jnp.float32), lo, jnp.zeros((112, LANES), jnp.float32)], axis=0)
         tiles.append(full.T)
     for v in range(14):
@@ -442,7 +439,7 @@
     lows = pl.pallas_call(
         join_kernel,
         out_shape=strips,
-        in_specs=[ANY] * 4,
+        in_specs=[ANY] + [VMEM] * 3,
         out_specs=ANY,
         input_output_aliases={0: 0},
         cost_estimate=pl.CostEstimate(flops=1, bytes_accessed=1, transcendentals=0),
@@ -450,21 +447,24 @@
     halo, lows, highs = lax.cond(place > 0, late, not_late, block, lows, highs)
     left = send(highs, FORWARD)
     right = send(lows, BACKWARD)
-    halo, late_final, late_last = call(
-        late_main_kernel, (halo_shape, out, out), [VMEM, HBM, HBM, VMEM], SCRATCH + [pltpu.SemaphoreType.DMA]
-    )(block, in_hbm(early_halo), in_hbm(halo), table)
+    halo, pair, late_final, late_last = call(
+        late_main_kernel,
+        (halo_shape, strips, out, out),
+        [VMEM] + [HBM] * 3 + [VMEM],
+        SCRATCH + [pltpu.SemaphoreType.DMA((2,))],
+    )(block, in_hbm(early_halo), in_hbm(halo), in_hbm(early_pair), table)
     final, last = pl.pallas_call(
         last_kernel,
         out_shape=(out, out),
-        in_specs=[VMEM] * 2 + [HBM] + [VMEM] * 7 + [HBM] * 2 + [VMEM] * 2,
+        in_specs=[VMEM] * 10 + [HBM] * 2 + [VMEM] * 2,
         out_specs=(HBM, HBM),
         scratch_shapes=SCRATCH
         + [pltpu.VMEM((14, OWN, LANES), jnp.float32)] * 2
-        + [pltpu.VMEM((18, LANES), jnp.float32), pltpu.SemaphoreType.DMA((3,)), pltpu.SemaphoreType.DMA((2, 14))],
+        + [pltpu.SemaphoreType.DMA((2,)), pltpu.SemaphoreType.DMA((2, 14))],
         compiler_params=PARAMS,
         cost_estimate=pl.CostEstimate(flops=1, bytes_accessed=1, transcendentals=0),
     )(
-        block, halo, in_hbm(early_pair), left, right, relay, wrap, wrap_up, wrap_down, table,
+        block, halo, pair, left, right, relay, wrap, wrap_up, wrap_down, table,
         in_hbm(early_final), in_hbm(early_last), late_final, late_last,
     )
     return final.reshape(14, 16, 2, LANES), last.reshape(14, 16, 2, LANES)

time: 34.7 us -> 34.8 us (level)
  transfers between devices with their start and end apart: 9 -> 9, of which waited for: 3 -> 3; matrix products, arithmetic and copies ran while one was open for 0% -> 0% of each run, Pallas kernels for 13% -> 16%
where the time goes in v6:
time: 34.8 us; the launch traced here: 34.4 us
  starting transfers between devices  18.7 us (54%)
  Pallas kernels  10.5 us (30%)
  waiting for transfers between devices  3.73 us (11%)
  between operations  0.82 us (2%)
  local copies, waits for them, and re-layouts  0.61 us (2%)
    ppermute x9, starting transfers between devices, send(): return lax.ppermute(x, ('blk', 'wn'), pairs)  18.7 us
    pallas_call x1, Pallas kernels, local(): pl.pallas_call(last_kernel, out_shape=(out, out), in_specs=[VMEM] * 10 +...  3.84 us
    ppermute x9, waiting for transfers between devices, send(): return lax.ppermute(x, ('blk', 'wn'), pairs)  3.73 us
    pallas_call x1, Pallas kernels, local(): call(late_main_kernel, (halo_shape, strips, out, out), [VMEM] + [HBM] * 3...  3.31 us
    pallas_call x1, Pallas kernels, local(): call(load_kernel, (out, f32(4, 8, LANES), f32(4, 8, LANES), f32(3, 8, LAN...  1.26 us
    pallas_call x1, Pallas kernels, local(): pl.pallas_call(join_kernel, out_shape=strips, in_specs=[ANY] + [VMEM] * 3...  0.74 us
  transfers between devices with their start and end apart: 9, of which 3 were waited for; matrix products, arithmetic and copies ran while one was open for 0% of the time, Pallas kernels for 16%

profile of v6, /device:TPU:64, one launch (start us, length us, event | category | flops | bytes accessed | tf_op | source)
XLA Modules:
  0.0 34.4 jit_solution(1483709710318492002)
XLA Ops:
  0.6 1.3 %shard_map.68 = (f32[14,32,128]{2,1,0:T(8,128)S(1)}, f32[4,8,128]{2,1,0:T(8,128)S(1)}, f32[4,8,128]{2,1,0:T(8,128)S(1)}, f32[3,8,128]{2,1,0:T(8,128)S(1)}, f32[248,128]{1,0:T(8,128)S(1)}) custom-call(f32[11,32,128]{2,1,0:T(8,128)} %bitcast.5, f32[2,32,128]{2,1,0:T(8,128)} %bitcast.6, f32[1,32,128]{2,1,0:T(8,128)} %bitcast.7, f32[11,11]{1,0:T(8,128)} %shear.1, ...), custom_call_target="tpu_custom_call" | custom-call | flops 1 | bytes 1 | tf_op jit(solution)/shard_map/pallas_call | solution.py:386
  1.9 0.7 %collective-permute-start.5 = (f32[4,8,128]{2,1,0:T(8,128)S(1)}, f32[4,8,128]{2,1,0:T(8,128)S(1)}, u32[]{:S(2)}, u32[]{:S(2)}) collective-permute-start(f32[4,8,128]{2,1,0:T(8,128)S(1)} %get-tuple-element.77), channel_id=1, source_target_pairs={{88,96},{89,97},{90,98},{91,99},{92,100},{93,101},{94,102},{95,103... | collective-permute-start | bytes 49160 | tf_op jit(solution)/shard_map/ppermute | solution.py:339
  2.6 0.7 %collective-permute-start.6 = (f32[4,8,128]{2,1,0:T(8,128)S(1)}, f32[4,8,128]{2,1,0:T(8,128)S(1)}, u32[]{:S(2)}, u32[]{:S(2)}) collective-permute-start(f32[4,8,128]{2,1,0:T(8,128)S(1)} %get-tuple-element.78), channel_id=1, source_target_pairs={{89,96},{90,97},{91,98},{92,99},{93,100},{94,101},{95,102},{185,19... | collective-permute-start | bytes 49160 | tf_op jit(solution)/shard_map/ppermute | solution.py:339
  3.2 0.7 %collective-permute-start.7 = (f32[3,8,128]{2,1,0:T(8,128)S(1)}, f32[3,8,128]{2,1,0:T(8,128)S(1)}, u32[]{:S(2)}, u32[]{:S(2)}) collective-permute-start(f32[3,8,128]{2,1,0:T(8,128)S(1)} %get-tuple-element.79), channel_id=1, source_target_pairs={{88,97},{89,98},{90,99},{91,100},{92,101},{93,102},{94,103},{184,1... | collective-permute-start | bytes 36872 | tf_op jit(solution)/shard_map/ppermute | solution.py:339
  3.9 16.9 %conditional.4 = ((f32[14,16,128]{2,1,0:T(8,128)}, f32[18,128]{1,0:T(8,128)}, f32[18,128]{1,0:T(8,128)S(1)}, f32[18,128]{1,0:T(8,128)S(1)}, f32[20,128]{1,0:T(8,...) conditional(s32[]{:T(128)} %convert_element_type.12, () %tuple.34, (f32[14,32,128]{2,1,0:T(8,128)S(1)}, ...), branch_computations={%region_0.1_spmd, %region_1.4_spmd} | conditional | flops 5 | bytes 438505 | solution.py:437
  4.0 0.7 %collective-permute-start.1 = (f32[14,8,128]{2,1,0:T(8,128)S(1)}, f32[14,8,128]{2,1,0:T(8,128)S(1)}, u32[]{:S(2)}, u32[]{:S(2)}) collective-permute-start(f32[14,8,128]{2,1,0:T(8,128)S(1)} %get-tuple-element.30), channel_id=1, source_target_pairs={{1,2},{3,4},{5,6},{9,10},{11,12},{13,14},{97,98},{99,100},{101,102... | collective-permute-start | bytes 172040 | tf_op jit(solution)/shard_map/cond/branch_1_fun/ppermute | solution.py:339
  4.7 5.9 %collective-permute-start = (f32[84,128]{1,0:T(8,128)S(1)}, f32[84,128]{1,0:T(8,128)S(1)}, u32[]{:S(2)}, u32[]{:S(2)}) collective-permute-start(f32[84,128]{1,0:T(8,128)S(1)} %get-tuple-element.29), channel_id=1, source_target_pairs={{0,1},{2,3},{4,5},{6,7},{8,9},{10,11},{12,13},{14,15},{96,97},{98,... | collective-permute-start | bytes 129032 | tf_op jit(solution)/shard_map/cond/branch_1_fun/ppermute | solution.py:339
  10.5 0.9 %collective-permute-done.first = f32[84,128]{1,0:T(8,128)S(1)} collective-permute-done((f32[84,128]{1,0:T(8,128)S(1)}, f32[84,128]{1,0:T(8,128)S(1)}, u32[]{:S(2)}, u32[]{:S(2)}) %collective-permute-start) | collective-permute-done | bytes 43040 | tf_op jit(solution)/shard_map/cond/branch_1_fun/ppermute | solution.py:339
  11.4 0.0 collective-permute-done.1.second
  11.4 0.7 %branch_1_fun.7 = (f32[14,16,128]{2,1,0:T(8,128)}, f32[18,128]{1,0:T(8,128)S(1)}, f32[18,128]{1,0:T(8,128)S(1)}, f32[18,128]{1,0:T(8,128)S(1)}, f32[20,128]{1,0:T(8,128)S(1)}) custom-call(f32[84,128]{1,0:T(8,128)S(1)} %collective-permute-done.first, f32[14,8,128]{2,1,0:T(8,128)S(1)} %collective-permute-done.1.second, f32[14,32,128]{2,1,0:T(8,128)S(1)} %get-tuple-element.28.block), custom_call_target="tpu_custom_call" | custom-call | flops 1 | bytes 1 | tf_op jit(solution)/shard_map/cond/branch_1_fun/pallas_call | solution.py:408
  12.1 7.0 %collective-permute-start.2 = (f32[18,128]{1,0:T(8,128)S(1)}, f32[18,128]{1,0:T(8,128)}, u32[]{:S(2)}, u32[]{:S(2)}) collective-permute-start(f32[18,128]{1,0:T(8,128)S(1)} %get-tuple-element.32), channel_id=1, source_target_pairs={{0,8},{1,9},{2,10},{3,11},{4,12},{5,13},{6,14},{7,15},{96,104},{97... | collective-permute-start | bytes 27656 | tf_op jit(solution)/shard_map/cond/branch_1_fun/ppermute | solution.py:339
  19.1 1.7 %collective-permute-done.2 = f32[18,128]{1,0:T(8,128)} collective-permute-done((f32[18,128]{1,0:T(8,128)S(1)}, f32[18,128]{1,0:T(8,128)}, u32[]{:S(2)}, u32[]{:S(2)}) %collective-permute-start.2) | collective-permute-done | bytes 9248 | tf_op jit(solution)/shard_map/cond/branch_1_fun/ppermute | solution.py:339
  20.8 0.7 %collective-permute-start.10 = (f32[20,128]{1,0:T(8,128)S(1)}, f32[20,128]{1,0:T(8,128)S(1)}, u32[]{:S(2)}, u32[]{:S(2)}) collective-permute-start(f32[20,128]{1,0:T(8,128)S(1)} %get-tuple-element.87), channel_id=1, source_target_pairs={{96,88},{97,89},{98,90},{99,91},{100,92},{101,93},{102,94},{103,95... | collective-permute-start | bytes 30728 | tf_op jit(solution)/shard_map/ppermute | solution.py:339
  21.5 0.0 collective-permute-done.7.c.wrap_down
  21.5 0.0 copy-start.4
  21.5 0.0 collective-permute-done.5.a.wrap
  21.5 0.0 copy-start
  21.5 0.0 collective-permute-done.6.b.wrap_up
  21.5 0.0 copy-start.2
  21.5 0.5 %copy-done.4 = f32[3,8,128]{2,1,0:T(8,128)} copy-done((f32[3,8,128]{2,1,0:T(8,128)}, f32[3,8,128]{2,1,0:T(8,128)S(1)}, u32[]{:S(2)}) %copy-start.4) | copy-done | bytes 12312
  22.1 0.0 copy-done
  22.1 0.0 copy-done.2
  22.1 0.7 %shard_map.69 = f32[18,128]{1,0:T(8,128)S(1)} custom-call(f32[18,128]{1,0:T(8,128)S(1)} %get-tuple-element.76.value, f32[4,8,128]{2,1,0:T(8,128)} %copy-done, f32[4,8,128]{2,1,0:T(8,128)} %copy-done.2, f32[3,8,128]{2,1,0:T(8,128)} %copy-done.4), custom_call_target="tpu_custom_call", output_to_operand_aliasing={{}: (0, {})} | custom-call | flops 1 | bytes 1 | tf_op jit(solution)/shard_map/pallas_call | solution.py:439
  22.9 0.6 %conditional.5 = ((f32[14,16,128]{2,1,0:T(8,128)}, f32[18,128]{1,0:T(8,128)}, f32[18,128]{1,0:T(8,128)})) conditional(s32[]{:T(128)} %convert_element_type.13, () %tuple.36, (s32[]{:T(128)}, f32[18,128]{1,0:T(8,128)S(1)}, f32[18,128]{1,0:T(8,128)S(1)}, f32[14,32,128]{2,1,0:T(8,128)S(1)}) %tuple.37), branch_computations={%region_4.5_spmd, %region_5.8_spmd} | conditional | flops 4 | bytes 401528 | solution.py:447
  22.9 0.6 %conditional.1 = ((f32[14,16,128]{2,1,0:T(8,128)}, f32[18,128]{1,0:T(8,128)}, f32[18,128]{1,0:T(8,128)})) conditional(s32[]{:T(128)} %convert_element_type.9, (f32[18,128]{1,0:T(8,128)S(1)}, f32[18,128]{1,0:T(8,128)S(1)}) %tuple.27, f32[14,32,128]{2,1,0:T(8,128)S(1)} %get-tuple-element.49), branch_computations={%region_6.6_spmd, %region_7.7_spmd} | conditional | flops 2 | bytes 401498 | solution.py:432
  22.9 0.6 %branch_0_fun.9 = (f32[18,128]{1,0:T(8,128)}, f32[18,128]{1,0:T(8,128)}) custom-call(f32[18,128]{1,0:T(8,128)S(1)} %get-tuple-element.40.early_lows, f32[18,128]{1,0:T(8,128)S(1)} %get-tuple-element.41.early_highs), custom_call_target="tpu_custom_call" | custom-call | flops 1 | bytes 1 | tf_op jit(solution)/shard_map/cond/branch_1_fun/cond/branch_0_fun/pallas_call | solution.py:429
  23.5 1.3 %collective-permute-start.8 = (f32[18,128]{1,0:T(8,128)}, f32[18,128]{1,0:T(8,128)S(1)}, u32[]{:S(2)}, u32[]{:S(2)}) collective-permute-start(f32[18,128]{1,0:T(8,128)} %get-tuple-element.85), channel_id=1, source_target_pairs={{8,16},{9,17},{10,18},{11,19},{12,20},{13,21},{14,22},{15,23},{16,... | collective-permute-start | bytes 27656 | tf_op jit(solution)/shard_map/ppermute | solution.py:339
  24.8 1.3 %collective-permute-start.9 = (f32[18,128]{1,0:T(8,128)}, f32[18,128]{1,0:T(8,128)S(1)}, u32[]{:S(2)}, u32[]{:S(2)}) collective-permute-start(f32[18,128]{1,0:T(8,128)} %get-tuple-element.86), channel_id=1, source_target_pairs={{16,8},{17,9},{18,10},{19,11},{20,12},{21,13},{22,14},{23,15},{24,... | collective-permute-start | bytes 27656 | tf_op jit(solution)/shard_map/ppermute | solution.py:339
  26.1 0.0 copy-start.1
  26.1 0.0 copy-start.3
  26.1 0.0 copy-start.5
  26.1 3.3 %shard_map.70 = (f32[14,16,128]{2,1,0:T(8,128)S(1)}, f32[18,128]{1,0:T(8,128)S(1)}, f32[14,32,128]{2,1,0:T(8,128)S(1)}, f32[14,32,128]{2,1,0:T(8,128)S(1)}) custom-call(f32[14,32,128]{2,1,0:T(8,128)S(1)} %get-tuple-element.73.block, f32[14,16,128]{2,1,0:T(8,128)} %get-tuple-element.75.early_halo, f32[14,16,128]{2,1,0:T(8,128)} %get-tuple-element.81.late_halo, ...), custom_call_target="tpu_custom_call" | custom-call | flops 1 | bytes 1 | tf_op jit(solution)/shard_map/pallas_call | solution.py:450
  29.4 0.0 collective-permute-done.10.relay
  29.4 0.0 collective-permute-done.8.left
  29.4 1.1 %collective-permute-done.9.right = f32[18,128]{1,0:T(8,128)S(1)} collective-permute-done((f32[18,128]{1,0:T(8,128)}, f32[18,128]{1,0:T(8,128)S(1)}, u32[]{:S(2)}, u32[]{:S(2)}) %collective-permute-start.9) | collective-permute-done | bytes 9248 | tf_op jit(solution)/shard_map/ppermute | solution.py:339
  30.6 0.0 copy-done.1
  30.6 0.0 copy-done.3
  30.6 0.0 copy-done.5
  30.6 3.8 %shard_map.71 = (f32[14,32,128]{2,1,0:T(8,128)}, f32[14,32,128]{2,1,0:T(8,128)}) custom-call(f32[14,32,128]{2,1,0:T(8,128)S(1)} %get-tuple-element.73.block, f32[14,16,128]{2,1,0:T(8,128)S(1)} %get-tuple-element.83.halo, f32[18,128]{1,0:T(8,128)S(1)} %get-tuple-element.84.pair, f32[18,128]{1,0:T(8,128)S(1)} %collective-permute-done.8.left, ...), custom_call_target="tpu_custom_call" | custom-call | flops 1 | bytes 1 | tf_op jit(solution)/shard_map/pallas_call | solution.py:456
  (4 shorter events, 0.0 us)
Async XLA Ops:
  1.9 19.6 %collective-permute-start.5 = (f32[4,8,128]{2,1,0:T(8,128)S(1)}, f32[4,8,128]{2,1,0:T(8,128)S(1)}, u32[]{:S(2)}, u32[]{:S(2)}) collective-permute-start(f32[4,8,128]{2,1,0:T(8,128)S(1)} %get-tuple-element.77), channel_id=1, source_target_pairs={{88,96},{89,97},{90,98},{91,99},{92,100},{93,101},{94,102},{95,103... | collective-permute-start | bytes 49160 | tf_op jit(solution)/shard_map/ppermute | solution.py:339
  2.6 18.9 %collective-permute-start.6 = (f32[4,8,128]{2,1,0:T(8,128)S(1)}, f32[4,8,128]{2,1,0:T(8,128)S(1)}, u32[]{:S(2)}, u32[]{:S(2)}) collective-permute-start(f32[4,8,128]{2,1,0:T(8,128)S(1)} %get-tuple-element.78), channel_id=1, source_target_pairs={{89,96},{90,97},{91,98},{92,99},{93,100},{94,101},{95,102},{185,19... | collective-permute-start | bytes 49160 | tf_op jit(solution)/shard_map/ppermute | solution.py:339
  3.2 18.2 %collective-permute-start.7 = (f32[3,8,128]{2,1,0:T(8,128)S(1)}, f32[3,8,128]{2,1,0:T(8,128)S(1)}, u32[]{:S(2)}, u32[]{:S(2)}) collective-permute-start(f32[3,8,128]{2,1,0:T(8,128)S(1)} %get-tuple-element.79), channel_id=1, source_target_pairs={{88,97},{89,98},{90,99},{91,100},{92,101},{93,102},{94,103},{184,1... | collective-permute-start | bytes 36872 | tf_op jit(solution)/shard_map/ppermute | solution.py:339
  4.0 7.4 %collective-permute-start.1 = (f32[14,8,128]{2,1,0:T(8,128)S(1)}, f32[14,8,128]{2,1,0:T(8,128)S(1)}, u32[]{:S(2)}, u32[]{:S(2)}) collective-permute-start(f32[14,8,128]{2,1,0:T(8,128)S(1)} %get-tuple-element.30), channel_id=1, source_target_pairs={{1,2},{3,4},{5,6},{9,10},{11,12},{13,14},{97,98},{99,100},{101,102... | collective-permute-start | bytes 172040 | tf_op jit(solution)/shard_map/cond/branch_1_fun/ppermute | solution.py:339
  4.7 6.7 %collective-permute-start = (f32[84,128]{1,0:T(8,128)S(1)}, f32[84,128]{1,0:T(8,128)S(1)}, u32[]{:S(2)}, u32[]{:S(2)}) collective-permute-start(f32[84,128]{1,0:T(8,128)S(1)} %get-tuple-element.29), channel_id=1, source_target_pairs={{0,1},{2,3},{4,5},{6,7},{8,9},{10,11},{12,13},{14,15},{96,97},{98,... | collective-permute-start | bytes 129032 | tf_op jit(solution)/shard_map/cond/branch_1_fun/ppermute | solution.py:339
  12.1 8.7 %collective-permute-start.2 = (f32[18,128]{1,0:T(8,128)S(1)}, f32[18,128]{1,0:T(8,128)}, u32[]{:S(2)}, u32[]{:S(2)}) collective-permute-start(f32[18,128]{1,0:T(8,128)S(1)} %get-tuple-element.32), channel_id=1, source_target_pairs={{0,8},{1,9},{2,10},{3,11},{4,12},{5,13},{6,14},{7,15},{96,104},{97... | collective-permute-start | bytes 27656 | tf_op jit(solution)/shard_map/cond/branch_1_fun/ppermute | solution.py:339
  20.8 8.6 %collective-permute-start.10 = (f32[20,128]{1,0:T(8,128)S(1)}, f32[20,128]{1,0:T(8,128)S(1)}, u32[]{:S(2)}, u32[]{:S(2)}) collective-permute-start(f32[20,128]{1,0:T(8,128)S(1)} %get-tuple-element.87), channel_id=1, source_target_pairs={{96,88},{97,89},{98,90},{99,91},{100,92},{101,93},{102,94},{103,95... | collective-permute-start | bytes 30728 | tf_op jit(solution)/shard_map/ppermute | solution.py:339
  21.5 0.6 %copy-start.4 = (f32[3,8,128]{2,1,0:T(8,128)}, f32[3,8,128]{2,1,0:T(8,128)S(1)}, u32[]{:S(2)}) copy-start(f32[3,8,128]{2,1,0:T(8,128)S(1)} %collective-permute-done.7.c.wrap_down) | copy-start | bytes 36868
  21.5 0.6 %copy-start = (f32[4,8,128]{2,1,0:T(8,128)}, f32[4,8,128]{2,1,0:T(8,128)S(1)}, u32[]{:S(2)}) copy-start(f32[4,8,128]{2,1,0:T(8,128)S(1)} %collective-permute-done.5.a.wrap) | copy-start | bytes 49156
  21.5 0.6 %copy-start.2 = (f32[4,8,128]{2,1,0:T(8,128)}, f32[4,8,128]{2,1,0:T(8,128)S(1)}, u32[]{:S(2)}) copy-start(f32[4,8,128]{2,1,0:T(8,128)S(1)} %collective-permute-done.6.b.wrap_up) | copy-start | bytes 49156
  23.5 5.9 %collective-permute-start.8 = (f32[18,128]{1,0:T(8,128)}, f32[18,128]{1,0:T(8,128)S(1)}, u32[]{:S(2)}, u32[]{:S(2)}) collective-permute-start(f32[18,128]{1,0:T(8,128)} %get-tuple-element.85), channel_id=1, source_target_pairs={{8,16},{9,17},{10,18},{11,19},{12,20},{13,21},{14,22},{15,23},{16,... | collective-permute-start | bytes 27656 | tf_op jit(solution)/shard_map/ppermute | solution.py:339
  24.8 5.8 %collective-permute-start.9 = (f32[18,128]{1,0:T(8,128)}, f32[18,128]{1,0:T(8,128)S(1)}, u32[]{:S(2)}, u32[]{:S(2)}) collective-permute-start(f32[18,128]{1,0:T(8,128)} %get-tuple-element.86), channel_id=1, source_target_pairs={{16,8},{17,9},{18,10},{19,11},{20,12},{21,13},{22,14},{23,15},{24,... | collective-permute-start | bytes 27656 | tf_op jit(solution)/shard_map/ppermute | solution.py:339
  26.1 4.5 %copy-start.1 = (f32[4,8,128]{2,1,0:T(8,128)S(1)}, f32[4,8,128]{2,1,0:T(8,128)}, u32[]{:S(2)}) copy-start(f32[4,8,128]{2,1,0:T(8,128)} %copy-done) | copy-start | bytes 49156
  26.1 4.5 %copy-start.3 = (f32[4,8,128]{2,1,0:T(8,128)S(1)}, f32[4,8,128]{2,1,0:T(8,128)}, u32[]{:S(2)}) copy-start(f32[4,8,128]{2,1,0:T(8,128)} %copy-done.2) | copy-start | bytes 49156
  26.1 4.5 %copy-start.5 = (f32[3,8,128]{2,1,0:T(8,128)S(1)}, f32[3,8,128]{2,1,0:T(8,128)}, u32[]{:S(2)}) copy-start(f32[3,8,128]{2,1,0:T(8,128)} %copy-done.4) | copy-start | bytes 36868

commit v7 on v6

--- a/solution.py
+++ b/solution.py
@@ -439,11 +439,11 @@
     lows = pl.pallas_call(
         join_kernel,
         out_shape=strips,
-        in_specs=[ANY] + [VMEM] * 3,
+        in_specs=[ANY] * 4,
         out_specs=ANY,
         input_output_aliases={0: 0},
         cost_estimate=pl.CostEstimate(flops=1, bytes_accessed=1, transcendentals=0),
-    )(lows, wrap, wrap_up, wrap_down)
+    )(lows, *(pltpu.with_memory_space_constraint(x, pltpu.VMEM) for x in (wrap, wrap_up, wrap_down)))
     halo, lows, highs = lax.cond(place > 0, late, not_late, block, lows, highs)
     left = send(highs, FORWARD)
     right = send(lows, BACKWARD)

time: 34.8 us -> 33.4 us (0.960)
  Pallas kernels: 10.5 us -> 9.71 us
  local copies, waits for them, and re-layouts: 0.61 us -> 0 us
    pallas_call x1, Pallas kernels: 0.74 us -> 0.01 us  [local(): pl.pallas_call(join_kernel, out_shape=strips, in_specs=[ANY] * 4, out_spe...]
    unnamed x12 -> x0, local copies, waits for them, and re-layouts: 0.61 us -> none
  transfers between devices with their start and end apart: 9 -> 9, of which waited for: 3 -> 3; matrix products, arithmetic and copies ran while one was open for 0% -> 0% of each run, Pallas kernels for 16% -> 14%
where the time goes in v7:
time: 33.4 us; the launch traced here: 33.1 us
  starting transfers between devices  18.7 us (56%)
  Pallas kernels  9.71 us (29%)
  waiting for transfers between devices  3.75 us (11%)
  between operations  0.78 us (2%)
    ppermute x9, starting transfers between devices, send(): return lax.ppermute(x, ('blk', 'wn'), pairs)  18.7 us
    pallas_call x1, Pallas kernels, local(): pl.pallas_call(last_kernel, out_shape=(out, out), in_specs=[VMEM] * 10 +...  3.8 us
    ppermute x9, waiting for transfers between devices, send(): return lax.ppermute(x, ('blk', 'wn'), pairs)  3.75 us
    pallas_call x1, Pallas kernels, local(): call(late_main_kernel, (halo_shape, strips, out, out), [VMEM] + [HBM] * 3...  3.32 us
    pallas_call x1, Pallas kernels, local(): call(load_kernel, (out, f32(4, 8, LANES), f32(4, 8, LANES), f32(3, 8, LAN...  1.26 us
    pallas_call x1, Pallas kernels, early(): call(early_columns_kernel, (halo_shape, strips, strips, strips, offered),...  0.68 us
  transfers between devices with their start and end apart: 9, of which 3 were waited for; matrix products, arithmetic and copies ran while one was open for 0% of the time, Pallas kernels for 14%

profile of v7, /device:TPU:64, one launch (start us, length us, event | category | flops | bytes accessed | tf_op | source)
XLA Modules:
  0.0 33.1 jit_solution(18377529091993734633)
XLA Ops:
  0.6 1.3 %shard_map.68 = (f32[14,32,128]{2,1,0:T(8,128)S(1)}, f32[4,8,128]{2,1,0:T(8,128)S(1)}, f32[4,8,128]{2,1,0:T(8,128)S(1)}, f32[3,8,128]{2,1,0:T(8,128)S(1)}, f32[248,128]{1,0:T(8,128)S(1)}) custom-call(f32[11,32,128]{2,1,0:T(8,128)} %bitcast.5, f32[2,32,128]{2,1,0:T(8,128)} %bitcast.6, f32[1,32,128]{2,1,0:T(8,128)} %bitcast.7, f32[11,11]{1,0:T(8,128)} %shear.1, ...), custom_call_target="tpu_custom_call" | custom-call | flops 1 | bytes 1 | tf_op jit(solution)/shard_map/pallas_call | solution.py:386
  1.9 0.7 %collective-permute-start.5 = (f32[4,8,128]{2,1,0:T(8,128)S(1)}, f32[4,8,128]{2,1,0:T(8,128)S(1)}, u32[]{:S(2)}, u32[]{:S(2)}) collective-permute-start(f32[4,8,128]{2,1,0:T(8,128)S(1)} %get-tuple-element.77), channel_id=1, source_target_pairs={{88,96},{89,97},{90,98},{91,99},{92,100},{93,101},{94,102},{95,103... | collective-permute-start | bytes 49160 | tf_op jit(solution)/shard_map/ppermute | solution.py:339
  2.6 0.7 %collective-permute-start.6 = (f32[4,8,128]{2,1,0:T(8,128)S(1)}, f32[4,8,128]{2,1,0:T(8,128)S(1)}, u32[]{:S(2)}, u32[]{:S(2)}) collective-permute-start(f32[4,8,128]{2,1,0:T(8,128)S(1)} %get-tuple-element.78), channel_id=1, source_target_pairs={{89,96},{90,97},{91,98},{92,99},{93,100},{94,101},{95,102},{185,19... | collective-permute-start | bytes 49160 | tf_op jit(solution)/shard_map/ppermute | solution.py:339
  3.2 0.7 %collective-permute-start.7 = (f32[3,8,128]{2,1,0:T(8,128)S(1)}, f32[3,8,128]{2,1,0:T(8,128)S(1)}, u32[]{:S(2)}, u32[]{:S(2)}) collective-permute-start(f32[3,8,128]{2,1,0:T(8,128)S(1)} %get-tuple-element.79), channel_id=1, source_target_pairs={{88,97},{89,98},{90,99},{91,100},{92,101},{93,102},{94,103},{184,1... | collective-permute-start | bytes 36872 | tf_op jit(solution)/shard_map/ppermute | solution.py:339
  3.9 16.9 %conditional.4 = ((f32[14,16,128]{2,1,0:T(8,128)}, f32[18,128]{1,0:T(8,128)}, f32[18,128]{1,0:T(8,128)S(1)}, f32[18,128]{1,0:T(8,128)S(1)}, f32[20,128]{1,0:T(8,...) conditional(s32[]{:T(128)} %convert_element_type.12, () %tuple.34, (f32[14,32,128]{2,1,0:T(8,128)S(1)}, ...), branch_computations={%region_0.1_spmd, %region_1.4_spmd} | conditional | flops 5 | bytes 438505 | solution.py:437
  4.0 0.7 %collective-permute-start.1 = (f32[14,8,128]{2,1,0:T(8,128)S(1)}, f32[14,8,128]{2,1,0:T(8,128)S(1)}, u32[]{:S(2)}, u32[]{:S(2)}) collective-permute-start(f32[14,8,128]{2,1,0:T(8,128)S(1)} %get-tuple-element.30), channel_id=1, source_target_pairs={{1,2},{3,4},{5,6},{9,10},{11,12},{13,14},{97,98},{99,100},{101,102... | collective-permute-start | bytes 172040 | tf_op jit(solution)/shard_map/cond/branch_1_fun/ppermute | solution.py:339
  4.7 5.9 %collective-permute-start = (f32[84,128]{1,0:T(8,128)S(1)}, f32[84,128]{1,0:T(8,128)S(1)}, u32[]{:S(2)}, u32[]{:S(2)}) collective-permute-start(f32[84,128]{1,0:T(8,128)S(1)} %get-tuple-element.29), channel_id=1, source_target_pairs={{0,1},{2,3},{4,5},{6,7},{8,9},{10,11},{12,13},{14,15},{96,97},{98,... | collective-permute-start | bytes 129032 | tf_op jit(solution)/shard_map/cond/branch_1_fun/ppermute | solution.py:339
  10.5 0.9 %collective-permute-done.first = f32[84,128]{1,0:T(8,128)S(1)} collective-permute-done((f32[84,128]{1,0:T(8,128)S(1)}, f32[84,128]{1,0:T(8,128)S(1)}, u32[]{:S(2)}, u32[]{:S(2)}) %collective-permute-start) | collective-permute-done | bytes 43040 | tf_op jit(solution)/shard_map/cond/branch_1_fun/ppermute | solution.py:339
  11.4 0.0 collective-permute-done.1.second
  11.4 0.7 %branch_1_fun.7 = (f32[14,16,128]{2,1,0:T(8,128)}, f32[18,128]{1,0:T(8,128)S(1)}, f32[18,128]{1,0:T(8,128)S(1)}, f32[18,128]{1,0:T(8,128)S(1)}, f32[20,128]{1,0:T(8,128)S(1)}) custom-call(f32[84,128]{1,0:T(8,128)S(1)} %collective-permute-done.first, f32[14,8,128]{2,1,0:T(8,128)S(1)} %collective-permute-done.1.second, f32[14,32,128]{2,1,0:T(8,128)S(1)} %get-tuple-element.28.block), custom_call_target="tpu_custom_call" | custom-call | flops 1 | bytes 1 | tf_op jit(solution)/shard_map/cond/branch_1_fun/pallas_call | solution.py:408
  12.1 7.0 %collective-permute-start.2 = (f32[18,128]{1,0:T(8,128)S(1)}, f32[18,128]{1,0:T(8,128)}, u32[]{:S(2)}, u32[]{:S(2)}) collective-permute-start(f32[18,128]{1,0:T(8,128)S(1)} %get-tuple-element.32), channel_id=1, source_target_pairs={{0,8},{1,9},{2,10},{3,11},{4,12},{5,13},{6,14},{7,15},{96,104},{97... | collective-permute-start | bytes 27656 | tf_op jit(solution)/shard_map/cond/branch_1_fun/ppermute | solution.py:339
  19.1 1.7 %collective-permute-done.2 = f32[18,128]{1,0:T(8,128)} collective-permute-done((f32[18,128]{1,0:T(8,128)S(1)}, f32[18,128]{1,0:T(8,128)}, u32[]{:S(2)}, u32[]{:S(2)}) %collective-permute-start.2) | collective-permute-done | bytes 9248 | tf_op jit(solution)/shard_map/cond/branch_1_fun/ppermute | solution.py:339
  20.8 0.7 %collective-permute-start.10 = (f32[20,128]{1,0:T(8,128)S(1)}, f32[20,128]{1,0:T(8,128)S(1)}, u32[]{:S(2)}, u32[]{:S(2)}) collective-permute-start(f32[20,128]{1,0:T(8,128)S(1)} %get-tuple-element.87), channel_id=1, source_target_pairs={{96,88},{97,89},{98,90},{99,91},{100,92},{101,93},{102,94},{103,95... | collective-permute-start | bytes 30728 | tf_op jit(solution)/shard_map/ppermute | solution.py:339
  21.5 0.0 collective-permute-done.7.c.wrap_down
  21.5 0.0 collective-permute-done.5.a.wrap
  21.5 0.0 collective-permute-done.6.b.wrap_up
  21.5 0.7 %conditional.5 = ((f32[14,16,128]{2,1,0:T(8,128)}, f32[18,128]{1,0:T(8,128)}, f32[18,128]{1,0:T(8,128)})) conditional(s32[]{:T(128)} %convert_element_type.13, () %tuple.36, (s32[]{:T(128)}, f32[18,128]{1,0:T(8,128)S(1)}, f32[18,128]{1,0:T(8,128)S(1)}, f32[14,32,128]{2,1,0:T(8,128)S(1)}) %tuple.37), branch_computations={%region_4.5_spmd, %region_5.8_spmd} | conditional | flops 4 | bytes 401528 | solution.py:447
  21.5 0.6 %conditional.1 = ((f32[14,16,128]{2,1,0:T(8,128)}, f32[18,128]{1,0:T(8,128)}, f32[18,128]{1,0:T(8,128)})) conditional(s32[]{:T(128)} %convert_element_type.9, (f32[18,128]{1,0:T(8,128)S(1)}, f32[18,128]{1,0:T(8,128)S(1)}) %tuple.27, f32[14,32,128]{2,1,0:T(8,128)S(1)} %get-tuple-element.49), branch_computations={%region_6.6_spmd, %region_7.7_spmd} | conditional | flops 2 | bytes 401498 | solution.py:432
  21.5 0.6 %branch_0_fun.9 = (f32[18,128]{1,0:T(8,128)}, f32[18,128]{1,0:T(8,128)}) custom-call(f32[18,128]{1,0:T(8,128)S(1)} %get-tuple-element.40.early_lows, f32[18,128]{1,0:T(8,128)S(1)} %get-tuple-element.41.early_highs), custom_call_target="tpu_custom_call" | custom-call | flops 1 | bytes 1 | tf_op jit(solution)/shard_map/cond/branch_1_fun/cond/branch_0_fun/pallas_call | solution.py:429
  22.2 1.3 %collective-permute-start.8 = (f32[18,128]{1,0:T(8,128)}, f32[18,128]{1,0:T(8,128)S(1)}, u32[]{:S(2)}, u32[]{:S(2)}) collective-permute-start(f32[18,128]{1,0:T(8,128)} %get-tuple-element.85), channel_id=1, source_target_pairs={{8,16},{9,17},{10,18},{11,19},{12,20},{13,21},{14,22},{15,23},{16,... | collective-permute-start | bytes 27656 | tf_op jit(solution)/shard_map/ppermute | solution.py:339
  23.4 1.3 %collective-permute-start.9 = (f32[18,128]{1,0:T(8,128)}, f32[18,128]{1,0:T(8,128)S(1)}, u32[]{:S(2)}, u32[]{:S(2)}) collective-permute-start(f32[18,128]{1,0:T(8,128)} %get-tuple-element.86), channel_id=1, source_target_pairs={{16,8},{17,9},{18,10},{19,11},{20,12},{21,13},{22,14},{23,15},{24,... | collective-permute-start | bytes 27656 | tf_op jit(solution)/shard_map/ppermute | solution.py:339
  24.7 3.3 %shard_map.70 = (f32[14,16,128]{2,1,0:T(8,128)S(1)}, f32[18,128]{1,0:T(8,128)S(1)}, f32[14,32,128]{2,1,0:T(8,128)S(1)}, f32[14,32,128]{2,1,0:T(8,128)S(1)}) custom-call(f32[14,32,128]{2,1,0:T(8,128)S(1)} %get-tuple-element.73.block, f32[14,16,128]{2,1,0:T(8,128)} %get-tuple-element.75.early_halo, f32[14,16,128]{2,1,0:T(8,128)} %get-tuple-element.81.late_halo, ...), custom_call_target="tpu_custom_call" | custom-call | flops 1 | bytes 1 | tf_op jit(solution)/shard_map/pallas_call | solution.py:450
  28.1 0.0 collective-permute-done.10.relay
  28.1 0.0 collective-permute-done.8.left
  28.1 1.1 %collective-permute-done.9.right = f32[18,128]{1,0:T(8,128)S(1)} collective-permute-done((f32[18,128]{1,0:T(8,128)}, f32[18,128]{1,0:T(8,128)S(1)}, u32[]{:S(2)}, u32[]{:S(2)}) %collective-permute-start.9) | collective-permute-done | bytes 9248 | tf_op jit(solution)/shard_map/ppermute | solution.py:339
  29.2 3.8 %shard_map.71 = (f32[14,32,128]{2,1,0:T(8,128)}, f32[14,32,128]{2,1,0:T(8,128)}) custom-call(f32[14,32,128]{2,1,0:T(8,128)S(1)} %get-tuple-element.73.block, f32[14,16,128]{2,1,0:T(8,128)S(1)} %get-tuple-element.83.halo, f32[18,128]{1,0:T(8,128)S(1)} %get-tuple-element.84.pair, f32[18,128]{1,0:T(8,128)S(1)} %collective-permute-done.8.left, ...), custom_call_target="tpu_custom_call" | custom-call | flops 1 | bytes 1 | tf_op jit(solution)/shard_map/pallas_call | solution.py:456
  (5 shorter events, 0.0 us)
Async XLA Ops:
  1.9 19.6 %collective-permute-start.5 = (f32[4,8,128]{2,1,0:T(8,128)S(1)}, f32[4,8,128]{2,1,0:T(8,128)S(1)}, u32[]{:S(2)}, u32[]{:S(2)}) collective-permute-start(f32[4,8,128]{2,1,0:T(8,128)S(1)} %get-tuple-element.77), channel_id=1, source_target_pairs={{88,96},{89,97},{90,98},{91,99},{92,100},{93,101},{94,102},{95,103... | collective-permute-start | bytes 49160 | tf_op jit(solution)/shard_map/ppermute | solution.py:339
  2.6 18.9 %collective-permute-start.6 = (f32[4,8,128]{2,1,0:T(8,128)S(1)}, f32[4,8,128]{2,1,0:T(8,128)S(1)}, u32[]{:S(2)}, u32[]{:S(2)}) collective-permute-start(f32[4,8,128]{2,1,0:T(8,128)S(1)} %get-tuple-element.78), channel_id=1, source_target_pairs={{89,96},{90,97},{91,98},{92,99},{93,100},{94,101},{95,102},{185,19... | collective-permute-start | bytes 49160 | tf_op jit(solution)/shard_map/ppermute | solution.py:339
  3.2 18.2 %collective-permute-start.7 = (f32[3,8,128]{2,1,0:T(8,128)S(1)}, f32[3,8,128]{2,1,0:T(8,128)S(1)}, u32[]{:S(2)}, u32[]{:S(2)}) collective-permute-start(f32[3,8,128]{2,1,0:T(8,128)S(1)} %get-tuple-element.79), channel_id=1, source_target_pairs={{88,97},{89,98},{90,99},{91,100},{92,101},{93,102},{94,103},{184,1... | collective-permute-start | bytes 36872 | tf_op jit(solution)/shard_map/ppermute | solution.py:339
  4.0 7.4 %collective-permute-start.1 = (f32[14,8,128]{2,1,0:T(8,128)S(1)}, f32[14,8,128]{2,1,0:T(8,128)S(1)}, u32[]{:S(2)}, u32[]{:S(2)}) collective-permute-start(f32[14,8,128]{2,1,0:T(8,128)S(1)} %get-tuple-element.30), channel_id=1, source_target_pairs={{1,2},{3,4},{5,6},{9,10},{11,12},{13,14},{97,98},{99,100},{101,102... | collective-permute-start | bytes 172040 | tf_op jit(solution)/shard_map/cond/branch_1_fun/ppermute | solution.py:339
  4.7 6.7 %collective-permute-start = (f32[84,128]{1,0:T(8,128)S(1)}, f32[84,128]{1,0:T(8,128)S(1)}, u32[]{:S(2)}, u32[]{:S(2)}) collective-permute-start(f32[84,128]{1,0:T(8,128)S(1)} %get-tuple-element.29), channel_id=1, source_target_pairs={{0,1},{2,3},{4,5},{6,7},{8,9},{10,11},{12,13},{14,15},{96,97},{98,... | collective-permute-start | bytes 129032 | tf_op jit(solution)/shard_map/cond/branch_1_fun/ppermute | solution.py:339
  12.1 8.7 %collective-permute-start.2 = (f32[18,128]{1,0:T(8,128)S(1)}, f32[18,128]{1,0:T(8,128)}, u32[]{:S(2)}, u32[]{:S(2)}) collective-permute-start(f32[18,128]{1,0:T(8,128)S(1)} %get-tuple-element.32), channel_id=1, source_target_pairs={{0,8},{1,9},{2,10},{3,11},{4,12},{5,13},{6,14},{7,15},{96,104},{97... | collective-permute-start | bytes 27656 | tf_op jit(solution)/shard_map/cond/branch_1_fun/ppermute | solution.py:339
  20.8 7.3 %collective-permute-start.10 = (f32[20,128]{1,0:T(8,128)S(1)}, f32[20,128]{1,0:T(8,128)S(1)}, u32[]{:S(2)}, u32[]{:S(2)}) collective-permute-start(f32[20,128]{1,0:T(8,128)S(1)} %get-tuple-element.87), channel_id=1, source_target_pairs={{96,88},{97,89},{98,90},{99,91},{100,92},{101,93},{102,94},{103,95... | collective-permute-start | bytes 30728 | tf_op jit(solution)/shard_map/ppermute | solution.py:339
  22.2 5.9 %collective-permute-start.8 = (f32[18,128]{1,0:T(8,128)}, f32[18,128]{1,0:T(8,128)S(1)}, u32[]{:S(2)}, u32[]{:S(2)}) collective-permute-start(f32[18,128]{1,0:T(8,128)} %get-tuple-element.85), channel_id=1, source_target_pairs={{8,16},{9,17},{10,18},{11,19},{12,20},{13,21},{14,22},{15,23},{16,... | collective-permute-start | bytes 27656 | tf_op jit(solution)/shard_map/ppermute | solution.py:339
  23.4 5.8 %collective-permute-start.9 = (f32[18,128]{1,0:T(8,128)}, f32[18,128]{1,0:T(8,128)S(1)}, u32[]{:S(2)}, u32[]{:S(2)}) collective-permute-start(f32[18,128]{1,0:T(8,128)} %get-tuple-element.86), channel_id=1, source_target_pairs={{16,8},{17,9},{18,10},{19,11},{20,12},{21,13},{22,14},{23,15},{24,... | collective-permute-start | bytes 27656 | tf_op jit(solution)/shard_map/ppermute | solution.py:339

commit v8 on v7

--- a/solution.py
+++ b/solution.py
@@ -219,6 +219,8 @@
         copies = [pltpu.make_async_copy(early_halo, halo, sems.at[0]), pltpu.make_async_copy(early_pair, pair, sems.at[1])]
         for copy in copies:
             copy.start()
+        for v in range(14):
+            w0[v, 0:OWN] = block[v]
         for copy in copies:
             copy.wait()
 
@@ -226,11 +228,15 @@
     def _():
         copy = pltpu.make_async_copy(late_halo, halo, sems.at[0])
         copy.start()
+        for v in range(14):
+            w0[v, 0:OWN] = block[v]
         copy.wait()
 
     @pl.when(place != 0)
     def _():
-        main_sections(block, halo, table, final, last, w0, wa, wb, coeff)
+        for v in range(14):
+            w0[v, OWN:ROWS] = halo[v]
+        main_sections(block, None, table, final, last, w0, wa, wb, coeff)
 
 
 def last_kernel(

time: 33.4 us -> 33.4 us (level)
  no operation moved by 1% of the time
where the time goes in v8:
time: 33.4 us; the launch traced here: 33.1 us
  starting transfers between devices  18.7 us (56%)
  Pallas kernels  9.77 us (29%)
  waiting for transfers between devices  3.69 us (11%)
  between operations  0.78 us (2%)
    ppermute x9, starting transfers between devices, send(): return lax.ppermute(x, ('blk', 'wn'), pairs)  18.7 us
    pallas_call x1, Pallas kernels, local(): pl.pallas_call(last_kernel, out_shape=(out, out), in_specs=[VMEM] * 10 +...  3.8 us
    ppermute x9, waiting for transfers between devices, send(): return lax.ppermute(x, ('blk', 'wn'), pairs)  3.69 us
    pallas_call x1, Pallas kernels, local(): call(late_main_kernel, (halo_shape, strips, out, out), [VMEM] + [HBM] * 3...  3.38 us
    pallas_call x1, Pallas kernels, local(): call(load_kernel, (out, f32(4, 8, LANES), f32(4, 8, LANES), f32(3, 8, LAN...  1.26 us
    pallas_call x1, Pallas kernels, early(): call(early_columns_kernel, (halo_shape, strips, strips, strips, offered),...  0.68 us
  transfers between devices with their start and end apart: 9, of which 3 were waited for; matrix products, arithmetic and copies ran while one was open for 0% of the time, Pallas kernels for 14%

profile of v8, /device:TPU:64, one launch (start us, length us, event | category | flops | bytes accessed | tf_op | source)
XLA Modules:
  0.0 33.1 jit_solution(3464785409488499202)
XLA Ops:
  0.6 1.3 %shard_map.68 = (f32[14,32,128]{2,1,0:T(8,128)S(1)}, f32[4,8,128]{2,1,0:T(8,128)S(1)}, f32[4,8,128]{2,1,0:T(8,128)S(1)}, f32[3,8,128]{2,1,0:T(8,128)S(1)}, f32[248,128]{1,0:T(8,128)S(1)}) custom-call(f32[11,32,128]{2,1,0:T(8,128)} %bitcast.5, f32[2,32,128]{2,1,0:T(8,128)} %bitcast.6, f32[1,32,128]{2,1,0:T(8,128)} %bitcast.7, f32[11,11]{1,0:T(8,128)} %shear.1, ...), custom_call_target="tpu_custom_call" | custom-call | flops 1 | bytes 1 | tf_op jit(solution)/shard_map/pallas_call | solution.py:392
  1.9 0.7 %collective-permute-start.5 = (f32[4,8,128]{2,1,0:T(8,128)S(1)}, f32[4,8,128]{2,1,0:T(8,128)S(1)}, u32[]{:S(2)}, u32[]{:S(2)}) collective-permute-start(f32[4,8,128]{2,1,0:T(8,128)S(1)} %get-tuple-element.77), channel_id=1, source_target_pairs={{88,96},{89,97},{90,98},{91,99},{92,100},{93,101},{94,102},{95,103... | collective-permute-start | bytes 49160 | tf_op jit(solution)/shard_map/ppermute | solution.py:345
  2.6 0.7 %collective-permute-start.6 = (f32[4,8,128]{2,1,0:T(8,128)S(1)}, f32[4,8,128]{2,1,0:T(8,128)S(1)}, u32[]{:S(2)}, u32[]{:S(2)}) collective-permute-start(f32[4,8,128]{2,1,0:T(8,128)S(1)} %get-tuple-element.78), channel_id=1, source_target_pairs={{89,96},{90,97},{91,98},{92,99},{93,100},{94,101},{95,102},{185,19... | collective-permute-start | bytes 49160 | tf_op jit(solution)/shard_map/ppermute | solution.py:345
  3.2 0.7 %collective-permute-start.7 = (f32[3,8,128]{2,1,0:T(8,128)S(1)}, f32[3,8,128]{2,1,0:T(8,128)S(1)}, u32[]{:S(2)}, u32[]{:S(2)}) collective-permute-start(f32[3,8,128]{2,1,0:T(8,128)S(1)} %get-tuple-element.79), channel_id=1, source_target_pairs={{88,97},{89,98},{90,99},{91,100},{92,101},{93,102},{94,103},{184,1... | collective-permute-start | bytes 36872 | tf_op jit(solution)/shard_map/ppermute | solution.py:345
  3.9 16.9 %conditional.4 = ((f32[14,16,128]{2,1,0:T(8,128)}, f32[18,128]{1,0:T(8,128)}, f32[18,128]{1,0:T(8,128)S(1)}, f32[18,128]{1,0:T(8,128)S(1)}, f32[20,128]{1,0:T(8,...) conditional(s32[]{:T(128)} %convert_element_type.12, () %tuple.34, (f32[14,32,128]{2,1,0:T(8,128)S(1)}, ...), branch_computations={%region_0.1_spmd, %region_1.4_spmd} | conditional | flops 5 | bytes 438505 | solution.py:443
  4.0 0.7 %collective-permute-start.1 = (f32[14,8,128]{2,1,0:T(8,128)S(1)}, f32[14,8,128]{2,1,0:T(8,128)S(1)}, u32[]{:S(2)}, u32[]{:S(2)}) collective-permute-start(f32[14,8,128]{2,1,0:T(8,128)S(1)} %get-tuple-element.30), channel_id=1, source_target_pairs={{1,2},{3,4},{5,6},{9,10},{11,12},{13,14},{97,98},{99,100},{101,102... | collective-permute-start | bytes 172040 | tf_op jit(solution)/shard_map/cond/branch_1_fun/ppermute | solution.py:345
  4.7 5.9 %collective-permute-start = (f32[84,128]{1,0:T(8,128)S(1)}, f32[84,128]{1,0:T(8,128)S(1)}, u32[]{:S(2)}, u32[]{:S(2)}) collective-permute-start(f32[84,128]{1,0:T(8,128)S(1)} %get-tuple-element.29), channel_id=1, source_target_pairs={{0,1},{2,3},{4,5},{6,7},{8,9},{10,11},{12,13},{14,15},{96,97},{98,... | collective-permute-start | bytes 129032 | tf_op jit(solution)/shard_map/cond/branch_1_fun/ppermute | solution.py:345
  10.5 0.9 %collective-permute-done.first = f32[84,128]{1,0:T(8,128)S(1)} collective-permute-done((f32[84,128]{1,0:T(8,128)S(1)}, f32[84,128]{1,0:T(8,128)S(1)}, u32[]{:S(2)}, u32[]{:S(2)}) %collective-permute-start) | collective-permute-done | bytes 43040 | tf_op jit(solution)/shard_map/cond/branch_1_fun/ppermute | solution.py:345
  11.4 0.0 collective-permute-done.1.second
  11.4 0.7 %branch_1_fun.7 = (f32[14,16,128]{2,1,0:T(8,128)}, f32[18,128]{1,0:T(8,128)S(1)}, f32[18,128]{1,0:T(8,128)S(1)}, f32[18,128]{1,0:T(8,128)S(1)}, f32[20,128]{1,0:T(8,128)S(1)}) custom-call(f32[84,128]{1,0:T(8,128)S(1)} %collective-permute-done.first, f32[14,8,128]{2,1,0:T(8,128)S(1)} %collective-permute-done.1.second, f32[14,32,128]{2,1,0:T(8,128)S(1)} %get-tuple-element.28.block), custom_call_target="tpu_custom_call" | custom-call | flops 1 | bytes 1 | tf_op jit(solution)/shard_map/cond/branch_1_fun/pallas_call | solution.py:414
  12.1 7.0 %collective-permute-start.2 = (f32[18,128]{1,0:T(8,128)S(1)}, f32[18,128]{1,0:T(8,128)}, u32[]{:S(2)}, u32[]{:S(2)}) collective-permute-start(f32[18,128]{1,0:T(8,128)S(1)} %get-tuple-element.32), channel_id=1, source_target_pairs={{0,8},{1,9},{2,10},{3,11},{4,12},{5,13},{6,14},{7,15},{96,104},{97... | collective-permute-start | bytes 27656 | tf_op jit(solution)/shard_map/cond/branch_1_fun/ppermute | solution.py:345
  19.1 1.7 %collective-permute-done.2 = f32[18,128]{1,0:T(8,128)} collective-permute-done((f32[18,128]{1,0:T(8,128)S(1)}, f32[18,128]{1,0:T(8,128)}, u32[]{:S(2)}, u32[]{:S(2)}) %collective-permute-start.2) | collective-permute-done | bytes 9248 | tf_op jit(solution)/shard_map/cond/branch_1_fun/ppermute | solution.py:345
  20.8 0.7 %collective-permute-start.10 = (f32[20,128]{1,0:T(8,128)S(1)}, f32[20,128]{1,0:T(8,128)S(1)}, u32[]{:S(2)}, u32[]{:S(2)}) collective-permute-start(f32[20,128]{1,0:T(8,128)S(1)} %get-tuple-element.87), channel_id=1, source_target_pairs={{96,88},{97,89},{98,90},{99,91},{100,92},{101,93},{102,94},{103,95... | collective-permute-start | bytes 30728 | tf_op jit(solution)/shard_map/ppermute | solution.py:345
  21.5 0.0 collective-permute-done.7.c.wrap_down
  21.5 0.0 collective-permute-done.5.a.wrap
  21.5 0.0 collective-permute-done.6.b.wrap_up
  21.5 0.7 %conditional.5 = ((f32[14,16,128]{2,1,0:T(8,128)}, f32[18,128]{1,0:T(8,128)}, f32[18,128]{1,0:T(8,128)})) conditional(s32[]{:T(128)} %convert_element_type.13, () %tuple.36, (s32[]{:T(128)}, f32[18,128]{1,0:T(8,128)S(1)}, f32[18,128]{1,0:T(8,128)S(1)}, f32[14,32,128]{2,1,0:T(8,128)S(1)}) %tuple.37), branch_computations={%region_4.5_spmd, %region_5.8_spmd} | conditional | flops 4 | bytes 401528 | solution.py:453
  21.5 0.6 %conditional.1 = ((f32[14,16,128]{2,1,0:T(8,128)}, f32[18,128]{1,0:T(8,128)}, f32[18,128]{1,0:T(8,128)})) conditional(s32[]{:T(128)} %convert_element_type.9, (f32[18,128]{1,0:T(8,128)S(1)}, f32[18,128]{1,0:T(8,128)S(1)}) %tuple.27, f32[14,32,128]{2,1,0:T(8,128)S(1)} %get-tuple-element.49), branch_computations={%region_6.6_spmd, %region_7.7_spmd} | conditional | flops 2 | bytes 401498 | solution.py:438
  21.5 0.6 %branch_0_fun.9 = (f32[18,128]{1,0:T(8,128)}, f32[18,128]{1,0:T(8,128)}) custom-call(f32[18,128]{1,0:T(8,128)S(1)} %get-tuple-element.40.early_lows, f32[18,128]{1,0:T(8,128)S(1)} %get-tuple-element.41.early_highs), custom_call_target="tpu_custom_call" | custom-call | flops 1 | bytes 1 | tf_op jit(solution)/shard_map/cond/branch_1_fun/cond/branch_0_fun/pallas_call | solution.py:435
  22.2 1.3 %collective-permute-start.8 = (f32[18,128]{1,0:T(8,128)}, f32[18,128]{1,0:T(8,128)S(1)}, u32[]{:S(2)}, u32[]{:S(2)}) collective-permute-start(f32[18,128]{1,0:T(8,128)} %get-tuple-element.85), channel_id=1, source_target_pairs={{8,16},{9,17},{10,18},{11,19},{12,20},{13,21},{14,22},{15,23},{16,... | collective-permute-start | bytes 27656 | tf_op jit(solution)/shard_map/ppermute | solution.py:345
  23.4 1.3 %collective-permute-start.9 = (f32[18,128]{1,0:T(8,128)}, f32[18,128]{1,0:T(8,128)S(1)}, u32[]{:S(2)}, u32[]{:S(2)}) collective-permute-start(f32[18,128]{1,0:T(8,128)} %get-tuple-element.86), channel_id=1, source_target_pairs={{16,8},{17,9},{18,10},{19,11},{20,12},{21,13},{22,14},{23,15},{24,... | collective-permute-start | bytes 27656 | tf_op jit(solution)/shard_map/ppermute | solution.py:345
  24.7 3.4 %shard_map.70 = (f32[14,16,128]{2,1,0:T(8,128)S(1)}, f32[18,128]{1,0:T(8,128)S(1)}, f32[14,32,128]{2,1,0:T(8,128)S(1)}, f32[14,32,128]{2,1,0:T(8,128)S(1)}) custom-call(f32[14,32,128]{2,1,0:T(8,128)S(1)} %get-tuple-element.73.block, f32[14,16,128]{2,1,0:T(8,128)} %get-tuple-element.75.early_halo, f32[14,16,128]{2,1,0:T(8,128)} %get-tuple-element.81.late_halo, ...), custom_call_target="tpu_custom_call" | custom-call | flops 1 | bytes 1 | tf_op jit(solution)/shard_map/pallas_call | solution.py:456
  28.1 0.0 collective-permute-done.10.relay
  28.1 0.0 collective-permute-done.8.left
  28.2 1.1 %collective-permute-done.9.right = f32[18,128]{1,0:T(8,128)S(1)} collective-permute-done((f32[18,128]{1,0:T(8,128)}, f32[18,128]{1,0:T(8,128)S(1)}, u32[]{:S(2)}, u32[]{:S(2)}) %collective-permute-start.9) | collective-permute-done | bytes 9248 | tf_op jit(solution)/shard_map/ppermute | solution.py:345
  29.2 3.8 %shard_map.71 = (f32[14,32,128]{2,1,0:T(8,128)}, f32[14,32,128]{2,1,0:T(8,128)}) custom-call(f32[14,32,128]{2,1,0:T(8,128)S(1)} %get-tuple-element.73.block, f32[14,16,128]{2,1,0:T(8,128)S(1)} %get-tuple-element.83.halo, f32[18,128]{1,0:T(8,128)S(1)} %get-tuple-element.84.pair, f32[18,128]{1,0:T(8,128)S(1)} %collective-permute-done.8.left, ...), custom_call_target="tpu_custom_call" | custom-call | flops 1 | bytes 1 | tf_op jit(solution)/shard_map/pallas_call | solution.py:462
  (5 shorter events, 0.0 us)
Async XLA Ops:
  1.9 19.6 %collective-permute-start.5 = (f32[4,8,128]{2,1,0:T(8,128)S(1)}, f32[4,8,128]{2,1,0:T(8,128)S(1)}, u32[]{:S(2)}, u32[]{:S(2)}) collective-permute-start(f32[4,8,128]{2,1,0:T(8,128)S(1)} %get-tuple-element.77), channel_id=1, source_target_pairs={{88,96},{89,97},{90,98},{91,99},{92,100},{93,101},{94,102},{95,103... | collective-permute-start | bytes 49160 | tf_op jit(solution)/shard_map/ppermute | solution.py:345
  2.6 18.9 %collective-permute-start.6 = (f32[4,8,128]{2,1,0:T(8,128)S(1)}, f32[4,8,128]{2,1,0:T(8,128)S(1)}, u32[]{:S(2)}, u32[]{:S(2)}) collective-permute-start(f32[4,8,128]{2,1,0:T(8,128)S(1)} %get-tuple-element.78), channel_id=1, source_target_pairs={{89,96},{90,97},{91,98},{92,99},{93,100},{94,101},{95,102},{185,19... | collective-permute-start | bytes 49160 | tf_op jit(solution)/shard_map/ppermute | solution.py:345
  3.2 18.2 %collective-permute-start.7 = (f32[3,8,128]{2,1,0:T(8,128)S(1)}, f32[3,8,128]{2,1,0:T(8,128)S(1)}, u32[]{:S(2)}, u32[]{:S(2)}) collective-permute-start(f32[3,8,128]{2,1,0:T(8,128)S(1)} %get-tuple-element.79), channel_id=1, source_target_pairs={{88,97},{89,98},{90,99},{91,100},{92,101},{93,102},{94,103},{184,1... | collective-permute-start | bytes 36872 | tf_op jit(solution)/shard_map/ppermute | solution.py:345
  4.0 7.4 %collective-permute-start.1 = (f32[14,8,128]{2,1,0:T(8,128)S(1)}, f32[14,8,128]{2,1,0:T(8,128)S(1)}, u32[]{:S(2)}, u32[]{:S(2)}) collective-permute-start(f32[14,8,128]{2,1,0:T(8,128)S(1)} %get-tuple-element.30), channel_id=1, source_target_pairs={{1,2},{3,4},{5,6},{9,10},{11,12},{13,14},{97,98},{99,100},{101,102... | collective-permute-start | bytes 172040 | tf_op jit(solution)/shard_map/cond/branch_1_fun/ppermute | solution.py:345
  4.7 6.7 %collective-permute-start = (f32[84,128]{1,0:T(8,128)S(1)}, f32[84,128]{1,0:T(8,128)S(1)}, u32[]{:S(2)}, u32[]{:S(2)}) collective-permute-start(f32[84,128]{1,0:T(8,128)S(1)} %get-tuple-element.29), channel_id=1, source_target_pairs={{0,1},{2,3},{4,5},{6,7},{8,9},{10,11},{12,13},{14,15},{96,97},{98,... | collective-permute-start | bytes 129032 | tf_op jit(solution)/shard_map/cond/branch_1_fun/ppermute | solution.py:345
  12.1 8.7 %collective-permute-start.2 = (f32[18,128]{1,0:T(8,128)S(1)}, f32[18,128]{1,0:T(8,128)}, u32[]{:S(2)}, u32[]{:S(2)}) collective-permute-start(f32[18,128]{1,0:T(8,128)S(1)} %get-tuple-element.32), channel_id=1, source_target_pairs={{0,8},{1,9},{2,10},{3,11},{4,12},{5,13},{6,14},{7,15},{96,104},{97... | collective-permute-start | bytes 27656 | tf_op jit(solution)/shard_map/cond/branch_1_fun/ppermute | solution.py:345
  20.8 7.3 %collective-permute-start.10 = (f32[20,128]{1,0:T(8,128)S(1)}, f32[20,128]{1,0:T(8,128)S(1)}, u32[]{:S(2)}, u32[]{:S(2)}) collective-permute-start(f32[20,128]{1,0:T(8,128)S(1)} %get-tuple-element.87), channel_id=1, source_target_pairs={{96,88},{97,89},{98,90},{99,91},{100,92},{101,93},{102,94},{103,95... | collective-permute-start | bytes 30728 | tf_op jit(solution)/shard_map/ppermute | solution.py:345
  22.2 6.0 %collective-permute-start.8 = (f32[18,128]{1,0:T(8,128)}, f32[18,128]{1,0:T(8,128)S(1)}, u32[]{:S(2)}, u32[]{:S(2)}) collective-permute-start(f32[18,128]{1,0:T(8,128)} %get-tuple-element.85), channel_id=1, source_target_pairs={{8,16},{9,17},{10,18},{11,19},{12,20},{13,21},{14,22},{15,23},{16,... | collective-permute-start | bytes 27656 | tf_op jit(solution)/shard_map/ppermute | solution.py:345
  23.4 5.8 %collective-permute-start.9 = (f32[18,128]{1,0:T(8,128)}, f32[18,128]{1,0:T(8,128)S(1)}, u32[]{:S(2)}, u32[]{:S(2)}) collective-permute-start(f32[18,128]{1,0:T(8,128)} %get-tuple-element.86), channel_id=1, source_target_pairs={{16,8},{17,9},{18,10},{19,11},{20,12},{21,13},{22,14},{23,15},{24,... | collective-permute-start | bytes 27656 | tf_op jit(solution)/shard_map/ppermute | solution.py:345
